TPU v7x, 256 devices: a whole 4x4x8 slice. The times are simulated.
256 devices in a mesh: row: 32 (over z_lo, x, core), col: 8 (over z_hi, y).
Axes of the slice: x: 4, y: 4, z: 8 (z_hi: 2, z_lo: 4; z = z_hi * 4 + z_lo), core: 2. Of those that a mesh axis runs over, the one named last changes fastest.
Arguments:
- tokens: bfloat16 [768, 8192], P('row', 'col'), may hold values from -6 to 6
- gate_weight: bfloat16 [8192, 16384], P('col', 'row'), may hold values from -0.0625 to 0.0625
- up_weight: bfloat16 [8192, 16384], P('col', 'row'), may hold values from -0.0625 to 0.0625
- down_weight: bfloat16 [16384, 8192], P('row', 'col'), may hold values from -0.046875 to 0.046875
- cotangent: bfloat16 [768, 8192], P('row', 'col'), may hold values from -0.59765625 to 0.59765625
Outputs:
- output: bfloat16 [768, 8192], P('row', 'col')
- grad_tokens: bfloat16 [768, 8192], P('row', 'col')
- grad_gate: bfloat16 [8192, 16384], P('col', 'row')
- grad_up: bfloat16 [8192, 16384], P('col', 'row')
- grad_down: bfloat16 [16384, 8192], P('row', 'col')
All inputs are finite; a program needn't handle non-finite values.
Results may differ from a plain program's by a relative error of at most 0.005.
Values may be sent and summed in bfloat16 or wider, within the bound.
No kernel may reach another device: no remote copies, remote signals or barrier semaphores. Data moves between devices by JAX's collectives and lax.ppermute only.
A program may use at most 64 MiB of HBM per device.

v0:
```python
import jax
import jax.numpy as jnp
from jax import lax
from jax.experimental import pallas as pl
from jax.experimental.pallas import tpu as pltpu
from jax.sharding import PartitionSpec as P

Z, X, CORES, ZH, Y = 4, 4, 2, 2, 4
BF = jnp.bfloat16
F32 = jnp.float32
VMEM_LIMIT = 32 * 1024 * 1024


def row_perm(move):
    pairs = []
    for z in range(Z):
        for x in range(X):
            for c in range(CORES):
                tz, tx, tc = move(z, x, c)
                pairs.append(
                    ((z * X + x) * CORES + c, ((tz % Z) * X + tx % X) * CORES + tc % CORES)
                )
    return pairs


def col_perm(move):
    pairs = []
    for h in range(ZH):
        for y in range(Y):
            th, ty = move(h, y)
            pairs.append((h * Y + y, (th % ZH) * Y + ty % Y))
    return pairs


def send_z(a, k):
    return lax.ppermute(a, "row", row_perm(lambda z, x, c: (z + k, x, c)))


def send_x(a, k):
    return lax.ppermute(a, "row", row_perm(lambda z, x, c: (z, x + k, c)))


def send_core(a):
    return lax.ppermute(a, "row", row_perm(lambda z, x, c: (z, x, c + 1)))


def send_y(a, k):
    return lax.ppermute(a, "col", col_perm(lambda h, y: (h, y + k)))


def send_half(a):
    return lax.ppermute(a, "col", col_perm(lambda h, y: (h + 1, y)))


def dot(left, right, ldim, rdim):
    return lax.dot_general(
        left, right, (((ldim,), (rdim,)), ((), ())), preferred_element_type=F32
    )


def call(kernel, outs, args, flops=0, scalar=None, after=()):
    out_shape = [jax.ShapeDtypeStruct(s, d) for s, d in outs]
    moved = sum(a.size * a.dtype.itemsize for a in args)
    moved += sum(o.size * o.dtype.itemsize for o in out_shape)
    vmem = pl.BlockSpec(memory_space=pltpu.VMEM)
    in_specs = [vmem] * len(args)
    if scalar is not None:
        in_specs = [pl.BlockSpec(memory_space=pltpu.SMEM)] + in_specs
        args = [scalar, *args]
    n = len(args)
    body = kernel
    if after:
        in_specs = in_specs + [pl.BlockSpec(memory_space=pl.ANY)] * len(after)
        args = [*args, *after]

        def body(*refs):
            kernel(*refs[:n], *refs[n + len(after) :])

    return pl.pallas_call(
        body,
        out_shape=out_shape,
        in_specs=in_specs,
        out_specs=[vmem] * len(outs),
        compiler_params=pltpu.CompilerParams(vmem_limit_bytes=VMEM_LIMIT),
        cost_estimate=pl.CostEstimate(
            flops=flops, bytes_accessed=moved, transcendentals=0
        ),
    )(*args)


def block_at(index, size):
    return pl.ds(pl.multiple_of(lax.rem(index, Y) * size, size), size)


def cat_z_kernel(a, b, c, d, out):
    parts = [r[...].astype(F32) for r in (a, b, c, d)]
    out[...] = jnp.concatenate(parts, axis=0).astype(BF)


def cat_x_kernel(a, b, c, d, out):
    size = a.shape[0]
    for k, r in enumerate((a, b, c, d)):
        out[k * size : (k + 1) * size] = r[...]


def hold_kernel(*refs):
    half = len(refs) // 2
    for src, dst in zip(refs[:half], refs[half:]):
        dst[...] = src[...]


def hold(args, after):
    return call(hold_kernel, [(a.shape, a.dtype) for a in args], list(args), after=after)


def gather_z(a):
    n, w = a.shape
    parts = [a] + [send_z(a, k) for k in (2, 1, 3)]
    a, c, b, d = parts
    return call(cat_z_kernel, [((Z * n, w), BF)], [a, b, c, d])[0]


def gather_x(a, got, after=()):
    n, w = a.shape
    return call(cat_x_kernel, [((X * n, w), BF)], [a, *got], after=after)[0]


def all_x(a):
    c, b, d = [send_x(a, k) for k in (2, 1, 3)]
    return [b, c, d]


def all_y(sends):
    c, b, d = [send_y(sends[k - 1], k) for k in (2, 1, 3)]
    return [b, c, d]


def up_kernel(y, mine, theirs, wg, wu, whole, s1, s2, s3, own):
    half = mine.shape[0]
    whole[:half] = mine[...]
    whole[half:] = theirs[...]
    n, f = s1.shape[0], wg.shape[1]
    for k, o in ((1, s1), (2, s2), (3, s3), (0, own)):
        rows = whole[block_at(y[0] + k, n), :]
        o[:, :f] = dot(rows, wg[...], 1, 0).astype(o.dtype)
        o[:, f:] = dot(rows, wu[...], 1, 0).astype(o.dtype)


def back_kernel(y, mine, theirs, wd, whole, s1, s2, s3, own):
    half = mine.shape[0]
    whole[:half] = mine[...]
    whole[half:] = theirs[...]
    n = s1.shape[0]
    for k, o in ((1, s1), (2, s2), (3, s3), (0, own)):
        rows = whole[block_at(y[0] + k, n), :]
        o[...] = dot(rows, wd[...], 1, 1).astype(o.dtype)


def sum_y_kernel(own, a, b, c, total, send):
    t = own[...] + a[...].astype(F32) + b[...].astype(F32) + c[...].astype(F32)
    total[...] = t
    send[...] = t.astype(BF)


def hidden_kernel(mine, theirs, out):
    f = out.shape[1]
    gate = mine[:, :f] + theirs[:, :f].astype(F32)
    up = mine[:, f:] + theirs[:, f:].astype(F32)
    out[...] = (gate * jax.nn.sigmoid(gate) * up).astype(BF)


def grads_kernel(mine, theirs, mine_h, theirs_h, out):
    f = mine_h.shape[1]
    gate = mine[:, :f] + theirs[:, :f].astype(F32)
    up = mine[:, f:] + theirs[:, f:].astype(F32)
    gh = mine_h[...] + theirs_h[...].astype(F32)
    sig = jax.nn.sigmoid(gate)
    out[:, :f] = (gh * up * sig * (1.0 + gate * (1.0 - sig))).astype(BF)
    out[:, f:] = (gh * gate * sig).astype(BF)


def place(y, parts, whole):
    n = parts[0].shape[0]
    for k, r in enumerate(parts):
        whole[block_at(y[0] + Y - k, n), :] = r[...]


def out_kernel(y, a, b, c, d, wd, whole, own, theirs):
    place(y, (a, b, c, d), whole)
    half = own.shape[0]
    theirs[...] = dot(whole[half:, :], wd[...], 1, 0).astype(theirs.dtype)
    own[...] = dot(whole[:half, :], wd[...], 1, 0)


def tokens_kernel(y, a, b, c, d, wg, wu, gg, ug, own, theirs):
    f = gg.shape[1]
    n = a.shape[0]
    for k, r in enumerate((a, b, c, d)):
        at = block_at(y[0] + Y - k, n)
        gg[at, :] = r[:, :f]
        ug[at, :] = r[:, f:]
    half = own.shape[0]
    for o, at in ((theirs, slice(half, None)), (own, slice(0, half))):
        t = dot(gg[at, :], wg[...], 1, 1) + dot(ug[at, :], wu[...], 1, 1)
        o[...] = t.astype(o.dtype)


def rs_first_kernel(mine, theirs, s1, s2, s3, own):
    n = own.shape[0]
    for k, o in enumerate((own, s1, s2, s3)):
        at = slice(k * n, (k + 1) * n)
        o[...] = (mine[at, :] + theirs[at, :].astype(F32)).astype(o.dtype)


def rs_next_kernel(mine, a, b, c, s1, s2, s3, own):
    n = own.shape[0]
    t = mine[...] + a[...].astype(F32) + b[...].astype(F32) + c[...].astype(F32)
    for k, o in enumerate((own, s1, s2, s3)):
        o[...] = t[k * n : (k + 1) * n].astype(o.dtype)


def rs_last_kernel(mine, a, b, c, out):
    t = mine[...] + a[...].astype(F32) + b[...].astype(F32) + c[...].astype(F32)
    out[...] = t.astype(BF)


def first_row(own, theirs, after=()):
    rows, w = own.shape
    sends = [((rows // X, w), BF)] * 3 + [((rows // X, w), F32)]
    return call(rs_first_kernel, sends, [own, theirs], after=after)


def back_x(sends):
    c, b, d = [send_x(sends[k - 1], -k) for k in (2, 1, 3)]
    return [b, c, d]


def next_row(own, got, after=()):
    rows, w = own.shape
    sends = [((rows // Z, w), BF)] * 3 + [((rows // Z, w), F32)]
    return call(rs_next_kernel, sends, [own, *got], after=after)


def back_z(sends):
    c, b, d = [send_z(sends[k - 1], -k) for k in (2, 1, 3)]
    return [b, c, d]


def last_row(own, got):
    return call(rs_last_kernel, [(own.shape, BF)], [own, *got])[0]


def on_device(tokens, gate_weight, up_weight, down_weight, cotangent):
    y = lax.rem(lax.axis_index("col"), Y).astype(jnp.int32).reshape(1)
    d, f = gate_weight.shape

    t = gather_z(tokens)
    g = gather_z(hold([cotangent], [t])[0])
    t = gather_x(t, all_x(t), after=[g])
    half = t.shape[0]
    n = CORES * half // Y
    flops = 2 * CORES * half * d * f

    def sends(w):
        return [((CORES * half, d), BF)] + [((n, w), BF)] * 3 + [((n, w), F32)]

    all_tokens, s1, s2, s3, own = call(
        up_kernel, sends(2 * f), [t, send_core(t), gate_weight, up_weight], 2 * flops, y
    )
    g = hold([g], [s1])[0]
    got_x = all_x(g)
    got = all_y([s1, s2, s3])
    g = gather_x(g, got_x, after=got)
    gate_up, part = call(
        sum_y_kernel, [((n, 2 * f), F32), ((n, 2 * f), BF)], [own, *got], after=got_x
    )

    gate_up2 = send_half(part)
    all_cotangent, s1, s2, s3, own = call(
        back_kernel, sends(f), [g, send_core(g), down_weight], flops, y
    )
    got = all_y([s1, s2, s3])
    gh, part = call(
        sum_y_kernel, [((n, f), F32), ((n, f), BF)], [own, *got], after=[gate_up2]
    )
    hidden = call(hidden_kernel, [((n, f), BF)], [gate_up, gate_up2], after=got)[0]

    gh2 = send_half(part)
    got = all_y([hidden] * 3)
    all_hidden, own_out, their_out = call(
        out_kernel,
        [((Y * n, f), BF), ((half, d), F32), ((half, d), OUT_CORE)],
        [hidden, *got, down_weight],
        flops,
        y,
        after=[gh2],
    )
    grads = call(
        grads_kernel, [((n, 2 * f), BF)], [gate_up, gate_up2, gh, gh2], after=got
    )[0]

    s1, s2, s3, own_out = first_row(own_out, send_core(their_out))
    got_out = back_x([s1, s2, s3])
    got = all_y([grads] * 3)
    gg, ug, own_gt, their_gt = call(
        tokens_kernel,
        [((Y * n, f), BF), ((Y * n, f), BF), ((half, d), F32), ((half, d), OUT_CORE)],
        [grads, *got, gate_weight, up_weight],
        2 * flops,
        y,
        after=got_out,
    )
    s1, s2, s3, own_out = next_row(own_out, got_out, after=got)
    z_out = [s1, s2, s3]
    s1, s2, s3, own_gt = first_row(own_gt, send_core(their_gt))
    z_out = hold(z_out, [s1])
    got_z = back_z(z_out)
    got = back_x([s1, s2, s3])
    output = last_row(own_out, got_z)
    grad_down = dot(all_hidden, all_cotangent, 0, 0).astype(BF)
    s1, s2, s3, own_gt = next_row(own_gt, got, after=got_z)
    grad_tokens = last_row(own_gt, back_z([s1, s2, s3]))
    grad_gate = dot(all_tokens, gg, 0, 0).astype(BF)
    grad_up = dot(all_tokens, ug, 0, 0).astype(BF)
    return (output, grad_tokens, grad_gate, grad_up, grad_down)


OUT_CORE = F32


def solution(mesh):
    return jax.shard_map(
        on_device,
        mesh=mesh,
        in_specs=(
            P("row", "col"),
            P("col", "row"),
            P("col", "row"),
            P("row", "col"),
            P("row", "col"),
        ),
        out_specs=(
            P("row", "col"),
            P("row", "col"),
            P("col", "row"),
            P("col", "row"),
            P("row", "col"),
        ),
        check_vma=False,
    )
```

profile of v0, /device:TPU:1, one launch (start us, length us, event | category | flops | bytes accessed | tf_op | source)
XLA Modules:
  0.0 155.6 jit_solution(10834024724412048608)
XLA Ops:
  0.6 3.9 %collective-permute-start.1 = (bf16[24,1024]{1,0:T(8,128)(2,1)}, bf16[24,1024]{1,0:T(8,128)(2,1)S(1)}, u32[]{:S(2)}, u32[]{:S(2)}) collective-permute-start(bf16[24,1024]{1,0:T(8,128)(2,1)} %a.1), channel_id=1, source_target_pairs={{0,128},{8,136},{16,144},{24,152},{32,160},{40,168},{48,176},{56,1... | collective-permute-start | bytes 147464 | tf_op jit(solution)/shard_map/ppermute | solution.py:36
  4.5 1.6 %collective-permute-start = (bf16[24,1024]{1,0:T(8,128)(2,1)}, bf16[24,1024]{1,0:T(8,128)(2,1)S(1)}, u32[]{:S(2)}, u32[]{:S(2)}) collective-permute-start(bf16[24,1024]{1,0:T(8,128)(2,1)} %a.1), channel_id=1, source_target_pairs={{0,64},{8,72},{16,80},{24,88},{32,96},{40,104},{48,112},{56,120},{... | collective-permute-start | bytes 147464 | tf_op jit(solution)/shard_map/ppermute | solution.py:36
  6.2 1.6 %collective-permute-start.2 = (bf16[24,1024]{1,0:T(8,128)(2,1)}, bf16[24,1024]{1,0:T(8,128)(2,1)S(1)}, u32[]{:S(2)}, u32[]{:S(2)}) collective-permute-start(bf16[24,1024]{1,0:T(8,128)(2,1)} %a.1), channel_id=1, source_target_pairs={{0,192},{8,200},{16,208},{24,216},{32,224},{40,232},{48,240},{56,2... | collective-permute-start | bytes 147464 | tf_op jit(solution)/shard_map/ppermute | solution.py:36
  7.8 1.8 %collective-permute-done.b = bf16[24,1024]{1,0:T(8,128)(2,1)S(1)} collective-permute-done((bf16[24,1024]{1,0:T(8,128)(2,1)}, bf16[24,1024]{1,0:T(8,128)(2,1)S(1)}, u32[]{:S(2)}, u32[]{:S(2)}) %collective-permute-start) | collective-permute-done | bytes 49184 | tf_op jit(solution)/shard_map/ppermute | solution.py:36
  9.6 0.8 collective-permute-done.2.d
  10.5 0.8 copy-done
  11.3 2.0 %collective-permute-start.5 = (bf16[96,1024]{1,0:T(8,128)(2,1)S(1)}, bf16[96,1024]{1,0:T(8,128)(2,1)S(1)}, u32[]{:S(2)}, u32[]{:S(2)}) collective-permute-start(bf16[96,1024]{1,0:T(8,128)(2,1)S(1)} %shard_map.92.refs_1_.refs_0_), channel_id=1, source_target_pairs={{0,48},{8,56},{16,0},{24,8},{32,16},{40,24},{48,32},{56,40},{64,11... | collective-permute-start | bytes 589832 | tf_op jit(solution)/shard_map/ppermute | solution.py:40
  13.7 0.6 collective-permute-start.3
  14.4 0.8 copy-done.1
  15.2 3.3 %collective-permute-start.8 = (bf16[24,1024]{1,0:T(8,128)(2,1)S(1)}, bf16[24,1024]{1,0:T(8,128)(2,1)S(1)}, u32[]{:S(2)}, u32[]{:S(2)}) collective-permute-start(bf16[24,1024]{1,0:T(8,128)(2,1)S(1)} %shard_map.93.a), channel_id=1, source_target_pairs={{0,192},{8,200},{16,208},{24,216},{32,224},{40,232},{48,240},{56,2... | collective-permute-start | bytes 147464 | tf_op jit(solution)/shard_map/ppermute | solution.py:36
  18.5 1.2 collective-permute-done.8.d
  19.6 3.0 %collective-permute-done.7.c = bf16[24,1024]{1,0:T(8,128)(2,1)S(1)} collective-permute-done((bf16[24,1024]{1,0:T(8,128)(2,1)S(1)}, bf16[24,1024]{1,0:T(8,128)(2,1)S(1)}, u32[]{:S(2)}, u32[]{:S(2)}) %collective-permute-start.7) | collective-permute-done | bytes 49184 | tf_op jit(solution)/shard_map/ppermute | solution.py:36
  22.6 2.1 %collective-permute-done.6.b = bf16[24,1024]{1,0:T(8,128)(2,1)S(1)} collective-permute-done((bf16[24,1024]{1,0:T(8,128)(2,1)S(1)}, bf16[24,1024]{1,0:T(8,128)(2,1)S(1)}, u32[]{:S(2)}, u32[]{:S(2)}) %collective-permute-start.6) | collective-permute-done | bytes 49184 | tf_op jit(solution)/shard_map/ppermute | solution.py:36
  24.8 5.0 %collective-permute-start.9 = (bf16[384,1024]{1,0:T(8,128)(2,1)S(1)}, bf16[384,1024]{1,0:T(8,128)(2,1)}, u32[]{:S(2)}, u32[]{:S(2)}) collective-permute-start(bf16[384,1024]{1,0:T(8,128)(2,1)S(1)} %shard_map.95.mine), channel_id=1, source_target_pairs={{0,8},{8,0},{16,24},{24,16},{32,40},{40,32},{48,56},{56,48},{64,72... | collective-permute-start | bytes 2359304 | tf_op jit(solution)/shard_map/ppermute | solution.py:44
  29.9 2.0 %collective-permute-done.9.theirs = bf16[384,1024]{1,0:T(8,128)(2,1)} collective-permute-done((bf16[384,1024]{1,0:T(8,128)(2,1)S(1)}, bf16[384,1024]{1,0:T(8,128)(2,1)}, u32[]{:S(2)}, u32[]{:S(2)}) %collective-permute-start.9) | collective-permute-done | bytes 786464 | tf_op jit(solution)/shard_map/ppermute | solution.py:44
  31.9 3.1 %shard_map.96 = (bf16[768,1024]{1,0:T(8,128)(2,1)S(1)}, bf16[192,1024]{1,0:T(8,128)(2,1)S(1)}, bf16[192,1024]{1,0:T(8,128)(2,1)S(1)}, bf16[192,1024]{1,0:T(8,128)(2,1)S(1)}, f32[192,1024]{1,0:T(8,128)S(1)}) custom-call(s32[1]{0:T(128)} %bitcast.y.refs_0_, bf16[384,1024]{1,0:T(8,128)(2,1)S(1)} %shard_map.95.mine, ...), custom_call_target="tpu_custom_call" | custom-call | flops 1610612736 | bytes 7208960 | tf_op jit(solution)/shard_map/pallas_call | solution.py:79
  35.0 2.2 %collective-permute-start.15 = (bf16[96,1024]{1,0:T(8,128)(2,1)S(1)}, bf16[96,1024]{1,0:T(8,128)(2,1)S(1)}, u32[]{:S(2)}, u32[]{:S(2)}) collective-permute-start(bf16[96,1024]{1,0:T(8,128)(2,1)S(1)} %shard_map.97.refs_0_), channel_id=1, source_target_pairs={{0,48},{8,56},{16,0},{24,8},{32,16},{40,24},{48,32},{56,40},{64,11... | collective-permute-start | bytes 589832 | tf_op jit(solution)/shard_map/ppermute | solution.py:40
  37.2 2.9 %collective-permute-start.11 = (bf16[192,1024]{1,0:T(8,128)(2,1)S(1)}, bf16[192,1024]{1,0:T(8,128)(2,1)S(1)}, u32[]{:S(2)}, u32[]{:S(2)}) collective-permute-start(bf16[192,1024]{1,0:T(8,128)(2,1)S(1)} %get-tuple-element.47), channel_id=1, source_target_pairs={{0,2},{1,3},{2,0},{3,1},{4,6},{5,7},{6,4},{7,5},{8,10},{9,11},{10,... | collective-permute-start | bytes 1179656 | tf_op jit(solution)/shard_map/ppermute | solution.py:48
  40.1 0.8 collective-permute-start.12
  40.9 0.7 collective-permute-start.10
  41.6 1.2 collective-permute-start.14
  42.8 5.2 %collective-permute-done.14.refs_5_.refs_2_ = bf16[96,1024]{1,0:T(8,128)(2,1)S(1)} collective-permute-done((bf16[96,1024]{1,0:T(8,128)(2,1)S(1)}, bf16[96,1024]{1,0:T(8,128)(2,1)S(1)}, u32[]{:S(2)}, u32[]{:S(2)}) %collective-permute-start.14) | collective-permute-done | bytes 196640 | tf_op jit(solution)/shard_map/ppermute | solution.py:40
  48.0 5.7 %collective-permute-done.13.refs_4_.refs_1_ = bf16[96,1024]{1,0:T(8,128)(2,1)S(1)} collective-permute-done((bf16[96,1024]{1,0:T(8,128)(2,1)S(1)}, bf16[96,1024]{1,0:T(8,128)(2,1)S(1)}, u32[]{:S(2)}, u32[]{:S(2)}) %collective-permute-start.13) | collective-permute-done | bytes 196640 | tf_op jit(solution)/shard_map/ppermute | solution.py:40
  53.7 3.8 %collective-permute-done.12.refs_3_.refs_6_ = bf16[192,1024]{1,0:T(8,128)(2,1)S(1)} collective-permute-done((bf16[192,1024]{1,0:T(8,128)(2,1)S(1)}, bf16[192,1024]{1,0:T(8,128)(2,1)S(1)}, u32[]{:S(2)}, u32[]{:S(2)}) %collective-permute-start.12) | collective-permute-done | bytes 393248 | tf_op jit(solution)/shard_map/ppermute | solution.py:48
  57.5 0.7 collective-permute-done.10.refs_1_.refs_4_
  58.3 1.0 collective-permute-start.17
  59.4 5.1 %collective-permute-start.16 = (bf16[192,1024]{1,0:T(8,128)(2,1)S(1)}, bf16[192,1024]{1,0:T(8,128)(2,1)S(1)}, u32[]{:S(2)}, u32[]{:S(2)}) collective-permute-start(bf16[192,1024]{1,0:T(8,128)(2,1)S(1)} %get-tuple-element.50), channel_id=1, source_target_pairs={{0,4},{1,5},{2,6},{3,7},{4,0},{5,1},{6,2},{7,3},{8,12},{9,13},{10,... | collective-permute-start | bytes 1179656 | tf_op jit(solution)/shard_map/ppermute | solution.py:52
  64.6 1.5 shard_map.100
  66.1 1.1 collective-permute-start.18
  67.3 2.5 %collective-permute-start.19 = (bf16[192,512]{1,0:T(8,128)(2,1)S(1)}, bf16[192,512]{1,0:T(8,128)(2,1)S(1)}, u32[]{:S(2)}, u32[]{:S(2)}) collective-permute-start(bf16[192,512]{1,0:T(8,128)(2,1)S(1)} %get-tuple-element.52), channel_id=1, source_target_pairs={{0,2},{1,3},{2,0},{3,1},{4,6},{5,7},{6,4},{7,5},{8,10},{9,11},{10,... | collective-permute-start | bytes 589832 | tf_op jit(solution)/shard_map/ppermute | solution.py:48
  69.8 1.1 collective-permute-start.20
  70.8 8.1 %collective-permute-done.16.refs_1_.refs_4_ = bf16[192,1024]{1,0:T(8,128)(2,1)S(1)} collective-permute-done((bf16[192,1024]{1,0:T(8,128)(2,1)S(1)}, bf16[192,1024]{1,0:T(8,128)(2,1)S(1)}, u32[]{:S(2)}, u32[]{:S(2)}) %collective-permute-start.16) | collective-permute-done | bytes 393248 | tf_op jit(solution)/shard_map/ppermute | solution.py:52
  79.0 5.4 %collective-permute-start.24 = (bf16[192,512]{1,0:T(8,128)(2,1)S(1)}, bf16[192,512]{1,0:T(8,128)(2,1)S(1)}, u32[]{:S(2)}, u32[]{:S(2)}) collective-permute-start(bf16[192,512]{1,0:T(8,128)(2,1)S(1)} %get-tuple-element.55), channel_id=1, source_target_pairs={{0,4},{1,5},{2,6},{3,7},{4,0},{5,1},{6,2},{7,3},{8,12},{9,13},{10,... | collective-permute-start | bytes 589832 | tf_op jit(solution)/shard_map/ppermute | solution.py:52
  84.6 2.4 %collective-permute-start.23 = (bf16[192,512]{1,0:T(8,128)(2,1)S(1)}, bf16[192,512]{1,0:T(8,128)(2,1)S(1)}, u32[]{:S(2)}, u32[]{:S(2)}) collective-permute-start(bf16[192,512]{1,0:T(8,128)(2,1)S(1)} %shard_map.101.refs_1_), channel_id=1, source_target_pairs={{0,3},{1,0},{2,1},{3,2},{4,7},{5,4},{6,5},{7,6},{8,11},{9,8},{10,9... | collective-permute-start | bytes 589832 | tf_op jit(solution)/shard_map/ppermute | solution.py:48
  88.1 1.6 %collective-permute-done.24.refs_6_.refs_3_ = bf16[192,512]{1,0:T(8,128)(2,1)S(1)} collective-permute-done((bf16[192,512]{1,0:T(8,128)(2,1)S(1)}, bf16[192,512]{1,0:T(8,128)(2,1)S(1)}, u32[]{:S(2)}, u32[]{:S(2)}) %collective-permute-start.24) | collective-permute-done | bytes 196640 | tf_op jit(solution)/shard_map/ppermute | solution.py:52
  89.6 1.3 collective-permute-done.23.refs_4_.refs_6_
  91.0 2.6 %collective-permute-done.22.refs_3_.refs_5_ = bf16[192,512]{1,0:T(8,128)(2,1)S(1)} collective-permute-done((bf16[192,512]{1,0:T(8,128)(2,1)S(1)}, bf16[192,512]{1,0:T(8,128)(2,1)S(1)}, u32[]{:S(2)}, u32[]{:S(2)}) %collective-permute-start.22) | collective-permute-done | bytes 196640 | tf_op jit(solution)/shard_map/ppermute | solution.py:48
  93.6 6.0 %collective-permute-done.21.refs_2_.refs_4_ = bf16[192,512]{1,0:T(8,128)(2,1)S(1)} collective-permute-done((bf16[192,512]{1,0:T(8,128)(2,1)S(1)}, bf16[192,512]{1,0:T(8,128)(2,1)S(1)}, u32[]{:S(2)}, u32[]{:S(2)}) %collective-permute-start.21) | collective-permute-done | bytes 196640 | tf_op jit(solution)/shard_map/ppermute | solution.py:48
  99.6 1.0 shard_map.103
  100.6 0.6 collective-permute-start.25
  102.3 0.7 collective-permute-start.29
  102.9 1.2 collective-permute-done.25.theirs
  104.7 1.3 collective-permute-start.27
  106.0 6.2 %collective-permute-done.31.refs_6_.refs_4_ = bf16[192,1024]{1,0:T(8,128)(2,1)S(1)} collective-permute-done((bf16[192,1024]{1,0:T(8,128)(2,1)S(1)}, bf16[192,1024]{1,0:T(8,128)(2,1)S(1)}, u32[]{:S(2)}, u32[]{:S(2)}) %collective-permute-start.31) | collective-permute-done | bytes 393248 | tf_op jit(solution)/shard_map/ppermute | solution.py:48
  112.2 1.5 collective-permute-done.30.refs_5_.refs_3_
  113.8 9.0 %collective-permute-done.29.refs_4_.refs_2_ = bf16[192,1024]{1,0:T(8,128)(2,1)S(1)} collective-permute-done((bf16[192,1024]{1,0:T(8,128)(2,1)S(1)}, bf16[192,1024]{1,0:T(8,128)(2,1)S(1)}, u32[]{:S(2)}, u32[]{:S(2)}) %collective-permute-start.29) | collective-permute-done | bytes 393248 | tf_op jit(solution)/shard_map/ppermute | solution.py:48
  122.8 1.9 %shard_map.107 = (bf16[768,512]{1,0:T(8,128)(2,1)S(1)}, bf16[768,512]{1,0:T(8,128)(2,1)S(1)}, f32[384,1024]{1,0:T(8,128)S(1)}, f32[384,1024]{1,0:T(8,128)S(1)}) custom-call(s32[1]{0:T(128)} %bitcast.y.refs_0_, bf16[192,1024]{1,0:T(8,128)(2,1)S(1)} %shard_map.105.refs_1_, bf16[192,1024]{1,0:T(8,128)(2,1)S(1)} %collective-permute-done.29.refs_4_.refs_2_, ...), custom_call_target="tpu_custom_call" | custom-call | flops 1610612736 | bytes 8388608 | tf_op jit(solution)/shard_map/pallas_call | solution.py:79
  124.7 0.6 collective-permute-start.32
  125.3 2.9 %collective-permute-done.32.theirs = f32[384,1024]{1,0:T(8,128)S(1)} collective-permute-done((f32[384,1024]{1,0:T(8,128)S(1)}, f32[384,1024]{1,0:T(8,128)S(1)}, u32[]{:S(2)}, u32[]{:S(2)}) %collective-permute-start.32) | collective-permute-done | bytes 1572896 | tf_op jit(solution)/shard_map/ppermute | solution.py:44
  128.4 1.1 collective-permute-start.33
  129.6 2.0 %convolution_convert_fusion = bf16[512,1024]{1,0:T(8,128)(2,1)} fusion(bf16[768,512]{1,0:T(8,128)(2,1)S(1)} %get-tuple-element.83, bf16[768,1024]{1,0:T(8,128)(2,1)S(1)} %get-tuple-element.84), kind=kOutput, calls=%fused_computation | convolution fusion | flops 805830656 | bytes 3407872 | tf_op jit(solution)/shard_map/dot_general | solution.py:56
  131.7 2.4 %collective-permute-start.34 = (bf16[24,1024]{1,0:T(8,128)(2,1)S(1)}, bf16[24,1024]{1,0:T(8,128)(2,1)S(1)}, u32[]{:S(2)}, u32[]{:S(2)}) collective-permute-start(bf16[24,1024]{1,0:T(8,128)(2,1)S(1)} %get-tuple-element.71), channel_id=1, source_target_pairs={{0,128},{8,136},{16,144},{24,152},{32,160},{40,168},{48,176},{56,1... | collective-permute-start | bytes 147464 | tf_op jit(solution)/shard_map/ppermute | solution.py:36
  134.0 1.5 collective-permute-start.35
  135.5 1.2 collective-permute-start.37
  136.7 0.8 collective-permute-start.38
  137.5 2.0 %convolution_convert_fusion.2 = bf16[1024,512]{1,0:T(8,128)(2,1)} fusion(bf16[768,1024]{1,0:T(8,128)(2,1)S(1)} %get-tuple-element.80, bf16[768,512]{1,0:T(8,128)(2,1)S(1)} %get-tuple-element.81), kind=kOutput, calls=%fused_computation.2 | convolution fusion | flops 805830656 | bytes 3407872 | tf_op jit(solution)/shard_map/dot_general | solution.py:56
  139.5 2.4 %collective-permute-done.37.refs_2_ = bf16[96,1024]{1,0:T(8,128)(2,1)S(1)} collective-permute-done((bf16[96,1024]{1,0:T(8,128)(2,1)S(1)}, bf16[96,1024]{1,0:T(8,128)(2,1)S(1)}, u32[]{:S(2)}, u32[]{:S(2)}) %collective-permute-start.37) | collective-permute-done | bytes 196640 | tf_op jit(solution)/shard_map/ppermute | solution.py:40
  141.9 5.7 %collective-permute-done.38.refs_3_ = bf16[96,1024]{1,0:T(8,128)(2,1)S(1)} collective-permute-done((bf16[96,1024]{1,0:T(8,128)(2,1)S(1)}, bf16[96,1024]{1,0:T(8,128)(2,1)S(1)}, u32[]{:S(2)}, u32[]{:S(2)}) %collective-permute-start.38) | collective-permute-done | bytes 196640 | tf_op jit(solution)/shard_map/ppermute | solution.py:40
  147.6 2.2 %collective-permute-start.39 = (bf16[24,1024]{1,0:T(8,128)(2,1)S(1)}, bf16[24,1024]{1,0:T(8,128)(2,1)S(1)}, u32[]{:S(2)}, u32[]{:S(2)}) collective-permute-start(bf16[24,1024]{1,0:T(8,128)(2,1)S(1)} %get-tuple-element.77), channel_id=1, source_target_pairs={{0,192},{8,200},{16,208},{24,216},{32,224},{40,232},{48,240},{56,2... | collective-permute-start | bytes 147464 | tf_op jit(solution)/shard_map/ppermute | solution.py:36
  150.2 2.0 %convolution_convert_fusion.1 = bf16[1024,512]{1,0:T(8,128)(2,1)} fusion(bf16[768,1024]{1,0:T(8,128)(2,1)S(1)} %get-tuple-element.80, bf16[768,512]{1,0:T(8,128)(2,1)S(1)} %get-tuple-element.82), kind=kOutput, calls=%fused_computation.1 | convolution fusion | flops 805830656 | bytes 3407872 | tf_op jit(solution)/shard_map/dot_general | solution.py:56
  152.2 0.6 shard_map.110
  152.9 0.8 collective-permute-done.40.b
  153.7 1.3 collective-permute-done.41.c
  155.0 0.6 shard_map.112
  (54 shorter events, 4.7 us)
Async XLA Ops:
  0.6 7.2 %collective-permute-start.1 = (bf16[24,1024]{1,0:T(8,128)(2,1)}, bf16[24,1024]{1,0:T(8,128)(2,1)S(1)}, u32[]{:S(2)}, u32[]{:S(2)}) collective-permute-start(bf16[24,1024]{1,0:T(8,128)(2,1)} %a.1), channel_id=1, source_target_pairs={{0,128},{8,136},{16,144},{24,152},{32,160},{40,168},{48,176},{56,1... | collective-permute-start | bytes 147464 | tf_op jit(solution)/shard_map/ppermute | solution.py:36
  4.5 5.1 %collective-permute-start = (bf16[24,1024]{1,0:T(8,128)(2,1)}, bf16[24,1024]{1,0:T(8,128)(2,1)S(1)}, u32[]{:S(2)}, u32[]{:S(2)}) collective-permute-start(bf16[24,1024]{1,0:T(8,128)(2,1)} %a.1), channel_id=1, source_target_pairs={{0,64},{8,72},{16,80},{24,88},{32,96},{40,104},{48,112},{56,120},{... | collective-permute-start | bytes 147464 | tf_op jit(solution)/shard_map/ppermute | solution.py:36
  6.2 4.3 %collective-permute-start.2 = (bf16[24,1024]{1,0:T(8,128)(2,1)}, bf16[24,1024]{1,0:T(8,128)(2,1)S(1)}, u32[]{:S(2)}, u32[]{:S(2)}) collective-permute-start(bf16[24,1024]{1,0:T(8,128)(2,1)} %a.1), channel_id=1, source_target_pairs={{0,192},{8,200},{16,208},{24,216},{32,224},{40,232},{48,240},{56,2... | collective-permute-start | bytes 147464 | tf_op jit(solution)/shard_map/ppermute | solution.py:36
  10.5 0.8 copy-start
  11.3 13.5 %collective-permute-start.5 = (bf16[96,1024]{1,0:T(8,128)(2,1)S(1)}, bf16[96,1024]{1,0:T(8,128)(2,1)S(1)}, u32[]{:S(2)}, u32[]{:S(2)}) collective-permute-start(bf16[96,1024]{1,0:T(8,128)(2,1)S(1)} %shard_map.92.refs_1_.refs_0_), channel_id=1, source_target_pairs={{0,48},{8,56},{16,0},{24,8},{32,16},{40,24},{48,32},{56,40},{64,11... | collective-permute-start | bytes 589832 | tf_op jit(solution)/shard_map/ppermute | solution.py:40
  13.2 11.5 %collective-permute-start.4 = (bf16[96,1024]{1,0:T(8,128)(2,1)S(1)}, bf16[96,1024]{1,0:T(8,128)(2,1)S(1)}, u32[]{:S(2)}, u32[]{:S(2)}) collective-permute-start(bf16[96,1024]{1,0:T(8,128)(2,1)S(1)} %shard_map.92.refs_1_.refs_0_), channel_id=1, source_target_pairs={{0,32},{8,40},{16,48},{24,56},{32,0},{40,8},{48,16},{56,24},{64,96... | collective-permute-start | bytes 589832 | tf_op jit(solution)/shard_map/ppermute | solution.py:40
  13.7 11.0 %collective-permute-start.3 = (bf16[96,1024]{1,0:T(8,128)(2,1)S(1)}, bf16[96,1024]{1,0:T(8,128)(2,1)S(1)}, u32[]{:S(2)}, u32[]{:S(2)}) collective-permute-start(bf16[96,1024]{1,0:T(8,128)(2,1)S(1)} %shard_map.92.refs_1_.refs_0_), channel_id=1, source_target_pairs={{0,16},{8,24},{16,32},{24,40},{32,48},{40,56},{48,0},{56,8},{64,80... | collective-permute-start | bytes 589832 | tf_op jit(solution)/shard_map/ppermute | solution.py:40
  14.4 0.8 copy-start.1
  15.2 16.7 %copy-start.3 = (bf16[1024,512]{1,0:T(8,128)(2,1)S(1)}, bf16[1024,512]{1,0:T(8,128)(2,1)}, u32[]{:S(2)}) copy-start(bf16[1024,512]{1,0:T(8,128)(2,1)} %refs_5_.3) | copy-start | bytes 3145732
  15.2 16.7 %copy-start.4 = (bf16[1024,512]{1,0:T(8,128)(2,1)S(1)}, bf16[1024,512]{1,0:T(8,128)(2,1)}, u32[]{:S(2)}) copy-start(bf16[1024,512]{1,0:T(8,128)(2,1)} %refs_6_.1) | copy-start | bytes 3145732
  15.2 4.5 %collective-permute-start.8 = (bf16[24,1024]{1,0:T(8,128)(2,1)S(1)}, bf16[24,1024]{1,0:T(8,128)(2,1)S(1)}, u32[]{:S(2)}, u32[]{:S(2)}) collective-permute-start(bf16[24,1024]{1,0:T(8,128)(2,1)S(1)} %shard_map.93.a), channel_id=1, source_target_pairs={{0,192},{8,200},{16,208},{24,216},{32,224},{40,232},{48,240},{56,2... | collective-permute-start | bytes 147464 | tf_op jit(solution)/shard_map/ppermute | solution.py:36
  18.5 4.1 %collective-permute-start.7 = (bf16[24,1024]{1,0:T(8,128)(2,1)S(1)}, bf16[24,1024]{1,0:T(8,128)(2,1)S(1)}, u32[]{:S(2)}, u32[]{:S(2)}) collective-permute-start(bf16[24,1024]{1,0:T(8,128)(2,1)S(1)} %shard_map.93.a), channel_id=1, source_target_pairs={{0,128},{8,136},{16,144},{24,152},{32,160},{40,168},{48,176},{56,1... | collective-permute-start | bytes 147464 | tf_op jit(solution)/shard_map/ppermute | solution.py:36
  19.6 5.1 %collective-permute-start.6 = (bf16[24,1024]{1,0:T(8,128)(2,1)S(1)}, bf16[24,1024]{1,0:T(8,128)(2,1)S(1)}, u32[]{:S(2)}, u32[]{:S(2)}) collective-permute-start(bf16[24,1024]{1,0:T(8,128)(2,1)S(1)} %shard_map.93.a), channel_id=1, source_target_pairs={{0,64},{8,72},{16,80},{24,88},{32,96},{40,104},{48,112},{56,120},{... | collective-permute-start | bytes 147464 | tf_op jit(solution)/shard_map/ppermute | solution.py:36
  24.8 7.1 %collective-permute-start.9 = (bf16[384,1024]{1,0:T(8,128)(2,1)S(1)}, bf16[384,1024]{1,0:T(8,128)(2,1)}, u32[]{:S(2)}, u32[]{:S(2)}) collective-permute-start(bf16[384,1024]{1,0:T(8,128)(2,1)S(1)} %shard_map.95.mine), channel_id=1, source_target_pairs={{0,8},{8,0},{16,24},{24,16},{32,40},{40,32},{48,56},{56,48},{64,72... | collective-permute-start | bytes 2359304 | tf_op jit(solution)/shard_map/ppermute | solution.py:44
  35.0 7.8 %collective-permute-start.15 = (bf16[96,1024]{1,0:T(8,128)(2,1)S(1)}, bf16[96,1024]{1,0:T(8,128)(2,1)S(1)}, u32[]{:S(2)}, u32[]{:S(2)}) collective-permute-start(bf16[96,1024]{1,0:T(8,128)(2,1)S(1)} %shard_map.97.refs_0_), channel_id=1, source_target_pairs={{0,48},{8,56},{16,0},{24,8},{32,16},{40,24},{48,32},{56,40},{64,11... | collective-permute-start | bytes 589832 | tf_op jit(solution)/shard_map/ppermute | solution.py:40
  37.2 16.5 %collective-permute-start.11 = (bf16[192,1024]{1,0:T(8,128)(2,1)S(1)}, bf16[192,1024]{1,0:T(8,128)(2,1)S(1)}, u32[]{:S(2)}, u32[]{:S(2)}) collective-permute-start(bf16[192,1024]{1,0:T(8,128)(2,1)S(1)} %get-tuple-element.47), channel_id=1, source_target_pairs={{0,2},{1,3},{2,0},{3,1},{4,6},{5,7},{6,4},{7,5},{8,10},{9,11},{10,... | collective-permute-start | bytes 1179656 | tf_op jit(solution)/shard_map/ppermute | solution.py:48
  40.1 17.4 %collective-permute-start.12 = (bf16[192,1024]{1,0:T(8,128)(2,1)S(1)}, bf16[192,1024]{1,0:T(8,128)(2,1)S(1)}, u32[]{:S(2)}, u32[]{:S(2)}) collective-permute-start(bf16[192,1024]{1,0:T(8,128)(2,1)S(1)} %get-tuple-element.48), channel_id=1, source_target_pairs={{0,3},{1,0},{2,1},{3,2},{4,7},{5,4},{6,5},{7,6},{8,11},{9,8},{10,9... | collective-permute-start | bytes 1179656 | tf_op jit(solution)/shard_map/ppermute | solution.py:48
  40.9 17.3 %collective-permute-start.10 = (bf16[192,1024]{1,0:T(8,128)(2,1)S(1)}, bf16[192,1024]{1,0:T(8,128)(2,1)S(1)}, u32[]{:S(2)}, u32[]{:S(2)}) collective-permute-start(bf16[192,1024]{1,0:T(8,128)(2,1)S(1)} %get-tuple-element.46.refs_1_), channel_id=1, source_target_pairs={{0,1},{1,2},{2,3},{3,0},{4,5},{5,6},{6,7},{7,4},{8,9},{9,10},{10,1... | collective-permute-start | bytes 1179656 | tf_op jit(solution)/shard_map/ppermute | solution.py:48
  41.6 6.4 %collective-permute-start.14 = (bf16[96,1024]{1,0:T(8,128)(2,1)S(1)}, bf16[96,1024]{1,0:T(8,128)(2,1)S(1)}, u32[]{:S(2)}, u32[]{:S(2)}) collective-permute-start(bf16[96,1024]{1,0:T(8,128)(2,1)S(1)} %shard_map.97.refs_0_), channel_id=1, source_target_pairs={{0,32},{8,40},{16,48},{24,56},{32,0},{40,8},{48,16},{56,24},{64,96... | collective-permute-start | bytes 589832 | tf_op jit(solution)/shard_map/ppermute | solution.py:40
  42.8 10.9 %collective-permute-start.13 = (bf16[96,1024]{1,0:T(8,128)(2,1)S(1)}, bf16[96,1024]{1,0:T(8,128)(2,1)S(1)}, u32[]{:S(2)}, u32[]{:S(2)}) collective-permute-start(bf16[96,1024]{1,0:T(8,128)(2,1)S(1)} %shard_map.97.refs_0_), channel_id=1, source_target_pairs={{0,16},{8,24},{16,32},{24,40},{32,48},{40,56},{48,0},{56,8},{64,80... | collective-permute-start | bytes 589832 | tf_op jit(solution)/shard_map/ppermute | solution.py:40
  58.2 6.4 %copy-start.2 = (bf16[512,1024]{1,0:T(8,128)(2,1)S(1)}, bf16[512,1024]{1,0:T(8,128)(2,1)}, u32[]{:S(2)}) copy-start(bf16[512,1024]{1,0:T(8,128)(2,1)} %refs_5_.2) | copy-start | bytes 3145732
  58.3 6.3 %collective-permute-start.17 = (bf16[384,1024]{1,0:T(8,128)(2,1)S(1)}, bf16[384,1024]{1,0:T(8,128)(2,1)S(1)}, u32[]{:S(2)}, u32[]{:S(2)}) collective-permute-start(bf16[384,1024]{1,0:T(8,128)(2,1)S(1)} %shard_map.99.mine), channel_id=1, source_target_pairs={{0,8},{8,0},{16,24},{24,16},{32,40},{40,32},{48,56},{56,48},{64,72... | collective-permute-start | bytes 2359304 | tf_op jit(solution)/shard_map/ppermute | solution.py:44
  59.4 19.4 %collective-permute-start.16 = (bf16[192,1024]{1,0:T(8,128)(2,1)S(1)}, bf16[192,1024]{1,0:T(8,128)(2,1)S(1)}, u32[]{:S(2)}, u32[]{:S(2)}) collective-permute-start(bf16[192,1024]{1,0:T(8,128)(2,1)S(1)} %get-tuple-element.50), channel_id=1, source_target_pairs={{0,4},{1,5},{2,6},{3,7},{4,0},{5,1},{6,2},{7,3},{8,12},{9,13},{10,... | collective-permute-start | bytes 1179656 | tf_op jit(solution)/shard_map/ppermute | solution.py:52
  66.1 12.8 %collective-permute-start.18 = (bf16[192,512]{1,0:T(8,128)(2,1)S(1)}, bf16[192,512]{1,0:T(8,128)(2,1)S(1)}, u32[]{:S(2)}, u32[]{:S(2)}) collective-permute-start(bf16[192,512]{1,0:T(8,128)(2,1)S(1)} %get-tuple-element.51), channel_id=1, source_target_pairs={{0,1},{1,2},{2,3},{3,0},{4,5},{5,6},{6,7},{7,4},{8,9},{9,10},{10,1... | collective-permute-start | bytes 589832 | tf_op jit(solution)/shard_map/ppermute | solution.py:48
  67.3 11.6 %collective-permute-start.19 = (bf16[192,512]{1,0:T(8,128)(2,1)S(1)}, bf16[192,512]{1,0:T(8,128)(2,1)S(1)}, u32[]{:S(2)}, u32[]{:S(2)}) collective-permute-start(bf16[192,512]{1,0:T(8,128)(2,1)S(1)} %get-tuple-element.52), channel_id=1, source_target_pairs={{0,2},{1,3},{2,0},{3,1},{4,6},{5,7},{6,4},{7,5},{8,10},{9,11},{10,... | collective-permute-start | bytes 589832 | tf_op jit(solution)/shard_map/ppermute | solution.py:48
  69.8 9.2 %collective-permute-start.20 = (bf16[192,512]{1,0:T(8,128)(2,1)S(1)}, bf16[192,512]{1,0:T(8,128)(2,1)S(1)}, u32[]{:S(2)}, u32[]{:S(2)}) collective-permute-start(bf16[192,512]{1,0:T(8,128)(2,1)S(1)} %get-tuple-element.53), channel_id=1, source_target_pairs={{0,3},{1,0},{2,1},{3,2},{4,7},{5,4},{6,5},{7,6},{8,11},{9,8},{10,9... | collective-permute-start | bytes 589832 | tf_op jit(solution)/shard_map/ppermute | solution.py:48
  79.0 10.6 %collective-permute-start.24 = (bf16[192,512]{1,0:T(8,128)(2,1)S(1)}, bf16[192,512]{1,0:T(8,128)(2,1)S(1)}, u32[]{:S(2)}, u32[]{:S(2)}) collective-permute-start(bf16[192,512]{1,0:T(8,128)(2,1)S(1)} %get-tuple-element.55), channel_id=1, source_target_pairs={{0,4},{1,5},{2,6},{3,7},{4,0},{5,1},{6,2},{7,3},{8,12},{9,13},{10,... | collective-permute-start | bytes 589832 | tf_op jit(solution)/shard_map/ppermute | solution.py:52
  84.6 6.4 %collective-permute-start.23 = (bf16[192,512]{1,0:T(8,128)(2,1)S(1)}, bf16[192,512]{1,0:T(8,128)(2,1)S(1)}, u32[]{:S(2)}, u32[]{:S(2)}) collective-permute-start(bf16[192,512]{1,0:T(8,128)(2,1)S(1)} %shard_map.101.refs_1_), channel_id=1, source_target_pairs={{0,3},{1,0},{2,1},{3,2},{4,7},{5,4},{6,5},{7,6},{8,11},{9,8},{10,9... | collective-permute-start | bytes 589832 | tf_op jit(solution)/shard_map/ppermute | solution.py:48
  87.0 6.5 %collective-permute-start.22 = (bf16[192,512]{1,0:T(8,128)(2,1)S(1)}, bf16[192,512]{1,0:T(8,128)(2,1)S(1)}, u32[]{:S(2)}, u32[]{:S(2)}) collective-permute-start(bf16[192,512]{1,0:T(8,128)(2,1)S(1)} %shard_map.101.refs_1_), channel_id=1, source_target_pairs={{0,2},{1,3},{2,0},{3,1},{4,6},{5,7},{6,4},{7,5},{8,10},{9,11},{10,... | collective-permute-start | bytes 589832 | tf_op jit(solution)/shard_map/ppermute | solution.py:48
  87.5 12.0 %collective-permute-start.21 = (bf16[192,512]{1,0:T(8,128)(2,1)S(1)}, bf16[192,512]{1,0:T(8,128)(2,1)S(1)}, u32[]{:S(2)}, u32[]{:S(2)}) collective-permute-start(bf16[192,512]{1,0:T(8,128)(2,1)S(1)} %shard_map.101.refs_1_), channel_id=1, source_target_pairs={{0,1},{1,2},{2,3},{3,0},{4,5},{5,6},{6,7},{7,4},{8,9},{9,10},{10,1... | collective-permute-start | bytes 589832 | tf_op jit(solution)/shard_map/ppermute | solution.py:48
  100.6 3.6 %collective-permute-start.25 = (f32[384,1024]{1,0:T(8,128)S(1)}, f32[384,1024]{1,0:T(8,128)S(1)}, u32[]{:S(2)}, u32[]{:S(2)}) collective-permute-start(f32[384,1024]{1,0:T(8,128)S(1)} %get-tuple-element.57), channel_id=1, source_target_pairs={{0,8},{8,0},{16,24},{24,16},{32,40},{40,32},{48,56},{56,48},{64,72... | collective-permute-start | bytes 4718600 | tf_op jit(solution)/shard_map/ppermute | solution.py:44
  101.4 10.8 %collective-permute-start.31 = (bf16[192,1024]{1,0:T(8,128)(2,1)S(1)}, bf16[192,1024]{1,0:T(8,128)(2,1)S(1)}, u32[]{:S(2)}, u32[]{:S(2)}) collective-permute-start(bf16[192,1024]{1,0:T(8,128)(2,1)S(1)} %shard_map.105.refs_1_), channel_id=1, source_target_pairs={{0,3},{1,0},{2,1},{3,2},{4,7},{5,4},{6,5},{7,6},{8,11},{9,8},{10,9... | collective-permute-start | bytes 1179656 | tf_op jit(solution)/shard_map/ppermute | solution.py:48
  101.8 12.0 %collective-permute-start.30 = (bf16[192,1024]{1,0:T(8,128)(2,1)S(1)}, bf16[192,1024]{1,0:T(8,128)(2,1)S(1)}, u32[]{:S(2)}, u32[]{:S(2)}) collective-permute-start(bf16[192,1024]{1,0:T(8,128)(2,1)S(1)} %shard_map.105.refs_1_), channel_id=1, source_target_pairs={{0,2},{1,3},{2,0},{3,1},{4,6},{5,7},{6,4},{7,5},{8,10},{9,11},{10,... | collective-permute-start | bytes 1179656 | tf_op jit(solution)/shard_map/ppermute | solution.py:48
  102.3 20.5 %collective-permute-start.29 = (bf16[192,1024]{1,0:T(8,128)(2,1)S(1)}, bf16[192,1024]{1,0:T(8,128)(2,1)S(1)}, u32[]{:S(2)}, u32[]{:S(2)}) collective-permute-start(bf16[192,1024]{1,0:T(8,128)(2,1)S(1)} %shard_map.105.refs_1_), channel_id=1, source_target_pairs={{0,1},{1,2},{2,3},{3,0},{4,5},{5,6},{6,7},{7,4},{8,9},{9,10},{10,1... | collective-permute-start | bytes 1179656 | tf_op jit(solution)/shard_map/ppermute | solution.py:48
  104.3 18.5 %collective-permute-start.26 = (bf16[96,1024]{1,0:T(8,128)(2,1)S(1)}, bf16[96,1024]{1,0:T(8,128)(2,1)S(1)}, u32[]{:S(2)}, u32[]{:S(2)}) collective-permute-start(bf16[96,1024]{1,0:T(8,128)(2,1)S(1)} %get-tuple-element.59), channel_id=1, source_target_pairs={{0,48},{8,56},{16,0},{24,8},{32,16},{40,24},{48,32},{56,40},{64,11... | collective-permute-start | bytes 589832 | tf_op jit(solution)/shard_map/ppermute | solution.py:40
  104.7 18.1 %collective-permute-start.27 = (bf16[96,1024]{1,0:T(8,128)(2,1)S(1)}, bf16[96,1024]{1,0:T(8,128)(2,1)S(1)}, u32[]{:S(2)}, u32[]{:S(2)}) collective-permute-start(bf16[96,1024]{1,0:T(8,128)(2,1)S(1)} %get-tuple-element.60), channel_id=1, source_target_pairs={{0,32},{8,40},{16,48},{24,56},{32,0},{40,8},{48,16},{56,24},{64,96... | collective-permute-start | bytes 589832 | tf_op jit(solution)/shard_map/ppermute | solution.py:40
  112.2 10.6 %collective-permute-start.28 = (bf16[96,1024]{1,0:T(8,128)(2,1)S(1)}, bf16[96,1024]{1,0:T(8,128)(2,1)S(1)}, u32[]{:S(2)}, u32[]{:S(2)}) collective-permute-start(bf16[96,1024]{1,0:T(8,128)(2,1)S(1)} %get-tuple-element.61), channel_id=1, source_target_pairs={{0,16},{8,24},{16,32},{24,40},{32,48},{40,56},{48,0},{56,8},{64,80... | collective-permute-start | bytes 589832 | tf_op jit(solution)/shard_map/ppermute | solution.py:40
  124.7 3.6 %collective-permute-start.32 = (f32[384,1024]{1,0:T(8,128)S(1)}, f32[384,1024]{1,0:T(8,128)S(1)}, u32[]{:S(2)}, u32[]{:S(2)}) collective-permute-start(f32[384,1024]{1,0:T(8,128)S(1)} %get-tuple-element.68), channel_id=1, source_target_pairs={{0,8},{8,0},{16,24},{24,16},{32,40},{40,32},{48,56},{56,48},{64,72... | collective-permute-start | bytes 4718600 | tf_op jit(solution)/shard_map/ppermute | solution.py:44
  128.4 8.3 %collective-permute-start.33 = (bf16[24,1024]{1,0:T(8,128)(2,1)S(1)}, bf16[24,1024]{1,0:T(8,128)(2,1)S(1)}, u32[]{:S(2)}, u32[]{:S(2)}) collective-permute-start(bf16[24,1024]{1,0:T(8,128)(2,1)S(1)} %get-tuple-element.70), channel_id=1, source_target_pairs={{0,192},{8,200},{16,208},{24,216},{32,224},{40,232},{48,240},{56,2... | collective-permute-start | bytes 147464 | tf_op jit(solution)/shard_map/ppermute | solution.py:36
  131.6 16.0 %collective-permute-start.36 = (bf16[96,1024]{1,0:T(8,128)(2,1)S(1)}, bf16[96,1024]{1,0:T(8,128)(2,1)S(1)}, u32[]{:S(2)}, u32[]{:S(2)}) collective-permute-start(bf16[96,1024]{1,0:T(8,128)(2,1)S(1)} %get-tuple-element.69.refs_3_), channel_id=1, source_target_pairs={{0,48},{8,56},{16,0},{24,8},{32,16},{40,24},{48,32},{56,40},{64,11... | collective-permute-start | bytes 589832 | tf_op jit(solution)/shard_map/ppermute | solution.py:40
  131.7 7.8 %collective-permute-start.34 = (bf16[24,1024]{1,0:T(8,128)(2,1)S(1)}, bf16[24,1024]{1,0:T(8,128)(2,1)S(1)}, u32[]{:S(2)}, u32[]{:S(2)}) collective-permute-start(bf16[24,1024]{1,0:T(8,128)(2,1)S(1)} %get-tuple-element.71), channel_id=1, source_target_pairs={{0,128},{8,136},{16,144},{24,152},{32,160},{40,168},{48,176},{56,1... | collective-permute-start | bytes 147464 | tf_op jit(solution)/shard_map/ppermute | solution.py:36
  134.0 5.4 %collective-permute-start.35 = (bf16[24,1024]{1,0:T(8,128)(2,1)S(1)}, bf16[24,1024]{1,0:T(8,128)(2,1)S(1)}, u32[]{:S(2)}, u32[]{:S(2)}) collective-permute-start(bf16[24,1024]{1,0:T(8,128)(2,1)S(1)} %get-tuple-element.72), channel_id=1, source_target_pairs={{0,64},{8,72},{16,80},{24,88},{32,96},{40,104},{48,112},{56,120},{... | collective-permute-start | bytes 147464 | tf_op jit(solution)/shard_map/ppermute | solution.py:36
  135.5 6.4 %collective-permute-start.37 = (bf16[96,1024]{1,0:T(8,128)(2,1)S(1)}, bf16[96,1024]{1,0:T(8,128)(2,1)S(1)}, u32[]{:S(2)}, u32[]{:S(2)}) collective-permute-start(bf16[96,1024]{1,0:T(8,128)(2,1)S(1)} %get-tuple-element.74), channel_id=1, source_target_pairs={{0,32},{8,40},{16,48},{24,56},{32,0},{40,8},{48,16},{56,24},{64,96... | collective-permute-start | bytes 589832 | tf_op jit(solution)/shard_map/ppermute | solution.py:40
  136.7 10.8 %collective-permute-start.38 = (bf16[96,1024]{1,0:T(8,128)(2,1)S(1)}, bf16[96,1024]{1,0:T(8,128)(2,1)S(1)}, u32[]{:S(2)}, u32[]{:S(2)}) collective-permute-start(bf16[96,1024]{1,0:T(8,128)(2,1)S(1)} %get-tuple-element.75), channel_id=1, source_target_pairs={{0,16},{8,24},{16,32},{24,40},{32,48},{40,56},{48,0},{56,8},{64,80... | collective-permute-start | bytes 589832 | tf_op jit(solution)/shard_map/ppermute | solution.py:40
  147.6 5.2 %collective-permute-start.39 = (bf16[24,1024]{1,0:T(8,128)(2,1)S(1)}, bf16[24,1024]{1,0:T(8,128)(2,1)S(1)}, u32[]{:S(2)}, u32[]{:S(2)}) collective-permute-start(bf16[24,1024]{1,0:T(8,128)(2,1)S(1)} %get-tuple-element.77), channel_id=1, source_target_pairs={{0,192},{8,200},{16,208},{24,216},{32,224},{40,232},{48,240},{56,2... | collective-permute-start | bytes 147464 | tf_op jit(solution)/shard_map/ppermute | solution.py:36
  149.9 3.8 %collective-permute-start.40 = (bf16[24,1024]{1,0:T(8,128)(2,1)S(1)}, bf16[24,1024]{1,0:T(8,128)(2,1)S(1)}, u32[]{:S(2)}, u32[]{:S(2)}) collective-permute-start(bf16[24,1024]{1,0:T(8,128)(2,1)S(1)} %get-tuple-element.78), channel_id=1, source_target_pairs={{0,128},{8,136},{16,144},{24,152},{32,160},{40,168},{48,176},{56,1... | collective-permute-start | bytes 147464 | tf_op jit(solution)/shard_map/ppermute | solution.py:36
  149.9 5.1 %collective-permute-start.41 = (bf16[24,1024]{1,0:T(8,128)(2,1)S(1)}, bf16[24,1024]{1,0:T(8,128)(2,1)S(1)}, u32[]{:S(2)}, u32[]{:S(2)}) collective-permute-start(bf16[24,1024]{1,0:T(8,128)(2,1)S(1)} %get-tuple-element.79), channel_id=1, source_target_pairs={{0,64},{8,72},{16,80},{24,88},{32,96},{40,104},{48,112},{56,120},{... | collective-permute-start | bytes 147464 | tf_op jit(solution)/shard_map/ppermute | solution.py:36
where the time goes:
time: 156 us
  waiting for transfers between devices  77.1 us (49%)
  starting transfers between devices  60.1 us (39%)
  Pallas kernels  10.1 us (6%)
  matrix products  5.92 us (4%)
  local copies, waits for them, and re-layouts  1.61 us (1%)
    ppermute x12, waiting for transfers between devices, send_y(): return lax.ppermute(a, 'col', col_perm(lambda h, y: (h, y + k)))  31.2 us
    ppermute x12, waiting for transfers between devices, send_x(): return lax.ppermute(a, 'row', row_perm(lambda z, x, c: (z, x + k, c)))  19 us
    ppermute x12, starting transfers between devices, send_z(): return lax.ppermute(a, 'row', row_perm(lambda z, x, c: (z + k, x, c)))  18 us
    ppermute x12, starting transfers between devices, send_y(): return lax.ppermute(a, 'col', col_perm(lambda h, y: (h, y + k)))  14.1 us
    ppermute x12, waiting for transfers between devices, send_z(): return lax.ppermute(a, 'row', row_perm(lambda z, x, c: (z + k, x, c)))  11 us
    ppermute x2, starting transfers between devices, send_half(): return lax.ppermute(a, 'col', col_perm(lambda h, y: (h + 1, y)))  10.6 us
    ppermute x12, starting transfers between devices, send_x(): return lax.ppermute(a, 'row', row_perm(lambda z, x, c: (z, x + k, c)))  10.3 us
    pallas_call x21, Pallas kernels, call(): pl.pallas_call(body, out_shape=out_shape, in_specs=in_specs, out_specs=[v...  10.1 us
  transfers between devices with their start and end apart: 42, of which 24 were waited for; matrix products, arithmetic and copies ran while one was open for 4% of the time, Pallas kernels for 2%

commit v1 on v0

--- a/solution.py
+++ b/solution.py
@@ -32,24 +32,29 @@
     return pairs
 
 
-def send_z(a, k):
-    return lax.ppermute(a, "row", row_perm(lambda z, x, c: (z + k, x, c)))
-
-
-def send_x(a, k):
-    return lax.ppermute(a, "row", row_perm(lambda z, x, c: (z, x + k, c)))
-
-
-def send_core(a):
-    return lax.ppermute(a, "row", row_perm(lambda z, x, c: (z, x, c + 1)))
-
-
-def send_y(a, k):
-    return lax.ppermute(a, "col", col_perm(lambda h, y: (h, y + k)))
-
-
-def send_half(a):
-    return lax.ppermute(a, "col", col_perm(lambda h, y: (h + 1, y)))
+def send_z(a, k, name):
+    with jax.named_scope(name):
+        return lax.ppermute(a, "row", row_perm(lambda z, x, c: (z + k, x, c)))
+
+
+def send_x(a, k, name):
+    with jax.named_scope(name):
+        return lax.ppermute(a, "row", row_perm(lambda z, x, c: (z, x + k, c)))
+
+
+def send_core(a, name):
+    with jax.named_scope(name):
+        return lax.ppermute(a, "row", row_perm(lambda z, x, c: (z, x, c + 1)))
+
+
+def send_y(a, k, name):
+    with jax.named_scope(name):
+        return lax.ppermute(a, "col", col_perm(lambda h, y: (h, y + k)))
+
+
+def send_half(a, name):
+    with jax.named_scope(name):
+        return lax.ppermute(a, "col", col_perm(lambda h, y: (h + 1, y)))
 
 
 def dot(left, right, ldim, rdim):
@@ -78,6 +83,7 @@
 
     return pl.pallas_call(
         body,
+        name=kernel.__name__.removesuffix("_kernel"),
         out_shape=out_shape,
         in_specs=in_specs,
         out_specs=[vmem] * len(outs),
@@ -113,11 +119,10 @@
     return call(hold_kernel, [(a.shape, a.dtype) for a in args], list(args), after=after)
 
 
-def gather_z(a):
+def gather_z(a, got):
     n, w = a.shape
-    parts = [a] + [send_z(a, k) for k in (2, 1, 3)]
-    a, c, b, d = parts
-    return call(cat_z_kernel, [((Z * n, w), BF)], [a, b, c, d])[0]
+    own = hold([a], [])[0]
+    return call(cat_z_kernel, [((Z * n, w), BF)], [own, *got])[0]
 
 
 def gather_x(a, got, after=()):
@@ -125,14 +130,29 @@
     return call(cat_x_kernel, [((X * n, w), BF)], [a, *got], after=after)[0]
 
 
-def all_x(a):
-    c, b, d = [send_x(a, k) for k in (2, 1, 3)]
+def by_distance(send, sends, name, sign=1):
+    c, b, d = [send(sends[k - 1], sign * k, name) for k in (2, 1, 3)]
     return [b, c, d]
 
 
-def all_y(sends):
-    c, b, d = [send_y(sends[k - 1], k) for k in (2, 1, 3)]
-    return [b, c, d]
+def all_z(a, name):
+    return by_distance(send_z, [a] * 3, name)
+
+
+def all_x(a, name):
+    return by_distance(send_x, [a] * 3, name)
+
+
+def all_y(sends, name):
+    return by_distance(send_y, sends, name)
+
+
+def back_z(sends, name):
+    return by_distance(send_z, sends, name, -1)
+
+
+def back_x(sends, name):
+    return by_distance(send_x, sends, name, -1)
 
 
 def up_kernel(y, mine, theirs, wg, wu, whole, s1, s2, s3, own):
@@ -192,17 +212,20 @@
     own[...] = dot(whole[:half, :], wd[...], 1, 0)
 
 
-def tokens_kernel(y, a, b, c, d, wg, wu, gg, ug, own, theirs):
+def tokens_kernel(y, a, b, c, d, wg, wu, gg, ug, theirs):
     f = gg.shape[1]
     n = a.shape[0]
     for k, r in enumerate((a, b, c, d)):
         at = block_at(y[0] + Y - k, n)
         gg[at, :] = r[:, :f]
         ug[at, :] = r[:, f:]
+    half = theirs.shape[0]
+    theirs[...] = dot(gg[half:, :], wg[...], 1, 1) + dot(ug[half:, :], wu[...], 1, 1)
+
+
+def tokens_own_kernel(gg, ug, wg, wu, own):
     half = own.shape[0]
-    for o, at in ((theirs, slice(half, None)), (own, slice(0, half))):
-        t = dot(gg[at, :], wg[...], 1, 1) + dot(ug[at, :], wu[...], 1, 1)
-        o[...] = t.astype(o.dtype)
+    own[...] = dot(gg[:half, :], wg[...], 1, 1) + dot(ug[:half, :], wu[...], 1, 1)
 
 
 def rs_first_kernel(mine, theirs, s1, s2, s3, own):
@@ -212,16 +235,22 @@
         o[...] = (mine[at, :] + theirs[at, :].astype(F32)).astype(o.dtype)
 
 
-def rs_next_kernel(mine, a, b, c, s1, s2, s3, own):
-    n = own.shape[0]
+def rs_next_kernel(o0, oa, ob, oc, t0, ta, tb, tc, s1, s2, s3, own):
+    both = []
+    for mine, a, b, c in ((o0, oa, ob, oc), (t0, ta, tb, tc)):
+        t = mine[...] + a[...].astype(F32) + b[...].astype(F32)
+        both.append(t + c[...].astype(F32))
+    n = own.shape[0] // 2
+    for k, o in enumerate((own, s1, s2, s3)):
+        t = jnp.concatenate([t[k * n : (k + 1) * n] for t in both], axis=0)
+        o[...] = t.astype(o.dtype)
+
+
+def rs_last_kernel(mine, a, b, c, output, grad):
     t = mine[...] + a[...].astype(F32) + b[...].astype(F32) + c[...].astype(F32)
-    for k, o in enumerate((own, s1, s2, s3)):
-        o[...] = t[k * n : (k + 1) * n].astype(o.dtype)
-
-
-def rs_last_kernel(mine, a, b, c, out):
-    t = mine[...] + a[...].astype(F32) + b[...].astype(F32) + c[...].astype(F32)
-    out[...] = t.astype(BF)
+    n = output.shape[0]
+    output[...] = t[:n].astype(BF)
+    grad[...] = t[n:].astype(BF)
 
 
 def first_row(own, theirs, after=()):
@@ -230,33 +259,14 @@
     return call(rs_first_kernel, sends, [own, theirs], after=after)
 
 
-def back_x(sends):
-    c, b, d = [send_x(sends[k - 1], -k) for k in (2, 1, 3)]
-    return [b, c, d]
-
-
-def next_row(own, got, after=()):
-    rows, w = own.shape
-    sends = [((rows // Z, w), BF)] * 3 + [((rows // Z, w), F32)]
-    return call(rs_next_kernel, sends, [own, *got], after=after)
-
-
-def back_z(sends):
-    c, b, d = [send_z(sends[k - 1], -k) for k in (2, 1, 3)]
-    return [b, c, d]
-
-
-def last_row(own, got):
-    return call(rs_last_kernel, [(own.shape, BF)], [own, *got])[0]
-
-
 def on_device(tokens, gate_weight, up_weight, down_weight, cotangent):
     y = lax.rem(lax.axis_index("col"), Y).astype(jnp.int32).reshape(1)
     d, f = gate_weight.shape
 
-    t = gather_z(tokens)
-    g = gather_z(hold([cotangent], [t])[0])
-    t = gather_x(t, all_x(t), after=[g])
+    t = gather_z(tokens, all_z(tokens, "tokens_z"))
+    g = hold([cotangent], [t])[0]
+    g = gather_z(g, all_z(g, "cotangent_z"))
+    t = gather_x(t, all_x(t, "tokens_x"), after=[g])
     half = t.shape[0]
     n = CORES * half // Y
     flops = 2 * CORES * half * d * f
@@ -265,28 +275,28 @@
         return [((CORES * half, d), BF)] + [((n, w), BF)] * 3 + [((n, w), F32)]
 
     all_tokens, s1, s2, s3, own = call(
-        up_kernel, sends(2 * f), [t, send_core(t), gate_weight, up_weight], 2 * flops, y
+        up_kernel, sends(2 * f), [t, send_core(t, "tokens_core"), gate_weight, up_weight], 2 * flops, y
     )
     g = hold([g], [s1])[0]
-    got_x = all_x(g)
-    got = all_y([s1, s2, s3])
+    got_x = all_x(g, "cotangent_x")
+    got = all_y([s1, s2, s3], "gate_up_y")
     g = gather_x(g, got_x, after=got)
     gate_up, part = call(
         sum_y_kernel, [((n, 2 * f), F32), ((n, 2 * f), BF)], [own, *got], after=got_x
     )
 
-    gate_up2 = send_half(part)
+    gate_up2 = send_half(part, "gate_up_half")
     all_cotangent, s1, s2, s3, own = call(
-        back_kernel, sends(f), [g, send_core(g), down_weight], flops, y
-    )
-    got = all_y([s1, s2, s3])
+        back_kernel, sends(f), [g, send_core(g, "cotangent_core"), down_weight], flops, y
+    )
+    got = all_y([s1, s2, s3], "hidden_grad_y")
     gh, part = call(
         sum_y_kernel, [((n, f), F32), ((n, f), BF)], [own, *got], after=[gate_up2]
     )
     hidden = call(hidden_kernel, [((n, f), BF)], [gate_up, gate_up2], after=got)[0]
 
-    gh2 = send_half(part)
-    got = all_y([hidden] * 3)
+    gh2 = send_half(part, "hidden_grad_half")
+    got = all_y([hidden] * 3, "hidden_y")
     all_hidden, own_out, their_out = call(
         out_kernel,
         [((Y * n, f), BF), ((half, d), F32), ((half, d), OUT_CORE)],
@@ -299,29 +309,41 @@
         grads_kernel, [((n, 2 * f), BF)], [gate_up, gate_up2, gh, gh2], after=got
     )[0]
 
-    s1, s2, s3, own_out = first_row(own_out, send_core(their_out))
-    got_out = back_x([s1, s2, s3])
-    got = all_y([grads] * 3)
-    gg, ug, own_gt, their_gt = call(
+    got = all_y([grads] * 3, "grads_y")
+    s1, s2, s3, own_out = first_row(own_out, send_core(their_out, "output_core"))
+    got_out = back_x([s1, s2, s3], "output_x")
+    gg, ug, their_gt = call(
         tokens_kernel,
-        [((Y * n, f), BF), ((Y * n, f), BF), ((half, d), F32), ((half, d), OUT_CORE)],
+        [((Y * n, f), BF), ((Y * n, f), BF), ((half, d), OUT_CORE)],
         [grads, *got, gate_weight, up_weight],
-        2 * flops,
+        flops,
         y,
         after=got_out,
     )
-    s1, s2, s3, own_out = next_row(own_out, got_out, after=got)
-    z_out = [s1, s2, s3]
-    s1, s2, s3, own_gt = first_row(own_gt, send_core(their_gt))
-    z_out = hold(z_out, [s1])
-    got_z = back_z(z_out)
-    got = back_x([s1, s2, s3])
-    output = last_row(own_out, got_z)
+    own_gt = call(
+        tokens_own_kernel,
+        [((half, d), F32)],
+        [gg, ug, gate_weight, up_weight],
+        flops,
+    )[0]
+
+    all_hidden = hold([all_hidden], [their_gt])[0]
     grad_down = dot(all_hidden, all_cotangent, 0, 0).astype(BF)
-    s1, s2, s3, own_gt = next_row(own_gt, got, after=got_z)
-    grad_tokens = last_row(own_gt, back_z([s1, s2, s3]))
+    their_gt = send_core(their_gt, "token_grad_core")
+    s1, s2, s3, own_gt = first_row(own_gt, their_gt, [grad_down])
+    got = back_x([s1, s2, s3], "token_grad_x")
+    gg, ug = hold([gg, ug], [got[1]])
     grad_gate = dot(all_tokens, gg, 0, 0).astype(BF)
     grad_up = dot(all_tokens, ug, 0, 0).astype(BF)
+    rows = tokens.shape[0]
+    s1, s2, s3, own = call(
+        rs_next_kernel,
+        [((2 * rows, d), BF)] * 3 + [((2 * rows, d), F32)],
+        [own_out, *got_out, own_gt, *got],
+        after=[grad_gate, grad_up],
+    )
+    got = back_z([s1, s2, s3], "both_z")
+    output, grad_tokens = call(rs_last_kernel, [((rows, d), BF)] * 2, [own, *got])
     return (output, grad_tokens, grad_gate, grad_up, grad_down)
 
 

time: 156 us -> 152 us (0.974)
  starting transfers between devices: 60.1 us -> 54 us
  waiting for transfers between devices: 77.1 us -> 82.2 us
  matrix products: 5.92 us -> 3.09 us
    ppermute x12 -> x9, waiting for transfers between devices: 11 us -> 18.3 us  [send_z(): return lax.ppermute(a, 'row', row_perm(lambda z, x, c: (z + k, x, c)))]
    ppermute x12 -> x9, starting transfers between devices: 18 us -> 12.1 us  [send_z(): return lax.ppermute(a, 'row', row_perm(lambda z, x, c: (z + k, x, c)))]
    dot_general x3, matrix products: 5.92 us -> 3.09 us  [dot(): lax.dot_general(left, right, (((ldim,), (rdim,)), ((), ())), preferred_el...]
    ppermute x4, waiting for transfers between devices: 6.24 us -> 4.2 us  [send_core(): return lax.ppermute(a, 'row', row_perm(lambda z, x, c: (z, x, c + 1)))]
    ppermute x4, starting transfers between devices: 7.13 us -> 5.38 us  [send_core(): return lax.ppermute(a, 'row', row_perm(lambda z, x, c: (z, x, c + 1)))]
    pallas_call x21 -> x23, Pallas kernels: 10.1 us -> 9.97 us  [call(): pl.pallas_call(body, name=kernel.__name__.removesuffix('_kernel'), out_sh...]
  transfers between devices with their start and end apart: 42 -> 39, of which waited for: 24 -> 24; matrix products, arithmetic and copies ran while one was open for 4% -> 2% of each run, Pallas kernels for 2% -> 2%
where the time goes in v1:
time: 152 us
  waiting for transfers between devices  82.2 us (54%)
  starting transfers between devices  54 us (36%)
  Pallas kernels  9.97 us (7%)
  matrix products  3.09 us (2%)
  local copies, waits for them, and re-layouts  1.66 us (1%)
    ppermute x12, waiting for transfers between devices, send_y(): return lax.ppermute(a, 'col', col_perm(lambda h, y: (h, y + k)))  32.1 us
    ppermute x12, waiting for transfers between devices, send_x(): return lax.ppermute(a, 'row', row_perm(lambda z, x, c: (z, x + k, c)))  18.5 us
    ppermute x9, waiting for transfers between devices, send_z(): return lax.ppermute(a, 'row', row_perm(lambda z, x, c: (z + k, x, c)))  18.3 us
    ppermute x12, starting transfers between devices, send_y(): return lax.ppermute(a, 'col', col_perm(lambda h, y: (h, y + k)))  14.1 us
    ppermute x9, starting transfers between devices, send_z(): return lax.ppermute(a, 'row', row_perm(lambda z, x, c: (z + k, x, c)))  12.1 us
    ppermute x2, starting transfers between devices, send_half(): return lax.ppermute(a, 'col', col_perm(lambda h, y: (h + 1, y)))  11.9 us
    ppermute x12, starting transfers between devices, send_x(): return lax.ppermute(a, 'row', row_perm(lambda z, x, c: (z, x + k, c)))  10.5 us
    pallas_call x23, Pallas kernels, call(): pl.pallas_call(body, name=kernel.__name__.removesuffix('_kernel'), out_sh...  9.97 us
  transfers between devices with their start and end apart: 39, of which 24 were waited for; matrix products, arithmetic and copies ran while one was open for 2% of the time, Pallas kernels for 2%

profile of v1, /device:TPU:1, one launch (start us, length us, event | category | flops | bytes accessed | tf_op | source)
XLA Modules:
  0.0 151.8 jit_solution(14536313196757730827)
XLA Ops:
  0.7 2.5 %collective-permute-start = (bf16[24,1024]{1,0:T(8,128)(2,1)}, bf16[24,1024]{1,0:T(8,128)(2,1)S(1)}, u32[]{:S(2)}, u32[]{:S(2)}) collective-permute-start(bf16[24,1024]{1,0:T(8,128)(2,1)} %refs_0_.2), channel_id=1, source_target_pairs={{0,64},{8,72},{16,80},{24,88},{32,96},{40,104},{48,112},{56,120},{... | collective-permute-start | bytes 147464 | tf_op jit(solution)/shard_map/tokens_z/ppermute | solution.py:37
  3.2 2.8 %collective-permute-start.2 = (bf16[24,1024]{1,0:T(8,128)(2,1)}, bf16[24,1024]{1,0:T(8,128)(2,1)S(1)}, u32[]{:S(2)}, u32[]{:S(2)}) collective-permute-start(bf16[24,1024]{1,0:T(8,128)(2,1)} %refs_0_.2), channel_id=1, source_target_pairs={{0,192},{8,200},{16,208},{24,216},{32,224},{40,232},{48,240},{56,2... | collective-permute-start | bytes 147464 | tf_op jit(solution)/shard_map/tokens_z/ppermute | solution.py:37
  6.2 0.8 copy-done.6
  7.0 0.6 collective-permute-done.b
  7.6 3.6 %collective-permute-done.1.c = bf16[24,1024]{1,0:T(8,128)(2,1)S(1)} collective-permute-done((bf16[24,1024]{1,0:T(8,128)(2,1)}, bf16[24,1024]{1,0:T(8,128)(2,1)S(1)}, u32[]{:S(2)}, u32[]{:S(2)}) %collective-permute-start.1) | collective-permute-done | bytes 49184 | tf_op jit(solution)/shard_map/tokens_z/ppermute | solution.py:37
  11.2 1.6 %collective-permute-start.5 = (bf16[96,1024]{1,0:T(8,128)(2,1)S(1)}, bf16[96,1024]{1,0:T(8,128)(2,1)S(1)}, u32[]{:S(2)}, u32[]{:S(2)}) collective-permute-start(bf16[96,1024]{1,0:T(8,128)(2,1)S(1)} %cat_z.2.refs_1_.refs_0_), channel_id=1, source_target_pairs={{0,48},{8,56},{16,0},{24,8},{32,16},{40,24},{48,32},{56,40},{64,11... | collective-permute-start | bytes 589832 | tf_op jit(solution)/shard_map/tokens_x/ppermute | solution.py:42
  12.8 0.5 collective-permute-start.4
  13.3 0.6 collective-permute-start.3
  13.9 0.8 copy-done.5
  14.7 3.5 %collective-permute-start.8 = (bf16[24,1024]{1,0:T(8,128)(2,1)S(1)}, bf16[24,1024]{1,0:T(8,128)(2,1)S(1)}, u32[]{:S(2)}, u32[]{:S(2)}) collective-permute-start(bf16[24,1024]{1,0:T(8,128)(2,1)S(1)} %hold.7.refs_0_), channel_id=1, source_target_pairs={{0,192},{8,200},{16,208},{24,216},{32,224},{40,232},{48,240},{56,2... | collective-permute-start | bytes 147464 | tf_op jit(solution)/shard_map/cotangent_z/ppermute | solution.py:37
  18.2 1.2 collective-permute-done.8.d
  19.4 2.9 %collective-permute-done.7.c = bf16[24,1024]{1,0:T(8,128)(2,1)S(1)} collective-permute-done((bf16[24,1024]{1,0:T(8,128)(2,1)S(1)}, bf16[24,1024]{1,0:T(8,128)(2,1)S(1)}, u32[]{:S(2)}, u32[]{:S(2)}) %collective-permute-start.7) | collective-permute-done | bytes 49184 | tf_op jit(solution)/shard_map/cotangent_z/ppermute | solution.py:37
  22.4 2.4 %collective-permute-done.6.b = bf16[24,1024]{1,0:T(8,128)(2,1)S(1)} collective-permute-done((bf16[24,1024]{1,0:T(8,128)(2,1)S(1)}, bf16[24,1024]{1,0:T(8,128)(2,1)S(1)}, u32[]{:S(2)}, u32[]{:S(2)}) %collective-permute-start.6) | collective-permute-done | bytes 49184 | tf_op jit(solution)/shard_map/cotangent_z/ppermute | solution.py:37
  24.9 3.3 %collective-permute-start.9 = (bf16[384,1024]{1,0:T(8,128)(2,1)S(1)}, bf16[384,1024]{1,0:T(8,128)(2,1)}, u32[]{:S(2)}, u32[]{:S(2)}) collective-permute-start(bf16[384,1024]{1,0:T(8,128)(2,1)S(1)} %cat_x.2.mine), channel_id=1, source_target_pairs={{0,8},{8,0},{16,24},{24,16},{32,40},{40,32},{48,56},{56,48},{64,72... | collective-permute-start | bytes 2359304 | tf_op jit(solution)/shard_map/tokens_core/ppermute | solution.py:47
  28.1 2.0 %collective-permute-done.9.theirs = bf16[384,1024]{1,0:T(8,128)(2,1)} collective-permute-done((bf16[384,1024]{1,0:T(8,128)(2,1)S(1)}, bf16[384,1024]{1,0:T(8,128)(2,1)}, u32[]{:S(2)}, u32[]{:S(2)}) %collective-permute-start.9) | collective-permute-done | bytes 786464 | tf_op jit(solution)/shard_map/tokens_core/ppermute | solution.py:47
  30.2 3.1 %up.1 = (bf16[768,1024]{1,0:T(8,128)(2,1)S(1)}, bf16[192,1024]{1,0:T(8,128)(2,1)S(1)}, bf16[192,1024]{1,0:T(8,128)(2,1)S(1)}, bf16[192,1024]{1,0:T(8,128)(2,1)S(1)}, f32[192,1024]{1,0:T(8,128)S(1)}) custom-call(s32[1]{0:T(128)} %bitcast.y.refs_0_, bf16[384,1024]{1,0:T(8,128)(2,1)S(1)} %cat_x.2.mine, bf16[384,1024]{1,0:T(8,128)(2,1)} %collective-permute-done.9.theirs, ...), custom_call_target="tpu_custom_call" | custom-call | flops 1610612736 | bytes 7208960 | tf_op jit(solution)/shard_map/up/pallas_call | solution.py:84
  33.3 2.1 %collective-permute-start.15 = (bf16[96,1024]{1,0:T(8,128)(2,1)S(1)}, bf16[96,1024]{1,0:T(8,128)(2,1)S(1)}, u32[]{:S(2)}, u32[]{:S(2)}) collective-permute-start(bf16[96,1024]{1,0:T(8,128)(2,1)S(1)} %hold.9.refs_0_), channel_id=1, source_target_pairs={{0,48},{8,56},{16,0},{24,8},{32,16},{40,24},{48,32},{56,40},{64,11... | collective-permute-start | bytes 589832 | tf_op jit(solution)/shard_map/cotangent_x/ppermute | solution.py:42
  35.5 2.9 %collective-permute-start.11 = (bf16[192,1024]{1,0:T(8,128)(2,1)S(1)}, bf16[192,1024]{1,0:T(8,128)(2,1)S(1)}, u32[]{:S(2)}, u32[]{:S(2)}) collective-permute-start(bf16[192,1024]{1,0:T(8,128)(2,1)S(1)} %get-tuple-element.43), channel_id=1, source_target_pairs={{0,2},{1,3},{2,0},{3,1},{4,6},{5,7},{6,4},{7,5},{8,10},{9,11},{10,... | collective-permute-start | bytes 1179656 | tf_op jit(solution)/shard_map/gate_up_y/ppermute | solution.py:52
  38.4 0.8 collective-permute-start.12
  39.2 0.7 collective-permute-start.10
  39.8 1.2 collective-permute-start.14
  41.1 5.2 %collective-permute-done.14.refs_5_.refs_2_ = bf16[96,1024]{1,0:T(8,128)(2,1)S(1)} collective-permute-done((bf16[96,1024]{1,0:T(8,128)(2,1)S(1)}, bf16[96,1024]{1,0:T(8,128)(2,1)S(1)}, u32[]{:S(2)}, u32[]{:S(2)}) %collective-permute-start.14) | collective-permute-done | bytes 196640 | tf_op jit(solution)/shard_map/cotangent_x/ppermute | solution.py:42
  46.2 5.7 %collective-permute-done.13.refs_4_.refs_1_ = bf16[96,1024]{1,0:T(8,128)(2,1)S(1)} collective-permute-done((bf16[96,1024]{1,0:T(8,128)(2,1)S(1)}, bf16[96,1024]{1,0:T(8,128)(2,1)S(1)}, u32[]{:S(2)}, u32[]{:S(2)}) %collective-permute-start.13) | collective-permute-done | bytes 196640 | tf_op jit(solution)/shard_map/cotangent_x/ppermute | solution.py:42
  51.9 3.9 %collective-permute-done.12.refs_3_.refs_6_ = bf16[192,1024]{1,0:T(8,128)(2,1)S(1)} collective-permute-done((bf16[192,1024]{1,0:T(8,128)(2,1)S(1)}, bf16[192,1024]{1,0:T(8,128)(2,1)S(1)}, u32[]{:S(2)}, u32[]{:S(2)}) %collective-permute-start.12) | collective-permute-done | bytes 393248 | tf_op jit(solution)/shard_map/gate_up_y/ppermute | solution.py:52
  55.8 0.6 collective-permute-done.10.refs_1_.refs_4_
  56.5 1.0 collective-permute-start.17
  57.7 5.6 %collective-permute-start.16 = (bf16[192,1024]{1,0:T(8,128)(2,1)S(1)}, bf16[192,1024]{1,0:T(8,128)(2,1)S(1)}, u32[]{:S(2)}, u32[]{:S(2)}) collective-permute-start(bf16[192,1024]{1,0:T(8,128)(2,1)S(1)} %get-tuple-element.46), channel_id=1, source_target_pairs={{0,4},{1,5},{2,6},{3,7},{4,0},{5,1},{6,2},{7,3},{8,12},{9,13},{10,... | collective-permute-start | bytes 1179656 | tf_op jit(solution)/shard_map/gate_up_half/ppermute | solution.py:57
  63.3 1.5 %back.1 = (bf16[768,1024]{1,0:T(8,128)(2,1)S(1)}, bf16[192,512]{1,0:T(8,128)(2,1)S(1)}, bf16[192,512]{1,0:T(8,128)(2,1)S(1)}, bf16[192,512]{1,0:T(8,128)(2,1)S(1)}, f32[192,512]{1,0:T(8,128)S(1)}) custom-call(s32[1]{0:T(128)} %bitcast.y.refs_0_, bf16[384,1024]{1,0:T(8,128)(2,1)S(1)} %cat_x.3.mine, bf16[384,1024]{1,0:T(8,128)(2,1)S(1)} %collective-permute-done.17.theirs, ...), custom_call_target="tpu_custom_call" | custom-call | flops 805306368 | bytes 5177344 | tf_op jit(solution)/shard_map/back/pallas_call | solution.py:84
  64.9 1.1 collective-permute-start.18
  66.0 2.5 %collective-permute-start.19 = (bf16[192,512]{1,0:T(8,128)(2,1)S(1)}, bf16[192,512]{1,0:T(8,128)(2,1)S(1)}, u32[]{:S(2)}, u32[]{:S(2)}) collective-permute-start(bf16[192,512]{1,0:T(8,128)(2,1)S(1)} %get-tuple-element.48), channel_id=1, source_target_pairs={{0,2},{1,3},{2,0},{3,1},{4,6},{5,7},{6,4},{7,5},{8,10},{9,11},{10,... | collective-permute-start | bytes 589832 | tf_op jit(solution)/shard_map/hidden_grad_y/ppermute | solution.py:52
  68.5 1.1 collective-permute-start.20
  69.5 8.4 %collective-permute-done.16.refs_1_.refs_4_ = bf16[192,1024]{1,0:T(8,128)(2,1)S(1)} collective-permute-done((bf16[192,1024]{1,0:T(8,128)(2,1)S(1)}, bf16[192,1024]{1,0:T(8,128)(2,1)S(1)}, u32[]{:S(2)}, u32[]{:S(2)}) %collective-permute-start.16) | collective-permute-done | bytes 393248 | tf_op jit(solution)/shard_map/gate_up_half/ppermute | solution.py:57
  78.1 6.3 %collective-permute-start.24 = (bf16[192,512]{1,0:T(8,128)(2,1)S(1)}, bf16[192,512]{1,0:T(8,128)(2,1)S(1)}, u32[]{:S(2)}, u32[]{:S(2)}) collective-permute-start(bf16[192,512]{1,0:T(8,128)(2,1)S(1)} %get-tuple-element.51), channel_id=1, source_target_pairs={{0,4},{1,5},{2,6},{3,7},{4,0},{5,1},{6,2},{7,3},{8,12},{9,13},{10,... | collective-permute-start | bytes 589832 | tf_op jit(solution)/shard_map/hidden_grad_half/ppermute | solution.py:57
  84.5 2.4 %collective-permute-start.23 = (bf16[192,512]{1,0:T(8,128)(2,1)S(1)}, bf16[192,512]{1,0:T(8,128)(2,1)S(1)}, u32[]{:S(2)}, u32[]{:S(2)}) collective-permute-start(bf16[192,512]{1,0:T(8,128)(2,1)S(1)} %hidden.1.refs_1_), channel_id=1, source_target_pairs={{0,3},{1,0},{2,1},{3,2},{4,7},{5,4},{6,5},{7,6},{8,11},{9,8},{10,9... | collective-permute-start | bytes 589832 | tf_op jit(solution)/shard_map/hidden_y/ppermute | solution.py:52
  87.4 0.5 collective-permute-start.21
  87.9 0.7 collective-permute-done.24.refs_6_.refs_3_
  88.7 2.2 %collective-permute-done.23.refs_4_.refs_6_ = bf16[192,512]{1,0:T(8,128)(2,1)S(1)} collective-permute-done((bf16[192,512]{1,0:T(8,128)(2,1)S(1)}, bf16[192,512]{1,0:T(8,128)(2,1)S(1)}, u32[]{:S(2)}, u32[]{:S(2)}) %collective-permute-start.23) | collective-permute-done | bytes 196640 | tf_op jit(solution)/shard_map/hidden_y/ppermute | solution.py:52
  90.8 2.6 %collective-permute-done.22.refs_3_.refs_5_ = bf16[192,512]{1,0:T(8,128)(2,1)S(1)} collective-permute-done((bf16[192,512]{1,0:T(8,128)(2,1)S(1)}, bf16[192,512]{1,0:T(8,128)(2,1)S(1)}, u32[]{:S(2)}, u32[]{:S(2)}) %collective-permute-start.22) | collective-permute-done | bytes 196640 | tf_op jit(solution)/shard_map/hidden_y/ppermute | solution.py:52
  93.4 6.0 %collective-permute-done.21.refs_2_.refs_4_ = bf16[192,512]{1,0:T(8,128)(2,1)S(1)} collective-permute-done((bf16[192,512]{1,0:T(8,128)(2,1)S(1)}, bf16[192,512]{1,0:T(8,128)(2,1)S(1)}, u32[]{:S(2)}, u32[]{:S(2)}) %collective-permute-start.21) | collective-permute-done | bytes 196640 | tf_op jit(solution)/shard_map/hidden_y/ppermute | solution.py:52
  99.4 1.0 out.1
  100.5 0.6 collective-permute-start.25
  102.2 0.7 collective-permute-start.29
  102.8 1.2 collective-permute-done.25.theirs
  104.6 1.2 collective-permute-start.27
  105.9 6.2 %collective-permute-done.31.refs_4_ = bf16[192,1024]{1,0:T(8,128)(2,1)S(1)} collective-permute-done((bf16[192,1024]{1,0:T(8,128)(2,1)S(1)}, bf16[192,1024]{1,0:T(8,128)(2,1)S(1)}, u32[]{:S(2)}, u32[]{:S(2)}) %collective-permute-start.31) | collective-permute-done | bytes 393248 | tf_op jit(solution)/shard_map/grads_y/ppermute | solution.py:52
  112.1 1.6 %collective-permute-done.30.refs_3_ = bf16[192,1024]{1,0:T(8,128)(2,1)S(1)} collective-permute-done((bf16[192,1024]{1,0:T(8,128)(2,1)S(1)}, bf16[192,1024]{1,0:T(8,128)(2,1)S(1)}, u32[]{:S(2)}, u32[]{:S(2)}) %collective-permute-start.30) | collective-permute-done | bytes 393248 | tf_op jit(solution)/shard_map/grads_y/ppermute | solution.py:52
  113.7 9.0 %collective-permute-done.29.refs_2_ = bf16[192,1024]{1,0:T(8,128)(2,1)S(1)} collective-permute-done((bf16[192,1024]{1,0:T(8,128)(2,1)S(1)}, bf16[192,1024]{1,0:T(8,128)(2,1)S(1)}, u32[]{:S(2)}, u32[]{:S(2)}) %collective-permute-start.29) | collective-permute-done | bytes 393248 | tf_op jit(solution)/shard_map/grads_y/ppermute | solution.py:52
  122.7 1.0 tokens.1
  123.8 0.5 collective-permute-start.32
  124.4 1.0 tokens_own.1.refs_0_
  125.4 1.0 convolution_convert_fusion.2.refs_2_
  126.4 0.9 collective-permute-done.32.refs_1_
  127.6 1.3 collective-permute-start.34
  129.0 0.7 collective-permute-start.33
  129.7 0.8 collective-permute-start.35
  130.4 4.9 %collective-permute-done.34.refs_2_.refs_6_ = bf16[96,1024]{1,0:T(8,128)(2,1)S(1)} collective-permute-done((bf16[96,1024]{1,0:T(8,128)(2,1)S(1)}, bf16[96,1024]{1,0:T(8,128)(2,1)S(1)}, u32[]{:S(2)}, u32[]{:S(2)}) %collective-permute-start.34) | collective-permute-done | bytes 196640 | tf_op jit(solution)/shard_map/token_grad_x/ppermute | solution.py:42
  135.5 1.0 convolution_convert_fusion.1.refs_8_
  136.5 1.0 convolution_convert_fusion.refs_9_
  137.6 2.7 %collective-permute-done.35.refs_7_ = bf16[96,1024]{1,0:T(8,128)(2,1)S(1)} collective-permute-done((bf16[96,1024]{1,0:T(8,128)(2,1)S(1)}, bf16[96,1024]{1,0:T(8,128)(2,1)S(1)}, u32[]{:S(2)}, u32[]{:S(2)}) %collective-permute-start.35) | collective-permute-done | bytes 196640 | tf_op jit(solution)/shard_map/token_grad_x/ppermute | solution.py:42
  140.6 1.6 %collective-permute-start.37 = (bf16[48,1024]{1,0:T(8,128)(2,1)S(1)}, bf16[48,1024]{1,0:T(8,128)(2,1)S(1)}, u32[]{:S(2)}, u32[]{:S(2)}) collective-permute-start(bf16[48,1024]{1,0:T(8,128)(2,1)S(1)} %get-tuple-element.73), channel_id=1, source_target_pairs={{0,128},{8,136},{16,144},{24,152},{32,160},{40,168},{48,176},{56,1... | collective-permute-start | bytes 294920 | tf_op jit(solution)/shard_map/both_z/ppermute | solution.py:37
  142.2 1.4 collective-permute-start.38
  143.5 0.9 collective-permute-done.36.a
  144.4 6.7 %collective-permute-done.37.b = bf16[48,1024]{1,0:T(8,128)(2,1)S(1)} collective-permute-done((bf16[48,1024]{1,0:T(8,128)(2,1)S(1)}, bf16[48,1024]{1,0:T(8,128)(2,1)S(1)}, u32[]{:S(2)}, u32[]{:S(2)}) %collective-permute-start.37) | collective-permute-done | bytes 98336 | tf_op jit(solution)/shard_map/both_z/ppermute | solution.py:37
  151.1 0.7 rs_last.1
  (56 shorter events, 3.8 us)
Async XLA Ops:
  0.6 29.6 %copy-start.1 = (bf16[1024,512]{1,0:T(8,128)(2,1)S(1)}, bf16[1024,512]{1,0:T(8,128)(2,1)}, u32[]{:S(2)}) copy-start(bf16[1024,512]{1,0:T(8,128)(2,1)} %wu.3) | copy-start | bytes 3145732
  0.6 29.5 %copy-start = (bf16[1024,512]{1,0:T(8,128)(2,1)S(1)}, bf16[1024,512]{1,0:T(8,128)(2,1)}, u32[]{:S(2)}) copy-start(bf16[1024,512]{1,0:T(8,128)(2,1)} %wg.3) | copy-start | bytes 3145732
  0.7 7.0 %collective-permute-start = (bf16[24,1024]{1,0:T(8,128)(2,1)}, bf16[24,1024]{1,0:T(8,128)(2,1)S(1)}, u32[]{:S(2)}, u32[]{:S(2)}) collective-permute-start(bf16[24,1024]{1,0:T(8,128)(2,1)} %refs_0_.2), channel_id=1, source_target_pairs={{0,64},{8,72},{16,80},{24,88},{32,96},{40,104},{48,112},{56,120},{... | collective-permute-start | bytes 147464 | tf_op jit(solution)/shard_map/tokens_z/ppermute | solution.py:37
  3.2 4.4 %collective-permute-start.2 = (bf16[24,1024]{1,0:T(8,128)(2,1)}, bf16[24,1024]{1,0:T(8,128)(2,1)S(1)}, u32[]{:S(2)}, u32[]{:S(2)}) collective-permute-start(bf16[24,1024]{1,0:T(8,128)(2,1)} %refs_0_.2), channel_id=1, source_target_pairs={{0,192},{8,200},{16,208},{24,216},{32,224},{40,232},{48,240},{56,2... | collective-permute-start | bytes 147464 | tf_op jit(solution)/shard_map/tokens_z/ppermute | solution.py:37
  6.0 5.2 %collective-permute-start.1 = (bf16[24,1024]{1,0:T(8,128)(2,1)}, bf16[24,1024]{1,0:T(8,128)(2,1)S(1)}, u32[]{:S(2)}, u32[]{:S(2)}) collective-permute-start(bf16[24,1024]{1,0:T(8,128)(2,1)} %refs_0_.2), channel_id=1, source_target_pairs={{0,128},{8,136},{16,144},{24,152},{32,160},{40,168},{48,176},{56,1... | collective-permute-start | bytes 147464 | tf_op jit(solution)/shard_map/tokens_z/ppermute | solution.py:37
  6.2 0.8 copy-start.6
  11.2 13.5 %collective-permute-start.5 = (bf16[96,1024]{1,0:T(8,128)(2,1)S(1)}, bf16[96,1024]{1,0:T(8,128)(2,1)S(1)}, u32[]{:S(2)}, u32[]{:S(2)}) collective-permute-start(bf16[96,1024]{1,0:T(8,128)(2,1)S(1)} %cat_z.2.refs_1_.refs_0_), channel_id=1, source_target_pairs={{0,48},{8,56},{16,0},{24,8},{32,16},{40,24},{48,32},{56,40},{64,11... | collective-permute-start | bytes 589832 | tf_op jit(solution)/shard_map/tokens_x/ppermute | solution.py:42
  12.8 12.0 %collective-permute-start.4 = (bf16[96,1024]{1,0:T(8,128)(2,1)S(1)}, bf16[96,1024]{1,0:T(8,128)(2,1)S(1)}, u32[]{:S(2)}, u32[]{:S(2)}) collective-permute-start(bf16[96,1024]{1,0:T(8,128)(2,1)S(1)} %cat_z.2.refs_1_.refs_0_), channel_id=1, source_target_pairs={{0,32},{8,40},{16,48},{24,56},{32,0},{40,8},{48,16},{56,24},{64,96... | collective-permute-start | bytes 589832 | tf_op jit(solution)/shard_map/tokens_x/ppermute | solution.py:42
  13.3 11.5 %collective-permute-start.3 = (bf16[96,1024]{1,0:T(8,128)(2,1)S(1)}, bf16[96,1024]{1,0:T(8,128)(2,1)S(1)}, u32[]{:S(2)}, u32[]{:S(2)}) collective-permute-start(bf16[96,1024]{1,0:T(8,128)(2,1)S(1)} %cat_z.2.refs_1_.refs_0_), channel_id=1, source_target_pairs={{0,16},{8,24},{16,32},{24,40},{32,48},{40,56},{48,0},{56,8},{64,80... | collective-permute-start | bytes 589832 | tf_op jit(solution)/shard_map/tokens_x/ppermute | solution.py:42
  13.9 0.8 copy-start.5
  14.7 4.7 %collective-permute-start.8 = (bf16[24,1024]{1,0:T(8,128)(2,1)S(1)}, bf16[24,1024]{1,0:T(8,128)(2,1)S(1)}, u32[]{:S(2)}, u32[]{:S(2)}) collective-permute-start(bf16[24,1024]{1,0:T(8,128)(2,1)S(1)} %hold.7.refs_0_), channel_id=1, source_target_pairs={{0,192},{8,200},{16,208},{24,216},{32,224},{40,232},{48,240},{56,2... | collective-permute-start | bytes 147464 | tf_op jit(solution)/shard_map/cotangent_z/ppermute | solution.py:37
  18.2 4.1 %collective-permute-start.7 = (bf16[24,1024]{1,0:T(8,128)(2,1)S(1)}, bf16[24,1024]{1,0:T(8,128)(2,1)S(1)}, u32[]{:S(2)}, u32[]{:S(2)}) collective-permute-start(bf16[24,1024]{1,0:T(8,128)(2,1)S(1)} %hold.7.refs_0_), channel_id=1, source_target_pairs={{0,128},{8,136},{16,144},{24,152},{32,160},{40,168},{48,176},{56,1... | collective-permute-start | bytes 147464 | tf_op jit(solution)/shard_map/cotangent_z/ppermute | solution.py:37
  19.4 5.3 %collective-permute-start.6 = (bf16[24,1024]{1,0:T(8,128)(2,1)S(1)}, bf16[24,1024]{1,0:T(8,128)(2,1)S(1)}, u32[]{:S(2)}, u32[]{:S(2)}) collective-permute-start(bf16[24,1024]{1,0:T(8,128)(2,1)S(1)} %hold.7.refs_0_), channel_id=1, source_target_pairs={{0,64},{8,72},{16,80},{24,88},{32,96},{40,104},{48,112},{56,120},{... | collective-permute-start | bytes 147464 | tf_op jit(solution)/shard_map/cotangent_z/ppermute | solution.py:37
  24.9 5.3 %collective-permute-start.9 = (bf16[384,1024]{1,0:T(8,128)(2,1)S(1)}, bf16[384,1024]{1,0:T(8,128)(2,1)}, u32[]{:S(2)}, u32[]{:S(2)}) collective-permute-start(bf16[384,1024]{1,0:T(8,128)(2,1)S(1)} %cat_x.2.mine), channel_id=1, source_target_pairs={{0,8},{8,0},{16,24},{24,16},{32,40},{40,32},{48,56},{56,48},{64,72... | collective-permute-start | bytes 2359304 | tf_op jit(solution)/shard_map/tokens_core/ppermute | solution.py:47
  33.3 7.8 %collective-permute-start.15 = (bf16[96,1024]{1,0:T(8,128)(2,1)S(1)}, bf16[96,1024]{1,0:T(8,128)(2,1)S(1)}, u32[]{:S(2)}, u32[]{:S(2)}) collective-permute-start(bf16[96,1024]{1,0:T(8,128)(2,1)S(1)} %hold.9.refs_0_), channel_id=1, source_target_pairs={{0,48},{8,56},{16,0},{24,8},{32,16},{40,24},{48,32},{56,40},{64,11... | collective-permute-start | bytes 589832 | tf_op jit(solution)/shard_map/cotangent_x/ppermute | solution.py:42
  35.5 16.5 %collective-permute-start.11 = (bf16[192,1024]{1,0:T(8,128)(2,1)S(1)}, bf16[192,1024]{1,0:T(8,128)(2,1)S(1)}, u32[]{:S(2)}, u32[]{:S(2)}) collective-permute-start(bf16[192,1024]{1,0:T(8,128)(2,1)S(1)} %get-tuple-element.43), channel_id=1, source_target_pairs={{0,2},{1,3},{2,0},{3,1},{4,6},{5,7},{6,4},{7,5},{8,10},{9,11},{10,... | collective-permute-start | bytes 1179656 | tf_op jit(solution)/shard_map/gate_up_y/ppermute | solution.py:52
  38.4 17.4 %collective-permute-start.12 = (bf16[192,1024]{1,0:T(8,128)(2,1)S(1)}, bf16[192,1024]{1,0:T(8,128)(2,1)S(1)}, u32[]{:S(2)}, u32[]{:S(2)}) collective-permute-start(bf16[192,1024]{1,0:T(8,128)(2,1)S(1)} %get-tuple-element.44), channel_id=1, source_target_pairs={{0,3},{1,0},{2,1},{3,2},{4,7},{5,4},{6,5},{7,6},{8,11},{9,8},{10,9... | collective-permute-start | bytes 1179656 | tf_op jit(solution)/shard_map/gate_up_y/ppermute | solution.py:52
  39.2 17.3 %collective-permute-start.10 = (bf16[192,1024]{1,0:T(8,128)(2,1)S(1)}, bf16[192,1024]{1,0:T(8,128)(2,1)S(1)}, u32[]{:S(2)}, u32[]{:S(2)}) collective-permute-start(bf16[192,1024]{1,0:T(8,128)(2,1)S(1)} %get-tuple-element.42.refs_1_), channel_id=1, source_target_pairs={{0,1},{1,2},{2,3},{3,0},{4,5},{5,6},{6,7},{7,4},{8,9},{9,10},{10,1... | collective-permute-start | bytes 1179656 | tf_op jit(solution)/shard_map/gate_up_y/ppermute | solution.py:52
  39.8 6.4 %collective-permute-start.14 = (bf16[96,1024]{1,0:T(8,128)(2,1)S(1)}, bf16[96,1024]{1,0:T(8,128)(2,1)S(1)}, u32[]{:S(2)}, u32[]{:S(2)}) collective-permute-start(bf16[96,1024]{1,0:T(8,128)(2,1)S(1)} %hold.9.refs_0_), channel_id=1, source_target_pairs={{0,32},{8,40},{16,48},{24,56},{32,0},{40,8},{48,16},{56,24},{64,96... | collective-permute-start | bytes 589832 | tf_op jit(solution)/shard_map/cotangent_x/ppermute | solution.py:42
  41.1 10.8 %collective-permute-start.13 = (bf16[96,1024]{1,0:T(8,128)(2,1)S(1)}, bf16[96,1024]{1,0:T(8,128)(2,1)S(1)}, u32[]{:S(2)}, u32[]{:S(2)}) collective-permute-start(bf16[96,1024]{1,0:T(8,128)(2,1)S(1)} %hold.9.refs_0_), channel_id=1, source_target_pairs={{0,16},{8,24},{16,32},{24,40},{32,48},{40,56},{48,0},{56,8},{64,80... | collective-permute-start | bytes 589832 | tf_op jit(solution)/shard_map/cotangent_x/ppermute | solution.py:42
  56.5 6.8 %copy-start.7 = (bf16[512,1024]{1,0:T(8,128)(2,1)S(1)}, bf16[512,1024]{1,0:T(8,128)(2,1)}, u32[]{:S(2)}) copy-start(bf16[512,1024]{1,0:T(8,128)(2,1)} %refs_5_.2) | copy-start | bytes 3145732
  56.5 6.8 %collective-permute-start.17 = (bf16[384,1024]{1,0:T(8,128)(2,1)S(1)}, bf16[384,1024]{1,0:T(8,128)(2,1)S(1)}, u32[]{:S(2)}, u32[]{:S(2)}) collective-permute-start(bf16[384,1024]{1,0:T(8,128)(2,1)S(1)} %cat_x.3.mine), channel_id=1, source_target_pairs={{0,8},{8,0},{16,24},{24,16},{32,40},{40,32},{48,56},{56,48},{64,72... | collective-permute-start | bytes 2359304 | tf_op jit(solution)/shard_map/cotangent_core/ppermute | solution.py:47
  57.7 20.2 %collective-permute-start.16 = (bf16[192,1024]{1,0:T(8,128)(2,1)S(1)}, bf16[192,1024]{1,0:T(8,128)(2,1)S(1)}, u32[]{:S(2)}, u32[]{:S(2)}) collective-permute-start(bf16[192,1024]{1,0:T(8,128)(2,1)S(1)} %get-tuple-element.46), channel_id=1, source_target_pairs={{0,4},{1,5},{2,6},{3,7},{4,0},{5,1},{6,2},{7,3},{8,12},{9,13},{10,... | collective-permute-start | bytes 1179656 | tf_op jit(solution)/shard_map/gate_up_half/ppermute | solution.py:57
  64.9 13.1 %collective-permute-start.18 = (bf16[192,512]{1,0:T(8,128)(2,1)S(1)}, bf16[192,512]{1,0:T(8,128)(2,1)S(1)}, u32[]{:S(2)}, u32[]{:S(2)}) collective-permute-start(bf16[192,512]{1,0:T(8,128)(2,1)S(1)} %get-tuple-element.47), channel_id=1, source_target_pairs={{0,1},{1,2},{2,3},{3,0},{4,5},{5,6},{6,7},{7,4},{8,9},{9,10},{10,1... | collective-permute-start | bytes 589832 | tf_op jit(solution)/shard_map/hidden_grad_y/ppermute | solution.py:52
  66.0 11.9 %collective-permute-start.19 = (bf16[192,512]{1,0:T(8,128)(2,1)S(1)}, bf16[192,512]{1,0:T(8,128)(2,1)S(1)}, u32[]{:S(2)}, u32[]{:S(2)}) collective-permute-start(bf16[192,512]{1,0:T(8,128)(2,1)S(1)} %get-tuple-element.48), channel_id=1, source_target_pairs={{0,2},{1,3},{2,0},{3,1},{4,6},{5,7},{6,4},{7,5},{8,10},{9,11},{10,... | collective-permute-start | bytes 589832 | tf_op jit(solution)/shard_map/hidden_grad_y/ppermute | solution.py:52
  68.5 9.5 %collective-permute-start.20 = (bf16[192,512]{1,0:T(8,128)(2,1)S(1)}, bf16[192,512]{1,0:T(8,128)(2,1)S(1)}, u32[]{:S(2)}, u32[]{:S(2)}) collective-permute-start(bf16[192,512]{1,0:T(8,128)(2,1)S(1)} %get-tuple-element.49), channel_id=1, source_target_pairs={{0,3},{1,0},{2,1},{3,2},{4,7},{5,4},{6,5},{7,6},{8,11},{9,8},{10,9... | collective-permute-start | bytes 589832 | tf_op jit(solution)/shard_map/hidden_grad_y/ppermute | solution.py:52
  78.1 10.6 %collective-permute-start.24 = (bf16[192,512]{1,0:T(8,128)(2,1)S(1)}, bf16[192,512]{1,0:T(8,128)(2,1)S(1)}, u32[]{:S(2)}, u32[]{:S(2)}) collective-permute-start(bf16[192,512]{1,0:T(8,128)(2,1)S(1)} %get-tuple-element.51), channel_id=1, source_target_pairs={{0,4},{1,5},{2,6},{3,7},{4,0},{5,1},{6,2},{7,3},{8,12},{9,13},{10,... | collective-permute-start | bytes 589832 | tf_op jit(solution)/shard_map/hidden_grad_half/ppermute | solution.py:57
  84.5 6.4 %collective-permute-start.23 = (bf16[192,512]{1,0:T(8,128)(2,1)S(1)}, bf16[192,512]{1,0:T(8,128)(2,1)S(1)}, u32[]{:S(2)}, u32[]{:S(2)}) collective-permute-start(bf16[192,512]{1,0:T(8,128)(2,1)S(1)} %hidden.1.refs_1_), channel_id=1, source_target_pairs={{0,3},{1,0},{2,1},{3,2},{4,7},{5,4},{6,5},{7,6},{8,11},{9,8},{10,9... | collective-permute-start | bytes 589832 | tf_op jit(solution)/shard_map/hidden_y/ppermute | solution.py:52
  86.9 6.5 %collective-permute-start.22 = (bf16[192,512]{1,0:T(8,128)(2,1)S(1)}, bf16[192,512]{1,0:T(8,128)(2,1)S(1)}, u32[]{:S(2)}, u32[]{:S(2)}) collective-permute-start(bf16[192,512]{1,0:T(8,128)(2,1)S(1)} %hidden.1.refs_1_), channel_id=1, source_target_pairs={{0,2},{1,3},{2,0},{3,1},{4,6},{5,7},{6,4},{7,5},{8,10},{9,11},{10,... | collective-permute-start | bytes 589832 | tf_op jit(solution)/shard_map/hidden_y/ppermute | solution.py:52
  87.4 12.0 %collective-permute-start.21 = (bf16[192,512]{1,0:T(8,128)(2,1)S(1)}, bf16[192,512]{1,0:T(8,128)(2,1)S(1)}, u32[]{:S(2)}, u32[]{:S(2)}) collective-permute-start(bf16[192,512]{1,0:T(8,128)(2,1)S(1)} %hidden.1.refs_1_), channel_id=1, source_target_pairs={{0,1},{1,2},{2,3},{3,0},{4,5},{5,6},{6,7},{7,4},{8,9},{9,10},{10,1... | collective-permute-start | bytes 589832 | tf_op jit(solution)/shard_map/hidden_y/ppermute | solution.py:52
  100.5 3.6 %collective-permute-start.25 = (f32[384,1024]{1,0:T(8,128)S(1)}, f32[384,1024]{1,0:T(8,128)S(1)}, u32[]{:S(2)}, u32[]{:S(2)}) collective-permute-start(f32[384,1024]{1,0:T(8,128)S(1)} %get-tuple-element.53), channel_id=1, source_target_pairs={{0,8},{8,0},{16,24},{24,16},{32,40},{40,32},{48,56},{56,48},{64,72... | collective-permute-start | bytes 4718600 | tf_op jit(solution)/shard_map/output_core/ppermute | solution.py:47
  101.3 10.8 %collective-permute-start.31 = (bf16[192,1024]{1,0:T(8,128)(2,1)S(1)}, bf16[192,1024]{1,0:T(8,128)(2,1)S(1)}, u32[]{:S(2)}, u32[]{:S(2)}) collective-permute-start(bf16[192,1024]{1,0:T(8,128)(2,1)S(1)} %grads.1.refs_1_), channel_id=1, source_target_pairs={{0,3},{1,0},{2,1},{3,2},{4,7},{5,4},{6,5},{7,6},{8,11},{9,8},{10,9... | collective-permute-start | bytes 1179656 | tf_op jit(solution)/shard_map/grads_y/ppermute | solution.py:52
  101.7 12.0 %collective-permute-start.30 = (bf16[192,1024]{1,0:T(8,128)(2,1)S(1)}, bf16[192,1024]{1,0:T(8,128)(2,1)S(1)}, u32[]{:S(2)}, u32[]{:S(2)}) collective-permute-start(bf16[192,1024]{1,0:T(8,128)(2,1)S(1)} %grads.1.refs_1_), channel_id=1, source_target_pairs={{0,2},{1,3},{2,0},{3,1},{4,6},{5,7},{6,4},{7,5},{8,10},{9,11},{10,... | collective-permute-start | bytes 1179656 | tf_op jit(solution)/shard_map/grads_y/ppermute | solution.py:52
  102.2 20.5 %collective-permute-start.29 = (bf16[192,1024]{1,0:T(8,128)(2,1)S(1)}, bf16[192,1024]{1,0:T(8,128)(2,1)S(1)}, u32[]{:S(2)}, u32[]{:S(2)}) collective-permute-start(bf16[192,1024]{1,0:T(8,128)(2,1)S(1)} %grads.1.refs_1_), channel_id=1, source_target_pairs={{0,1},{1,2},{2,3},{3,0},{4,5},{5,6},{6,7},{7,4},{8,9},{9,10},{10,1... | collective-permute-start | bytes 1179656 | tf_op jit(solution)/shard_map/grads_y/ppermute | solution.py:52
  104.2 18.5 %collective-permute-start.26 = (bf16[96,1024]{1,0:T(8,128)(2,1)S(1)}, bf16[96,1024]{1,0:T(8,128)(2,1)S(1)}, u32[]{:S(2)}, u32[]{:S(2)}) collective-permute-start(bf16[96,1024]{1,0:T(8,128)(2,1)S(1)} %get-tuple-element.55), channel_id=1, source_target_pairs={{0,48},{8,56},{16,0},{24,8},{32,16},{40,24},{48,32},{56,40},{64,11... | collective-permute-start | bytes 589832 | tf_op jit(solution)/shard_map/output_x/ppermute | solution.py:42
  104.6 18.1 %collective-permute-start.27 = (bf16[96,1024]{1,0:T(8,128)(2,1)S(1)}, bf16[96,1024]{1,0:T(8,128)(2,1)S(1)}, u32[]{:S(2)}, u32[]{:S(2)}) collective-permute-start(bf16[96,1024]{1,0:T(8,128)(2,1)S(1)} %get-tuple-element.56), channel_id=1, source_target_pairs={{0,32},{8,40},{16,48},{24,56},{32,0},{40,8},{48,16},{56,24},{64,96... | collective-permute-start | bytes 589832 | tf_op jit(solution)/shard_map/output_x/ppermute | solution.py:42
  112.1 10.6 %collective-permute-start.28 = (bf16[96,1024]{1,0:T(8,128)(2,1)S(1)}, bf16[96,1024]{1,0:T(8,128)(2,1)S(1)}, u32[]{:S(2)}, u32[]{:S(2)}) collective-permute-start(bf16[96,1024]{1,0:T(8,128)(2,1)S(1)} %get-tuple-element.57), channel_id=1, source_target_pairs={{0,16},{8,24},{16,32},{24,40},{32,48},{40,56},{48,0},{56,8},{64,80... | collective-permute-start | bytes 589832 | tf_op jit(solution)/shard_map/output_x/ppermute | solution.py:42
  123.8 3.6 %collective-permute-start.32 = (f32[384,1024]{1,0:T(8,128)S(1)}, f32[384,1024]{1,0:T(8,128)S(1)}, u32[]{:S(2)}, u32[]{:S(2)}) collective-permute-start(f32[384,1024]{1,0:T(8,128)S(1)} %get-tuple-element.61.refs_1_), channel_id=1, source_target_pairs={{0,8},{8,0},{16,24},{24,16},{32,40},{40,32},{48,56},{56,48},{64,72... | collective-permute-start | bytes 4718600 | tf_op jit(solution)/shard_map/token_grad_core/ppermute | solution.py:47
  126.4 1.2 copy-start.2
  127.6 7.7 %collective-permute-start.34 = (bf16[96,1024]{1,0:T(8,128)(2,1)S(1)}, bf16[96,1024]{1,0:T(8,128)(2,1)S(1)}, u32[]{:S(2)}, u32[]{:S(2)}) collective-permute-start(bf16[96,1024]{1,0:T(8,128)(2,1)S(1)} %get-tuple-element.66), channel_id=1, source_target_pairs={{0,32},{8,40},{16,48},{24,56},{32,0},{40,8},{48,16},{56,24},{64,96... | collective-permute-start | bytes 589832 | tf_op jit(solution)/shard_map/token_grad_x/ppermute | solution.py:42
  129.0 8.6 %collective-permute-start.33 = (bf16[96,1024]{1,0:T(8,128)(2,1)S(1)}, bf16[96,1024]{1,0:T(8,128)(2,1)S(1)}, u32[]{:S(2)}, u32[]{:S(2)}) collective-permute-start(bf16[96,1024]{1,0:T(8,128)(2,1)S(1)} %get-tuple-element.65), channel_id=1, source_target_pairs={{0,48},{8,56},{16,0},{24,8},{32,16},{40,24},{48,32},{56,40},{64,11... | collective-permute-start | bytes 589832 | tf_op jit(solution)/shard_map/token_grad_x/ppermute | solution.py:42
  129.7 10.6 %collective-permute-start.35 = (bf16[96,1024]{1,0:T(8,128)(2,1)S(1)}, bf16[96,1024]{1,0:T(8,128)(2,1)S(1)}, u32[]{:S(2)}, u32[]{:S(2)}) collective-permute-start(bf16[96,1024]{1,0:T(8,128)(2,1)S(1)} %get-tuple-element.67), channel_id=1, source_target_pairs={{0,16},{8,24},{16,32},{24,40},{32,48},{40,56},{48,0},{56,8},{64,80... | collective-permute-start | bytes 589832 | tf_op jit(solution)/shard_map/token_grad_x/ppermute | solution.py:42
  136.5 3.8 %copy-start.3 = (bf16[1024,512]{1,0:T(8,128)(2,1)}, bf16[1024,512]{1,0:T(8,128)(2,1)S(1)}, u32[]{:S(2)}) copy-start(bf16[1024,512]{1,0:T(8,128)(2,1)S(1)} %convolution_convert_fusion.1.refs_8_) | copy-start | bytes 3145732
  137.6 2.9 %copy-start.4 = (bf16[1024,512]{1,0:T(8,128)(2,1)}, bf16[1024,512]{1,0:T(8,128)(2,1)S(1)}, u32[]{:S(2)}) copy-start(bf16[1024,512]{1,0:T(8,128)(2,1)S(1)} %convolution_convert_fusion.refs_9_) | copy-start | bytes 3145732
  140.5 3.9 %collective-permute-start.36 = (bf16[48,1024]{1,0:T(8,128)(2,1)S(1)}, bf16[48,1024]{1,0:T(8,128)(2,1)S(1)}, u32[]{:S(2)}, u32[]{:S(2)}) collective-permute-start(bf16[48,1024]{1,0:T(8,128)(2,1)S(1)} %get-tuple-element.72), channel_id=1, source_target_pairs={{0,192},{8,200},{16,208},{24,216},{32,224},{40,232},{48,240},{56,2... | collective-permute-start | bytes 294920 | tf_op jit(solution)/shard_map/both_z/ppermute | solution.py:37
  140.6 10.6 %collective-permute-start.37 = (bf16[48,1024]{1,0:T(8,128)(2,1)S(1)}, bf16[48,1024]{1,0:T(8,128)(2,1)S(1)}, u32[]{:S(2)}, u32[]{:S(2)}) collective-permute-start(bf16[48,1024]{1,0:T(8,128)(2,1)S(1)} %get-tuple-element.73), channel_id=1, source_target_pairs={{0,128},{8,136},{16,144},{24,152},{32,160},{40,168},{48,176},{56,1... | collective-permute-start | bytes 294920 | tf_op jit(solution)/shard_map/both_z/ppermute | solution.py:37
  142.2 9.0 %collective-permute-start.38 = (bf16[48,1024]{1,0:T(8,128)(2,1)S(1)}, bf16[48,1024]{1,0:T(8,128)(2,1)S(1)}, u32[]{:S(2)}, u32[]{:S(2)}) collective-permute-start(bf16[48,1024]{1,0:T(8,128)(2,1)S(1)} %get-tuple-element.74), channel_id=1, source_target_pairs={{0,64},{8,72},{16,80},{24,88},{32,96},{40,104},{48,112},{56,120},{... | collective-permute-start | bytes 294920 | tf_op jit(solution)/shard_map/both_z/ppermute | solution.py:37

commit v2 on v1

--- a/solution.py
+++ b/solution.py
@@ -223,9 +223,21 @@
     theirs[...] = dot(gg[half:, :], wg[...], 1, 1) + dot(ug[half:, :], wu[...], 1, 1)
 
 
+TILE = 256
+
+
+def token_products(first, gg, ug, wg, wu, o):
+    rows = slice(first, first + o.shape[0])
+
+    @pl.loop(0, o.shape[1] // TILE)
+    def _(j):
+        at = pl.ds(pl.multiple_of(j * TILE, TILE), TILE)
+        t = dot(gg[rows, :], wg[at, :], 1, 1)
+        o[:, at] = t + dot(ug[rows, :], wu[at, :], 1, 1)
+
+
 def tokens_own_kernel(gg, ug, wg, wu, own):
-    half = own.shape[0]
-    own[...] = dot(gg[:half, :], wg[...], 1, 1) + dot(ug[:half, :], wu[...], 1, 1)
+    token_products(0, gg, ug, wg, wu, own)
 
 
 def rs_first_kernel(mine, theirs, s1, s2, s3, own):
@@ -235,22 +247,26 @@
         o[...] = (mine[at, :] + theirs[at, :].astype(F32)).astype(o.dtype)
 
 
-def rs_next_kernel(o0, oa, ob, oc, t0, ta, tb, tc, s1, s2, s3, own):
-    both = []
-    for mine, a, b, c in ((o0, oa, ob, oc), (t0, ta, tb, tc)):
-        t = mine[...] + a[...].astype(F32) + b[...].astype(F32)
-        both.append(t + c[...].astype(F32))
-    n = own.shape[0] // 2
+def rs_next_kernel(mine, a, b, c, s1, s2, s3, own):
+    n = own.shape[0]
+    t = mine[...] + a[...].astype(F32) + b[...].astype(F32) + c[...].astype(F32)
     for k, o in enumerate((own, s1, s2, s3)):
-        t = jnp.concatenate([t[k * n : (k + 1) * n] for t in both], axis=0)
-        o[...] = t.astype(o.dtype)
-
-
-def rs_last_kernel(mine, a, b, c, output, grad):
+        o[...] = t[k * n : (k + 1) * n].astype(o.dtype)
+
+
+def rs_last_kernel(mine, a, b, c, out):
     t = mine[...] + a[...].astype(F32) + b[...].astype(F32) + c[...].astype(F32)
-    n = output.shape[0]
-    output[...] = t[:n].astype(BF)
-    grad[...] = t[n:].astype(BF)
+    out[...] = t.astype(BF)
+
+
+def next_row(own, got, after=()):
+    rows, w = own.shape
+    sends = [((rows // Z, w), BF)] * 3 + [((rows // Z, w), F32)]
+    return call(rs_next_kernel, sends, [own, *got], after=after)
+
+
+def last_row(own, got):
+    return call(rs_last_kernel, [(own.shape, BF)], [own, *got])[0]
 
 
 def first_row(own, theirs, after=()):
@@ -265,8 +281,9 @@
 
     t = gather_z(tokens, all_z(tokens, "tokens_z"))
     g = hold([cotangent], [t])[0]
-    g = gather_z(g, all_z(g, "cotangent_z"))
-    t = gather_x(t, all_x(t, "tokens_x"), after=[g])
+    got = all_z(g, "cotangent_z")
+    g = gather_z(g, got)
+    t = gather_x(t, all_x(t, "tokens_x"), after=got[:2])
     half = t.shape[0]
     n = CORES * half // Y
     flops = 2 * CORES * half * d * f
@@ -329,21 +346,18 @@
 
     all_hidden = hold([all_hidden], [their_gt])[0]
     grad_down = dot(all_hidden, all_cotangent, 0, 0).astype(BF)
+    s1, s2, s3, own_out = next_row(own_out, got_out)
     their_gt = send_core(their_gt, "token_grad_core")
-    s1, s2, s3, own_gt = first_row(own_gt, their_gt, [grad_down])
-    got = back_x([s1, s2, s3], "token_grad_x")
+    t1, t2, t3, own_gt = first_row(own_gt, their_gt, [grad_down, s1])
+    got = back_x([t1, t2, t3], "token_grad_x")
+    got_out = back_z(hold([s1, s2, s3], [got[1]]), "output_z")
     gg, ug = hold([gg, ug], [got[1]])
     grad_gate = dot(all_tokens, gg, 0, 0).astype(BF)
     grad_up = dot(all_tokens, ug, 0, 0).astype(BF)
-    rows = tokens.shape[0]
-    s1, s2, s3, own = call(
-        rs_next_kernel,
-        [((2 * rows, d), BF)] * 3 + [((2 * rows, d), F32)],
-        [own_out, *got_out, own_gt, *got],
-        after=[grad_gate, grad_up],
-    )
-    got = back_z([s1, s2, s3], "both_z")
-    output, grad_tokens = call(rs_last_kernel, [((rows, d), BF)] * 2, [own, *got])
+    s1, s2, s3, own_gt = next_row(own_gt, got, after=[grad_gate, grad_up, got_out[1]])
+    got = back_z([s1, s2, s3], "token_grad_z")
+    grad_tokens = last_row(own_gt, got)
+    output = last_row(own_out, got_out)
     return (output, grad_tokens, grad_gate, grad_up, grad_down)
 
 

time: 152 us -> 151 us (level); the launches traced: 152 us -> 149 us
  waiting for transfers between devices: 82.2 us -> 75.2 us
  starting transfers between devices: 54 us -> 56.2 us
    ppermute x2, waiting for transfers between devices: 9.1 us -> 17.6 us  [send_half(): return lax.ppermute(a, 'col', col_perm(lambda h, y: (h + 1, y)))]
    ppermute x9 -> x12, waiting for transfers between devices: 18.3 us -> 10.9 us  [send_z(): return lax.ppermute(a, 'row', row_perm(lambda z, x, c: (z + k, x, c)))]
    ppermute x12, waiting for transfers between devices: 32.1 us -> 25.3 us  [send_y(): return lax.ppermute(a, 'col', col_perm(lambda h, y: (h, y + k)))]
    ppermute x9 -> x12, starting transfers between devices: 12.1 us -> 17.7 us  [send_z(): return lax.ppermute(a, 'row', row_perm(lambda z, x, c: (z + k, x, c)))]
    ppermute x2, starting transfers between devices: 11.9 us -> 8.97 us  [send_half(): return lax.ppermute(a, 'col', col_perm(lambda h, y: (h + 1, y)))]
    ppermute x4, waiting for transfers between devices: 4.2 us -> 1.47 us  [send_core(): return lax.ppermute(a, 'row', row_perm(lambda z, x, c: (z, x, c + 1)))]
    ppermute x4, starting transfers between devices: 5.38 us -> 3.56 us  [send_core(): return lax.ppermute(a, 'row', row_perm(lambda z, x, c: (z, x, c + 1)))]
    pallas_call x23 -> x26, Pallas kernels: 9.97 us -> 11.2 us  [call(): pl.pallas_call(body, name=kernel.__name__.removesuffix('_kernel'), out_sh...]
  transfers between devices with their start and end apart: 39 -> 42, of which waited for: 24 -> 24; matrix products, arithmetic and copies ran while one was open for 2% -> 2% of each run, Pallas kernels for 2% -> 3%
where the time goes in v2:
time: 151 us; the launch traced here: 149 us
  waiting for transfers between devices  75.2 us (50%)
  starting transfers between devices  56.2 us (37%)
  Pallas kernels  11.2 us (7%)
  matrix products  3.08 us (2%)
  local copies, waits for them, and re-layouts  2.13 us (1%)
    ppermute x12, waiting for transfers between devices, send_y(): return lax.ppermute(a, 'col', col_perm(lambda h, y: (h, y + k)))  25.3 us
    ppermute x12, waiting for transfers between devices, send_x(): return lax.ppermute(a, 'row', row_perm(lambda z, x, c: (z, x + k, c)))  20 us
    ppermute x12, starting transfers between devices, send_z(): return lax.ppermute(a, 'row', row_perm(lambda z, x, c: (z + k, x, c)))  17.7 us
    ppermute x2, waiting for transfers between devices, send_half(): return lax.ppermute(a, 'col', col_perm(lambda h, y: (h + 1, y)))  17.6 us
    ppermute x12, starting transfers between devices, send_y(): return lax.ppermute(a, 'col', col_perm(lambda h, y: (h, y + k)))  14.1 us
    ppermute x12, starting transfers between devices, send_x(): return lax.ppermute(a, 'row', row_perm(lambda z, x, c: (z, x + k, c)))  11.9 us
    pallas_call x26, Pallas kernels, call(): pl.pallas_call(body, name=kernel.__name__.removesuffix('_kernel'), out_sh...  11.2 us
    ppermute x12, waiting for transfers between devices, send_z(): return lax.ppermute(a, 'row', row_perm(lambda z, x, c: (z + k, x, c)))  10.9 us
  transfers between devices with their start and end apart: 42, of which 24 were waited for; matrix products, arithmetic and copies ran while one was open for 2% of the time, Pallas kernels for 3%

profile of v2, /device:TPU:1, one launch (start us, length us, event | category | flops | bytes accessed | tf_op | source)
XLA Modules:
  0.0 148.7 jit_solution(3804353837433330267)
XLA Ops:
  0.7 2.5 %collective-permute-start = (bf16[24,1024]{1,0:T(8,128)(2,1)}, bf16[24,1024]{1,0:T(8,128)(2,1)S(1)}, u32[]{:S(2)}, u32[]{:S(2)}) collective-permute-start(bf16[24,1024]{1,0:T(8,128)(2,1)} %refs_0_.2), channel_id=1, source_target_pairs={{0,64},{8,72},{16,80},{24,88},{32,96},{40,104},{48,112},{56,120},{... | collective-permute-start | bytes 147464 | tf_op jit(solution)/shard_map/tokens_z/ppermute | solution.py:37
  3.2 2.8 %collective-permute-start.2 = (bf16[24,1024]{1,0:T(8,128)(2,1)}, bf16[24,1024]{1,0:T(8,128)(2,1)S(1)}, u32[]{:S(2)}, u32[]{:S(2)}) collective-permute-start(bf16[24,1024]{1,0:T(8,128)(2,1)} %refs_0_.2), channel_id=1, source_target_pairs={{0,192},{8,200},{16,208},{24,216},{32,224},{40,232},{48,240},{56,2... | collective-permute-start | bytes 147464 | tf_op jit(solution)/shard_map/tokens_z/ppermute | solution.py:37
  6.2 0.8 copy-done.6
  7.0 0.6 collective-permute-done.b
  7.6 3.6 %collective-permute-done.1.c = bf16[24,1024]{1,0:T(8,128)(2,1)S(1)} collective-permute-done((bf16[24,1024]{1,0:T(8,128)(2,1)}, bf16[24,1024]{1,0:T(8,128)(2,1)S(1)}, u32[]{:S(2)}, u32[]{:S(2)}) %collective-permute-start.1) | collective-permute-done | bytes 49184 | tf_op jit(solution)/shard_map/tokens_z/ppermute | solution.py:37
  11.2 1.6 %collective-permute-start.5 = (bf16[96,1024]{1,0:T(8,128)(2,1)S(1)}, bf16[96,1024]{1,0:T(8,128)(2,1)S(1)}, u32[]{:S(2)}, u32[]{:S(2)}) collective-permute-start(bf16[96,1024]{1,0:T(8,128)(2,1)S(1)} %cat_z.2.refs_1_.refs_0_), channel_id=1, source_target_pairs={{0,48},{8,56},{16,0},{24,8},{32,16},{40,24},{48,32},{56,40},{64,11... | collective-permute-start | bytes 589832 | tf_op jit(solution)/shard_map/tokens_x/ppermute | solution.py:42
  12.8 0.5 collective-permute-start.4
  13.3 0.6 collective-permute-start.3
  13.9 0.8 copy-done.5
  15.1 3.4 %collective-permute-start.6 = (bf16[24,1024]{1,0:T(8,128)(2,1)S(1)}, bf16[24,1024]{1,0:T(8,128)(2,1)S(1)}, u32[]{:S(2)}, u32[]{:S(2)}) collective-permute-start(bf16[24,1024]{1,0:T(8,128)(2,1)S(1)} %hold.8.refs_0_), channel_id=1, source_target_pairs={{0,64},{8,72},{16,80},{24,88},{32,96},{40,104},{48,112},{56,120},{... | collective-permute-start | bytes 147464 | tf_op jit(solution)/shard_map/cotangent_z/ppermute | solution.py:37
  18.6 2.0 %collective-permute-done.6.refs_4_.b = bf16[24,1024]{1,0:T(8,128)(2,1)S(1)} collective-permute-done((bf16[24,1024]{1,0:T(8,128)(2,1)S(1)}, bf16[24,1024]{1,0:T(8,128)(2,1)S(1)}, u32[]{:S(2)}, u32[]{:S(2)}) %collective-permute-start.6) | collective-permute-done | bytes 49184 | tf_op jit(solution)/shard_map/cotangent_z/ppermute | solution.py:37
  20.5 3.9 %collective-permute-done.3.refs_1_ = bf16[96,1024]{1,0:T(8,128)(2,1)S(1)} collective-permute-done((bf16[96,1024]{1,0:T(8,128)(2,1)S(1)}, bf16[96,1024]{1,0:T(8,128)(2,1)S(1)}, u32[]{:S(2)}, u32[]{:S(2)}) %collective-permute-start.3) | collective-permute-done | bytes 196640 | tf_op jit(solution)/shard_map/tokens_x/ppermute | solution.py:42
  24.5 1.5 collective-permute-start.8
  26.0 3.5 %collective-permute-start.12 = (bf16[24,1024]{1,0:T(8,128)(2,1)S(1)}, bf16[24,1024]{1,0:T(8,128)(2,1)S(1)}, u32[]{:S(2)}, u32[]{:S(2)}) collective-permute-start(bf16[24,1024]{1,0:T(8,128)(2,1)S(1)} %hold.8.refs_0_), channel_id=1, source_target_pairs={{0,192},{8,200},{16,208},{24,216},{32,224},{40,232},{48,240},{56,2... | collective-permute-start | bytes 147464 | tf_op jit(solution)/shard_map/cotangent_z/ppermute | solution.py:37
  29.5 1.2 collective-permute-done.12.d
  30.7 3.1 %up.1 = (bf16[768,1024]{1,0:T(8,128)(2,1)S(1)}, bf16[192,1024]{1,0:T(8,128)(2,1)S(1)}, bf16[192,1024]{1,0:T(8,128)(2,1)S(1)}, bf16[192,1024]{1,0:T(8,128)(2,1)S(1)}, f32[192,1024]{1,0:T(8,128)S(1)}) custom-call(s32[1]{0:T(128)} %bitcast.y.refs_0_, bf16[384,1024]{1,0:T(8,128)(2,1)S(1)} %cat_x.2.mine, bf16[384,1024]{1,0:T(8,128)(2,1)} %collective-permute-done.8.theirs, ...), custom_call_target="tpu_custom_call" | custom-call | flops 1610612736 | bytes 7208960 | tf_op jit(solution)/shard_map/up/pallas_call | solution.py:84
  34.2 2.9 %collective-permute-start.10 = (bf16[192,1024]{1,0:T(8,128)(2,1)S(1)}, bf16[192,1024]{1,0:T(8,128)(2,1)S(1)}, u32[]{:S(2)}, u32[]{:S(2)}) collective-permute-start(bf16[192,1024]{1,0:T(8,128)(2,1)S(1)} %get-tuple-element.48), channel_id=1, source_target_pairs={{0,2},{1,3},{2,0},{3,1},{4,6},{5,7},{6,4},{7,5},{8,10},{9,11},{10,... | collective-permute-start | bytes 1179656 | tf_op jit(solution)/shard_map/gate_up_y/ppermute | solution.py:52
  37.2 0.8 collective-permute-start.11
  37.9 0.7 collective-permute-start.9
  38.6 0.5 collective-permute-start.14
  39.8 5.2 %collective-permute-done.14.refs_5_.refs_2_ = bf16[96,1024]{1,0:T(8,128)(2,1)S(1)} collective-permute-done((bf16[96,1024]{1,0:T(8,128)(2,1)S(1)}, bf16[96,1024]{1,0:T(8,128)(2,1)S(1)}, u32[]{:S(2)}, u32[]{:S(2)}) %collective-permute-start.14) | collective-permute-done | bytes 196640 | tf_op jit(solution)/shard_map/cotangent_x/ppermute | solution.py:42
  45.0 5.5 %collective-permute-done.13.refs_4_.refs_1_ = bf16[96,1024]{1,0:T(8,128)(2,1)S(1)} collective-permute-done((bf16[96,1024]{1,0:T(8,128)(2,1)S(1)}, bf16[96,1024]{1,0:T(8,128)(2,1)S(1)}, u32[]{:S(2)}, u32[]{:S(2)}) %collective-permute-start.13) | collective-permute-done | bytes 196640 | tf_op jit(solution)/shard_map/cotangent_x/ppermute | solution.py:42
  50.5 4.1 %collective-permute-done.11.refs_3_.refs_6_ = bf16[192,1024]{1,0:T(8,128)(2,1)S(1)} collective-permute-done((bf16[192,1024]{1,0:T(8,128)(2,1)S(1)}, bf16[192,1024]{1,0:T(8,128)(2,1)S(1)}, u32[]{:S(2)}, u32[]{:S(2)}) %collective-permute-start.11) | collective-permute-done | bytes 393248 | tf_op jit(solution)/shard_map/gate_up_y/ppermute | solution.py:52
  54.5 0.7 collective-permute-done.9.refs_1_.refs_4_
  55.3 1.0 collective-permute-start.17
  56.5 4.5 %collective-permute-start.16 = (bf16[192,1024]{1,0:T(8,128)(2,1)S(1)}, bf16[192,1024]{1,0:T(8,128)(2,1)S(1)}, u32[]{:S(2)}, u32[]{:S(2)}) collective-permute-start(bf16[192,1024]{1,0:T(8,128)(2,1)S(1)} %get-tuple-element.51), channel_id=1, source_target_pairs={{0,4},{1,5},{2,6},{3,7},{4,0},{5,1},{6,2},{7,3},{8,12},{9,13},{10,... | collective-permute-start | bytes 1179656 | tf_op jit(solution)/shard_map/gate_up_half/ppermute | solution.py:57
  60.9 1.5 %back.1 = (bf16[768,1024]{1,0:T(8,128)(2,1)S(1)}, bf16[192,512]{1,0:T(8,128)(2,1)S(1)}, bf16[192,512]{1,0:T(8,128)(2,1)S(1)}, bf16[192,512]{1,0:T(8,128)(2,1)S(1)}, f32[192,512]{1,0:T(8,128)S(1)}) custom-call(s32[1]{0:T(128)} %bitcast.y.refs_0_, bf16[384,1024]{1,0:T(8,128)(2,1)S(1)} %cat_x.3.mine, bf16[384,1024]{1,0:T(8,128)(2,1)S(1)} %collective-permute-done.17.theirs, ...), custom_call_target="tpu_custom_call" | custom-call | flops 805306368 | bytes 5177344 | tf_op jit(solution)/shard_map/back/pallas_call | solution.py:84
  62.5 1.1 collective-permute-start.18
  63.6 2.5 %collective-permute-start.19 = (bf16[192,512]{1,0:T(8,128)(2,1)S(1)}, bf16[192,512]{1,0:T(8,128)(2,1)S(1)}, u32[]{:S(2)}, u32[]{:S(2)}) collective-permute-start(bf16[192,512]{1,0:T(8,128)(2,1)S(1)} %get-tuple-element.53), channel_id=1, source_target_pairs={{0,2},{1,3},{2,0},{3,1},{4,6},{5,7},{6,4},{7,5},{8,10},{9,11},{10,... | collective-permute-start | bytes 589832 | tf_op jit(solution)/shard_map/hidden_grad_y/ppermute | solution.py:52
  66.1 1.1 collective-permute-start.20
  67.2 12.6 %collective-permute-done.16.refs_1_.refs_4_ = bf16[192,1024]{1,0:T(8,128)(2,1)S(1)} collective-permute-done((bf16[192,1024]{1,0:T(8,128)(2,1)S(1)}, bf16[192,1024]{1,0:T(8,128)(2,1)S(1)}, u32[]{:S(2)}, u32[]{:S(2)}) %collective-permute-start.16) | collective-permute-done | bytes 393248 | tf_op jit(solution)/shard_map/gate_up_half/ppermute | solution.py:57
  79.9 4.5 %collective-permute-start.24 = (bf16[192,512]{1,0:T(8,128)(2,1)S(1)}, bf16[192,512]{1,0:T(8,128)(2,1)S(1)}, u32[]{:S(2)}, u32[]{:S(2)}) collective-permute-start(bf16[192,512]{1,0:T(8,128)(2,1)S(1)} %get-tuple-element.56), channel_id=1, source_target_pairs={{0,4},{1,5},{2,6},{3,7},{4,0},{5,1},{6,2},{7,3},{8,12},{9,13},{10,... | collective-permute-start | bytes 589832 | tf_op jit(solution)/shard_map/hidden_grad_half/ppermute | solution.py:57
  84.5 2.4 %collective-permute-start.23 = (bf16[192,512]{1,0:T(8,128)(2,1)S(1)}, bf16[192,512]{1,0:T(8,128)(2,1)S(1)}, u32[]{:S(2)}, u32[]{:S(2)}) collective-permute-start(bf16[192,512]{1,0:T(8,128)(2,1)S(1)} %hidden.1.refs_1_), channel_id=1, source_target_pairs={{0,3},{1,0},{2,1},{3,2},{4,7},{5,4},{6,5},{7,6},{8,11},{9,8},{10,9... | collective-permute-start | bytes 589832 | tf_op jit(solution)/shard_map/hidden_y/ppermute | solution.py:52
  86.9 0.5 collective-permute-start.22
  87.4 0.5 collective-permute-start.21
  88.0 5.0 %collective-permute-done.24.refs_6_.refs_3_ = bf16[192,512]{1,0:T(8,128)(2,1)S(1)} collective-permute-done((bf16[192,512]{1,0:T(8,128)(2,1)S(1)}, bf16[192,512]{1,0:T(8,128)(2,1)S(1)}, u32[]{:S(2)}, u32[]{:S(2)}) %collective-permute-start.24) | collective-permute-done | bytes 196640 | tf_op jit(solution)/shard_map/hidden_grad_half/ppermute | solution.py:57
  93.0 0.8 collective-permute-done.22.refs_3_.refs_5_
  93.8 5.7 %collective-permute-done.21.refs_2_.refs_4_ = bf16[192,512]{1,0:T(8,128)(2,1)S(1)} collective-permute-done((bf16[192,512]{1,0:T(8,128)(2,1)S(1)}, bf16[192,512]{1,0:T(8,128)(2,1)S(1)}, u32[]{:S(2)}, u32[]{:S(2)}) %collective-permute-start.21) | collective-permute-done | bytes 196640 | tf_op jit(solution)/shard_map/hidden_y/ppermute | solution.py:52
  99.5 1.0 out.1
  100.5 0.6 collective-permute-start.25
  101.7 0.5 collective-permute-start.30
  102.2 0.7 collective-permute-start.29
  102.9 1.2 collective-permute-done.25.theirs
  104.2 0.8 collective-permute-start.26
  105.0 2.4 %collective-permute-start.27 = (bf16[96,1024]{1,0:T(8,128)(2,1)S(1)}, bf16[96,1024]{1,0:T(8,128)(2,1)S(1)}, u32[]{:S(2)}, u32[]{:S(2)}) collective-permute-start(bf16[96,1024]{1,0:T(8,128)(2,1)S(1)} %get-tuple-element.61), channel_id=1, source_target_pairs={{0,32},{8,40},{16,48},{24,56},{32,0},{40,8},{48,16},{56,24},{64,96... | collective-permute-start | bytes 589832 | tf_op jit(solution)/shard_map/output_x/ppermute | solution.py:42
  107.5 4.7 %collective-permute-done.31.refs_4_ = bf16[192,1024]{1,0:T(8,128)(2,1)S(1)} collective-permute-done((bf16[192,1024]{1,0:T(8,128)(2,1)S(1)}, bf16[192,1024]{1,0:T(8,128)(2,1)S(1)}, u32[]{:S(2)}, u32[]{:S(2)}) %collective-permute-start.31) | collective-permute-done | bytes 393248 | tf_op jit(solution)/shard_map/grads_y/ppermute | solution.py:52
  112.1 1.1 collective-permute-start.28
  113.7 9.0 %collective-permute-done.29.refs_2_ = bf16[192,1024]{1,0:T(8,128)(2,1)S(1)} collective-permute-done((bf16[192,1024]{1,0:T(8,128)(2,1)S(1)}, bf16[192,1024]{1,0:T(8,128)(2,1)S(1)}, u32[]{:S(2)}, u32[]{:S(2)}) %collective-permute-start.29) | collective-permute-done | bytes 393248 | tf_op jit(solution)/shard_map/grads_y/ppermute | solution.py:52
  122.7 1.1 tokens.1
  123.8 0.6 collective-permute-start.32
  124.5 1.6 %tokens_own.1.refs_0_ = f32[384,1024]{1,0:T(8,128)S(1)} custom-call(bf16[768,512]{1,0:T(8,128)(2,1)S(1)} %get-tuple-element.68.gg.refs_0_, bf16[768,512]{1,0:T(8,128)(2,1)S(1)} %get-tuple-element.69.ug.refs_1_, bf16[1024,512]{1,0:T(8,128)(2,1)S(1)} %copy-done, bf16[1024,512]{1,0:T(8,128)(2,1)S(1)} %copy-done.1), custom_call_target="tpu_custom_call" | custom-call | flops 805306368 | bytes 5242880 | tf_op jit(solution)/shard_map/tokens_own/pallas_call | solution.py:84
  126.1 1.0 convolution_convert_fusion.2.refs_2_
  128.1 3.5 %collective-permute-start.37 = (bf16[96,1024]{1,0:T(8,128)(2,1)S(1)}, bf16[96,1024]{1,0:T(8,128)(2,1)S(1)}, u32[]{:S(2)}, u32[]{:S(2)}) collective-permute-start(bf16[96,1024]{1,0:T(8,128)(2,1)S(1)} %get-tuple-element.78), channel_id=1, source_target_pairs={{0,48},{8,56},{16,0},{24,8},{32,16},{40,24},{48,32},{56,40},{64,11... | collective-permute-start | bytes 589832 | tf_op jit(solution)/shard_map/token_grad_x/ppermute | solution.py:42
  131.6 4.4 %collective-permute-done.33.refs_3_.refs_2_ = bf16[96,1024]{1,0:T(8,128)(2,1)S(1)} collective-permute-done((bf16[96,1024]{1,0:T(8,128)(2,1)S(1)}, bf16[96,1024]{1,0:T(8,128)(2,1)S(1)}, u32[]{:S(2)}, u32[]{:S(2)}) %collective-permute-start.33) | collective-permute-done | bytes 196640 | tf_op jit(solution)/shard_map/token_grad_x/ppermute | solution.py:42
  136.3 1.4 collective-permute-start.36
  137.8 1.0 convolution_convert_fusion.1.refs_4_
  138.8 1.0 convolution_convert_fusion.refs_5_
  139.9 0.6 collective-permute-done.38.refs_3_
  140.6 1.9 %collective-permute-start.39 = (bf16[24,1024]{1,0:T(8,128)(2,1)S(1)}, bf16[24,1024]{1,0:T(8,128)(2,1)S(1)}, u32[]{:S(2)}, u32[]{:S(2)}) collective-permute-start(bf16[24,1024]{1,0:T(8,128)(2,1)S(1)} %get-tuple-element.84), channel_id=1, source_target_pairs={{0,192},{8,200},{16,208},{24,216},{32,224},{40,232},{48,240},{56,2... | collective-permute-start | bytes 147464 | tf_op jit(solution)/shard_map/token_grad_z/ppermute | solution.py:37
  142.8 1.1 collective-permute-start.41
  143.9 0.6 rs_last.2
  144.6 1.8 %collective-permute-done.40.b = bf16[24,1024]{1,0:T(8,128)(2,1)S(1)} collective-permute-done((bf16[24,1024]{1,0:T(8,128)(2,1)S(1)}, bf16[24,1024]{1,0:T(8,128)(2,1)S(1)}, u32[]{:S(2)}, u32[]{:S(2)}) %collective-permute-start.40) | collective-permute-done | bytes 49184 | tf_op jit(solution)/shard_map/token_grad_z/ppermute | solution.py:37
  146.4 1.7 %collective-permute-done.41.c = bf16[24,1024]{1,0:T(8,128)(2,1)S(1)} collective-permute-done((bf16[24,1024]{1,0:T(8,128)(2,1)S(1)}, bf16[24,1024]{1,0:T(8,128)(2,1)S(1)}, u32[]{:S(2)}, u32[]{:S(2)}) %collective-permute-start.41) | collective-permute-done | bytes 49184 | tf_op jit(solution)/shard_map/token_grad_z/ppermute | solution.py:37
  148.0 0.6 rs_last.3
  (65 shorter events, 5.4 us)
Async XLA Ops:
  0.6 30.1 %copy-start.1 = (bf16[1024,512]{1,0:T(8,128)(2,1)S(1)}, bf16[1024,512]{1,0:T(8,128)(2,1)}, u32[]{:S(2)}) copy-start(bf16[1024,512]{1,0:T(8,128)(2,1)} %wu.3) | copy-start | bytes 3145732
  0.6 30.1 %copy-start = (bf16[1024,512]{1,0:T(8,128)(2,1)S(1)}, bf16[1024,512]{1,0:T(8,128)(2,1)}, u32[]{:S(2)}) copy-start(bf16[1024,512]{1,0:T(8,128)(2,1)} %wg.3) | copy-start | bytes 3145732
  0.7 7.0 %collective-permute-start = (bf16[24,1024]{1,0:T(8,128)(2,1)}, bf16[24,1024]{1,0:T(8,128)(2,1)S(1)}, u32[]{:S(2)}, u32[]{:S(2)}) collective-permute-start(bf16[24,1024]{1,0:T(8,128)(2,1)} %refs_0_.2), channel_id=1, source_target_pairs={{0,64},{8,72},{16,80},{24,88},{32,96},{40,104},{48,112},{56,120},{... | collective-permute-start | bytes 147464 | tf_op jit(solution)/shard_map/tokens_z/ppermute | solution.py:37
  3.2 4.4 %collective-permute-start.2 = (bf16[24,1024]{1,0:T(8,128)(2,1)}, bf16[24,1024]{1,0:T(8,128)(2,1)S(1)}, u32[]{:S(2)}, u32[]{:S(2)}) collective-permute-start(bf16[24,1024]{1,0:T(8,128)(2,1)} %refs_0_.2), channel_id=1, source_target_pairs={{0,192},{8,200},{16,208},{24,216},{32,224},{40,232},{48,240},{56,2... | collective-permute-start | bytes 147464 | tf_op jit(solution)/shard_map/tokens_z/ppermute | solution.py:37
  6.0 5.2 %collective-permute-start.1 = (bf16[24,1024]{1,0:T(8,128)(2,1)}, bf16[24,1024]{1,0:T(8,128)(2,1)S(1)}, u32[]{:S(2)}, u32[]{:S(2)}) collective-permute-start(bf16[24,1024]{1,0:T(8,128)(2,1)} %refs_0_.2), channel_id=1, source_target_pairs={{0,128},{8,136},{16,144},{24,152},{32,160},{40,168},{48,176},{56,1... | collective-permute-start | bytes 147464 | tf_op jit(solution)/shard_map/tokens_z/ppermute | solution.py:37
  6.2 0.8 copy-start.6
  11.2 9.3 %collective-permute-start.5 = (bf16[96,1024]{1,0:T(8,128)(2,1)S(1)}, bf16[96,1024]{1,0:T(8,128)(2,1)S(1)}, u32[]{:S(2)}, u32[]{:S(2)}) collective-permute-start(bf16[96,1024]{1,0:T(8,128)(2,1)S(1)} %cat_z.2.refs_1_.refs_0_), channel_id=1, source_target_pairs={{0,48},{8,56},{16,0},{24,8},{32,16},{40,24},{48,32},{56,40},{64,11... | collective-permute-start | bytes 589832 | tf_op jit(solution)/shard_map/tokens_x/ppermute | solution.py:42
  12.8 7.7 %collective-permute-start.4 = (bf16[96,1024]{1,0:T(8,128)(2,1)S(1)}, bf16[96,1024]{1,0:T(8,128)(2,1)S(1)}, u32[]{:S(2)}, u32[]{:S(2)}) collective-permute-start(bf16[96,1024]{1,0:T(8,128)(2,1)S(1)} %cat_z.2.refs_1_.refs_0_), channel_id=1, source_target_pairs={{0,32},{8,40},{16,48},{24,56},{32,0},{40,8},{48,16},{56,24},{64,96... | collective-permute-start | bytes 589832 | tf_op jit(solution)/shard_map/tokens_x/ppermute | solution.py:42
  13.3 11.1 %collective-permute-start.3 = (bf16[96,1024]{1,0:T(8,128)(2,1)S(1)}, bf16[96,1024]{1,0:T(8,128)(2,1)S(1)}, u32[]{:S(2)}, u32[]{:S(2)}) collective-permute-start(bf16[96,1024]{1,0:T(8,128)(2,1)S(1)} %cat_z.2.refs_1_.refs_0_), channel_id=1, source_target_pairs={{0,16},{8,24},{16,32},{24,40},{32,48},{40,56},{48,0},{56,8},{64,80... | collective-permute-start | bytes 589832 | tf_op jit(solution)/shard_map/tokens_x/ppermute | solution.py:42
  13.9 0.8 copy-start.5
  14.7 3.8 %collective-permute-start.7 = (bf16[24,1024]{1,0:T(8,128)(2,1)S(1)}, bf16[24,1024]{1,0:T(8,128)(2,1)S(1)}, u32[]{:S(2)}, u32[]{:S(2)}) collective-permute-start(bf16[24,1024]{1,0:T(8,128)(2,1)S(1)} %hold.8.refs_0_), channel_id=1, source_target_pairs={{0,128},{8,136},{16,144},{24,152},{32,160},{40,168},{48,176},{56,1... | collective-permute-start | bytes 147464 | tf_op jit(solution)/shard_map/cotangent_z/ppermute | solution.py:37
  15.1 5.4 %collective-permute-start.6 = (bf16[24,1024]{1,0:T(8,128)(2,1)S(1)}, bf16[24,1024]{1,0:T(8,128)(2,1)S(1)}, u32[]{:S(2)}, u32[]{:S(2)}) collective-permute-start(bf16[24,1024]{1,0:T(8,128)(2,1)S(1)} %hold.8.refs_0_), channel_id=1, source_target_pairs={{0,64},{8,72},{16,80},{24,88},{32,96},{40,104},{48,112},{56,120},{... | collective-permute-start | bytes 147464 | tf_op jit(solution)/shard_map/cotangent_z/ppermute | solution.py:37
  24.5 6.2 %collective-permute-start.8 = (bf16[384,1024]{1,0:T(8,128)(2,1)S(1)}, bf16[384,1024]{1,0:T(8,128)(2,1)}, u32[]{:S(2)}, u32[]{:S(2)}) collective-permute-start(bf16[384,1024]{1,0:T(8,128)(2,1)S(1)} %cat_x.2.mine), channel_id=1, source_target_pairs={{0,8},{8,0},{16,24},{24,16},{32,40},{40,32},{48,56},{56,48},{64,72... | collective-permute-start | bytes 2359304 | tf_op jit(solution)/shard_map/tokens_core/ppermute | solution.py:47
  26.0 4.7 %collective-permute-start.12 = (bf16[24,1024]{1,0:T(8,128)(2,1)S(1)}, bf16[24,1024]{1,0:T(8,128)(2,1)S(1)}, u32[]{:S(2)}, u32[]{:S(2)}) collective-permute-start(bf16[24,1024]{1,0:T(8,128)(2,1)S(1)} %hold.8.refs_0_), channel_id=1, source_target_pairs={{0,192},{8,200},{16,208},{24,216},{32,224},{40,232},{48,240},{56,2... | collective-permute-start | bytes 147464 | tf_op jit(solution)/shard_map/cotangent_z/ppermute | solution.py:37
  33.8 5.6 %collective-permute-start.15 = (bf16[96,1024]{1,0:T(8,128)(2,1)S(1)}, bf16[96,1024]{1,0:T(8,128)(2,1)S(1)}, u32[]{:S(2)}, u32[]{:S(2)}) collective-permute-start(bf16[96,1024]{1,0:T(8,128)(2,1)S(1)} %hold.10.refs_0_), channel_id=1, source_target_pairs={{0,48},{8,56},{16,0},{24,8},{32,16},{40,24},{48,32},{56,40},{64,11... | collective-permute-start | bytes 589832 | tf_op jit(solution)/shard_map/cotangent_x/ppermute | solution.py:42
  34.2 16.2 %collective-permute-start.10 = (bf16[192,1024]{1,0:T(8,128)(2,1)S(1)}, bf16[192,1024]{1,0:T(8,128)(2,1)S(1)}, u32[]{:S(2)}, u32[]{:S(2)}) collective-permute-start(bf16[192,1024]{1,0:T(8,128)(2,1)S(1)} %get-tuple-element.48), channel_id=1, source_target_pairs={{0,2},{1,3},{2,0},{3,1},{4,6},{5,7},{6,4},{7,5},{8,10},{9,11},{10,... | collective-permute-start | bytes 1179656 | tf_op jit(solution)/shard_map/gate_up_y/ppermute | solution.py:52
  37.2 17.4 %collective-permute-start.11 = (bf16[192,1024]{1,0:T(8,128)(2,1)S(1)}, bf16[192,1024]{1,0:T(8,128)(2,1)S(1)}, u32[]{:S(2)}, u32[]{:S(2)}) collective-permute-start(bf16[192,1024]{1,0:T(8,128)(2,1)S(1)} %get-tuple-element.49), channel_id=1, source_target_pairs={{0,3},{1,0},{2,1},{3,2},{4,7},{5,4},{6,5},{7,6},{8,11},{9,8},{10,9... | collective-permute-start | bytes 1179656 | tf_op jit(solution)/shard_map/gate_up_y/ppermute | solution.py:52
  37.9 17.3 %collective-permute-start.9 = (bf16[192,1024]{1,0:T(8,128)(2,1)S(1)}, bf16[192,1024]{1,0:T(8,128)(2,1)S(1)}, u32[]{:S(2)}, u32[]{:S(2)}) collective-permute-start(bf16[192,1024]{1,0:T(8,128)(2,1)S(1)} %get-tuple-element.47.refs_1_), channel_id=1, source_target_pairs={{0,1},{1,2},{2,3},{3,0},{4,5},{5,6},{6,7},{7,4},{8,9},{9,10},{10,1... | collective-permute-start | bytes 1179656 | tf_op jit(solution)/shard_map/gate_up_y/ppermute | solution.py:52
  38.6 6.3 %collective-permute-start.14 = (bf16[96,1024]{1,0:T(8,128)(2,1)S(1)}, bf16[96,1024]{1,0:T(8,128)(2,1)S(1)}, u32[]{:S(2)}, u32[]{:S(2)}) collective-permute-start(bf16[96,1024]{1,0:T(8,128)(2,1)S(1)} %hold.10.refs_0_), channel_id=1, source_target_pairs={{0,32},{8,40},{16,48},{24,56},{32,0},{40,8},{48,16},{56,24},{64,96... | collective-permute-start | bytes 589832 | tf_op jit(solution)/shard_map/cotangent_x/ppermute | solution.py:42
  39.4 11.1 %collective-permute-start.13 = (bf16[96,1024]{1,0:T(8,128)(2,1)S(1)}, bf16[96,1024]{1,0:T(8,128)(2,1)S(1)}, u32[]{:S(2)}, u32[]{:S(2)}) collective-permute-start(bf16[96,1024]{1,0:T(8,128)(2,1)S(1)} %hold.10.refs_0_), channel_id=1, source_target_pairs={{0,16},{8,24},{16,32},{24,40},{32,48},{40,56},{48,0},{56,8},{64,80... | collective-permute-start | bytes 589832 | tf_op jit(solution)/shard_map/cotangent_x/ppermute | solution.py:42
  55.3 5.7 %copy-start.7 = (bf16[512,1024]{1,0:T(8,128)(2,1)S(1)}, bf16[512,1024]{1,0:T(8,128)(2,1)}, u32[]{:S(2)}) copy-start(bf16[512,1024]{1,0:T(8,128)(2,1)} %refs_5_.2) | copy-start | bytes 3145732
  55.3 5.7 %collective-permute-start.17 = (bf16[384,1024]{1,0:T(8,128)(2,1)S(1)}, bf16[384,1024]{1,0:T(8,128)(2,1)S(1)}, u32[]{:S(2)}, u32[]{:S(2)}) collective-permute-start(bf16[384,1024]{1,0:T(8,128)(2,1)S(1)} %cat_x.3.mine), channel_id=1, source_target_pairs={{0,8},{8,0},{16,24},{24,16},{32,40},{40,32},{48,56},{56,48},{64,72... | collective-permute-start | bytes 2359304 | tf_op jit(solution)/shard_map/cotangent_core/ppermute | solution.py:47
  56.5 23.3 %collective-permute-start.16 = (bf16[192,1024]{1,0:T(8,128)(2,1)S(1)}, bf16[192,1024]{1,0:T(8,128)(2,1)S(1)}, u32[]{:S(2)}, u32[]{:S(2)}) collective-permute-start(bf16[192,1024]{1,0:T(8,128)(2,1)S(1)} %get-tuple-element.51), channel_id=1, source_target_pairs={{0,4},{1,5},{2,6},{3,7},{4,0},{5,1},{6,2},{7,3},{8,12},{9,13},{10,... | collective-permute-start | bytes 1179656 | tf_op jit(solution)/shard_map/gate_up_half/ppermute | solution.py:57
  62.5 17.3 %collective-permute-start.18 = (bf16[192,512]{1,0:T(8,128)(2,1)S(1)}, bf16[192,512]{1,0:T(8,128)(2,1)S(1)}, u32[]{:S(2)}, u32[]{:S(2)}) collective-permute-start(bf16[192,512]{1,0:T(8,128)(2,1)S(1)} %get-tuple-element.52), channel_id=1, source_target_pairs={{0,1},{1,2},{2,3},{3,0},{4,5},{5,6},{6,7},{7,4},{8,9},{9,10},{10,1... | collective-permute-start | bytes 589832 | tf_op jit(solution)/shard_map/hidden_grad_y/ppermute | solution.py:52
  63.6 16.1 %collective-permute-start.19 = (bf16[192,512]{1,0:T(8,128)(2,1)S(1)}, bf16[192,512]{1,0:T(8,128)(2,1)S(1)}, u32[]{:S(2)}, u32[]{:S(2)}) collective-permute-start(bf16[192,512]{1,0:T(8,128)(2,1)S(1)} %get-tuple-element.53), channel_id=1, source_target_pairs={{0,2},{1,3},{2,0},{3,1},{4,6},{5,7},{6,4},{7,5},{8,10},{9,11},{10,... | collective-permute-start | bytes 589832 | tf_op jit(solution)/shard_map/hidden_grad_y/ppermute | solution.py:52
  66.1 13.7 %collective-permute-start.20 = (bf16[192,512]{1,0:T(8,128)(2,1)S(1)}, bf16[192,512]{1,0:T(8,128)(2,1)S(1)}, u32[]{:S(2)}, u32[]{:S(2)}) collective-permute-start(bf16[192,512]{1,0:T(8,128)(2,1)S(1)} %get-tuple-element.54), channel_id=1, source_target_pairs={{0,3},{1,0},{2,1},{3,2},{4,7},{5,4},{6,5},{7,6},{8,11},{9,8},{10,9... | collective-permute-start | bytes 589832 | tf_op jit(solution)/shard_map/hidden_grad_y/ppermute | solution.py:52
  79.9 13.1 %collective-permute-start.24 = (bf16[192,512]{1,0:T(8,128)(2,1)S(1)}, bf16[192,512]{1,0:T(8,128)(2,1)S(1)}, u32[]{:S(2)}, u32[]{:S(2)}) collective-permute-start(bf16[192,512]{1,0:T(8,128)(2,1)S(1)} %get-tuple-element.56), channel_id=1, source_target_pairs={{0,4},{1,5},{2,6},{3,7},{4,0},{5,1},{6,2},{7,3},{8,12},{9,13},{10,... | collective-permute-start | bytes 589832 | tf_op jit(solution)/shard_map/hidden_grad_half/ppermute | solution.py:57
  84.5 8.5 %collective-permute-start.23 = (bf16[192,512]{1,0:T(8,128)(2,1)S(1)}, bf16[192,512]{1,0:T(8,128)(2,1)S(1)}, u32[]{:S(2)}, u32[]{:S(2)}) collective-permute-start(bf16[192,512]{1,0:T(8,128)(2,1)S(1)} %hidden.1.refs_1_), channel_id=1, source_target_pairs={{0,3},{1,0},{2,1},{3,2},{4,7},{5,4},{6,5},{7,6},{8,11},{9,8},{10,9... | collective-permute-start | bytes 589832 | tf_op jit(solution)/shard_map/hidden_y/ppermute | solution.py:52
  86.9 6.9 %collective-permute-start.22 = (bf16[192,512]{1,0:T(8,128)(2,1)S(1)}, bf16[192,512]{1,0:T(8,128)(2,1)S(1)}, u32[]{:S(2)}, u32[]{:S(2)}) collective-permute-start(bf16[192,512]{1,0:T(8,128)(2,1)S(1)} %hidden.1.refs_1_), channel_id=1, source_target_pairs={{0,2},{1,3},{2,0},{3,1},{4,6},{5,7},{6,4},{7,5},{8,10},{9,11},{10,... | collective-permute-start | bytes 589832 | tf_op jit(solution)/shard_map/hidden_y/ppermute | solution.py:52
  87.4 12.0 %collective-permute-start.21 = (bf16[192,512]{1,0:T(8,128)(2,1)S(1)}, bf16[192,512]{1,0:T(8,128)(2,1)S(1)}, u32[]{:S(2)}, u32[]{:S(2)}) collective-permute-start(bf16[192,512]{1,0:T(8,128)(2,1)S(1)} %hidden.1.refs_1_), channel_id=1, source_target_pairs={{0,1},{1,2},{2,3},{3,0},{4,5},{5,6},{6,7},{7,4},{8,9},{9,10},{10,1... | collective-permute-start | bytes 589832 | tf_op jit(solution)/shard_map/hidden_y/ppermute | solution.py:52
  100.5 3.6 %collective-permute-start.25 = (f32[384,1024]{1,0:T(8,128)S(1)}, f32[384,1024]{1,0:T(8,128)S(1)}, u32[]{:S(2)}, u32[]{:S(2)}) collective-permute-start(f32[384,1024]{1,0:T(8,128)S(1)} %get-tuple-element.58), channel_id=1, source_target_pairs={{0,8},{8,0},{16,24},{24,16},{32,40},{40,32},{48,56},{56,48},{64,72... | collective-permute-start | bytes 4718600 | tf_op jit(solution)/shard_map/output_core/ppermute | solution.py:47
  101.3 10.8 %collective-permute-start.31 = (bf16[192,1024]{1,0:T(8,128)(2,1)S(1)}, bf16[192,1024]{1,0:T(8,128)(2,1)S(1)}, u32[]{:S(2)}, u32[]{:S(2)}) collective-permute-start(bf16[192,1024]{1,0:T(8,128)(2,1)S(1)} %grads.1.refs_1_), channel_id=1, source_target_pairs={{0,3},{1,0},{2,1},{3,2},{4,7},{5,4},{6,5},{7,6},{8,11},{9,8},{10,9... | collective-permute-start | bytes 1179656 | tf_op jit(solution)/shard_map/grads_y/ppermute | solution.py:52
  101.7 12.0 %collective-permute-start.30 = (bf16[192,1024]{1,0:T(8,128)(2,1)S(1)}, bf16[192,1024]{1,0:T(8,128)(2,1)S(1)}, u32[]{:S(2)}, u32[]{:S(2)}) collective-permute-start(bf16[192,1024]{1,0:T(8,128)(2,1)S(1)} %grads.1.refs_1_), channel_id=1, source_target_pairs={{0,2},{1,3},{2,0},{3,1},{4,6},{5,7},{6,4},{7,5},{8,10},{9,11},{10,... | collective-permute-start | bytes 1179656 | tf_op jit(solution)/shard_map/grads_y/ppermute | solution.py:52
  102.2 20.5 %collective-permute-start.29 = (bf16[192,1024]{1,0:T(8,128)(2,1)S(1)}, bf16[192,1024]{1,0:T(8,128)(2,1)S(1)}, u32[]{:S(2)}, u32[]{:S(2)}) collective-permute-start(bf16[192,1024]{1,0:T(8,128)(2,1)S(1)} %grads.1.refs_1_), channel_id=1, source_target_pairs={{0,1},{1,2},{2,3},{3,0},{4,5},{5,6},{6,7},{7,4},{8,9},{9,10},{10,1... | collective-permute-start | bytes 1179656 | tf_op jit(solution)/shard_map/grads_y/ppermute | solution.py:52
  104.2 18.5 %collective-permute-start.26 = (bf16[96,1024]{1,0:T(8,128)(2,1)S(1)}, bf16[96,1024]{1,0:T(8,128)(2,1)S(1)}, u32[]{:S(2)}, u32[]{:S(2)}) collective-permute-start(bf16[96,1024]{1,0:T(8,128)(2,1)S(1)} %get-tuple-element.60), channel_id=1, source_target_pairs={{0,48},{8,56},{16,0},{24,8},{32,16},{40,24},{48,32},{56,40},{64,11... | collective-permute-start | bytes 589832 | tf_op jit(solution)/shard_map/output_x/ppermute | solution.py:42
  105.0 17.7 %collective-permute-start.27 = (bf16[96,1024]{1,0:T(8,128)(2,1)S(1)}, bf16[96,1024]{1,0:T(8,128)(2,1)S(1)}, u32[]{:S(2)}, u32[]{:S(2)}) collective-permute-start(bf16[96,1024]{1,0:T(8,128)(2,1)S(1)} %get-tuple-element.61), channel_id=1, source_target_pairs={{0,32},{8,40},{16,48},{24,56},{32,0},{40,8},{48,16},{56,24},{64,96... | collective-permute-start | bytes 589832 | tf_op jit(solution)/shard_map/output_x/ppermute | solution.py:42
  112.1 10.6 %collective-permute-start.28 = (bf16[96,1024]{1,0:T(8,128)(2,1)S(1)}, bf16[96,1024]{1,0:T(8,128)(2,1)S(1)}, u32[]{:S(2)}, u32[]{:S(2)}) collective-permute-start(bf16[96,1024]{1,0:T(8,128)(2,1)S(1)} %get-tuple-element.62), channel_id=1, source_target_pairs={{0,16},{8,24},{16,32},{24,40},{32,48},{40,56},{48,0},{56,8},{64,80... | collective-permute-start | bytes 589832 | tf_op jit(solution)/shard_map/output_x/ppermute | solution.py:42
  123.8 3.6 %collective-permute-start.32 = (f32[384,1024]{1,0:T(8,128)S(1)}, f32[384,1024]{1,0:T(8,128)S(1)}, u32[]{:S(2)}, u32[]{:S(2)}) collective-permute-start(f32[384,1024]{1,0:T(8,128)S(1)} %get-tuple-element.70.refs_1_), channel_id=1, source_target_pairs={{0,8},{8,0},{16,24},{24,16},{32,40},{40,32},{48,56},{56,48},{64,72... | collective-permute-start | bytes 4718600 | tf_op jit(solution)/shard_map/token_grad_core/ppermute | solution.py:47
  127.1 1.0 copy-start.4
  128.1 8.0 %collective-permute-start.33 = (bf16[96,1024]{1,0:T(8,128)(2,1)S(1)}, bf16[96,1024]{1,0:T(8,128)(2,1)S(1)}, u32[]{:S(2)}, u32[]{:S(2)}) collective-permute-start(bf16[96,1024]{1,0:T(8,128)(2,1)S(1)} %get-tuple-element.73), channel_id=1, source_target_pairs={{0,32},{8,40},{16,48},{24,56},{32,0},{40,8},{48,16},{56,24},{64,96... | collective-permute-start | bytes 589832 | tf_op jit(solution)/shard_map/token_grad_x/ppermute | solution.py:42
  128.1 11.8 %collective-permute-start.37 = (bf16[96,1024]{1,0:T(8,128)(2,1)S(1)}, bf16[96,1024]{1,0:T(8,128)(2,1)S(1)}, u32[]{:S(2)}, u32[]{:S(2)}) collective-permute-start(bf16[96,1024]{1,0:T(8,128)(2,1)S(1)} %get-tuple-element.78), channel_id=1, source_target_pairs={{0,48},{8,56},{16,0},{24,8},{32,16},{40,24},{48,32},{56,40},{64,11... | collective-permute-start | bytes 589832 | tf_op jit(solution)/shard_map/token_grad_x/ppermute | solution.py:42
  131.6 8.8 %collective-permute-start.38 = (bf16[96,1024]{1,0:T(8,128)(2,1)S(1)}, bf16[96,1024]{1,0:T(8,128)(2,1)S(1)}, u32[]{:S(2)}, u32[]{:S(2)}) collective-permute-start(bf16[96,1024]{1,0:T(8,128)(2,1)S(1)} %get-tuple-element.79), channel_id=1, source_target_pairs={{0,16},{8,24},{16,32},{24,40},{32,48},{40,56},{48,0},{56,8},{64,80... | collective-permute-start | bytes 589832 | tf_op jit(solution)/shard_map/token_grad_x/ppermute | solution.py:42
  136.1 7.8 %collective-permute-start.34 = (bf16[24,1024]{1,0:T(8,128)(2,1)S(1)}, bf16[24,1024]{1,0:T(8,128)(2,1)S(1)}, u32[]{:S(2)}, u32[]{:S(2)}) collective-permute-start(bf16[24,1024]{1,0:T(8,128)(2,1)S(1)} %get-tuple-element.74), channel_id=1, source_target_pairs={{0,192},{8,200},{16,208},{24,216},{32,224},{40,232},{48,240},{56,2... | collective-permute-start | bytes 147464 | tf_op jit(solution)/shard_map/output_z/ppermute | solution.py:37
  136.2 4.3 %collective-permute-start.35 = (bf16[24,1024]{1,0:T(8,128)(2,1)S(1)}, bf16[24,1024]{1,0:T(8,128)(2,1)S(1)}, u32[]{:S(2)}, u32[]{:S(2)}) collective-permute-start(bf16[24,1024]{1,0:T(8,128)(2,1)S(1)} %get-tuple-element.75), channel_id=1, source_target_pairs={{0,128},{8,136},{16,144},{24,152},{32,160},{40,168},{48,176},{56,1... | collective-permute-start | bytes 147464 | tf_op jit(solution)/shard_map/output_z/ppermute | solution.py:37
  136.3 7.6 %collective-permute-start.36 = (bf16[24,1024]{1,0:T(8,128)(2,1)S(1)}, bf16[24,1024]{1,0:T(8,128)(2,1)S(1)}, u32[]{:S(2)}, u32[]{:S(2)}) collective-permute-start(bf16[24,1024]{1,0:T(8,128)(2,1)S(1)} %get-tuple-element.76), channel_id=1, source_target_pairs={{0,64},{8,72},{16,80},{24,88},{32,96},{40,104},{48,112},{56,120},{... | collective-permute-start | bytes 147464 | tf_op jit(solution)/shard_map/output_z/ppermute | solution.py:37
  138.8 1.7 %copy-start.2 = (bf16[1024,512]{1,0:T(8,128)(2,1)}, bf16[1024,512]{1,0:T(8,128)(2,1)S(1)}, u32[]{:S(2)}) copy-start(bf16[1024,512]{1,0:T(8,128)(2,1)S(1)} %convolution_convert_fusion.1.refs_4_) | copy-start | bytes 3145732
  139.8 4.7 %copy-start.3 = (bf16[1024,512]{1,0:T(8,128)(2,1)}, bf16[1024,512]{1,0:T(8,128)(2,1)S(1)}, u32[]{:S(2)}) copy-start(bf16[1024,512]{1,0:T(8,128)(2,1)S(1)} %convolution_convert_fusion.refs_5_) | copy-start | bytes 3145732
  140.6 4.0 %collective-permute-start.39 = (bf16[24,1024]{1,0:T(8,128)(2,1)S(1)}, bf16[24,1024]{1,0:T(8,128)(2,1)S(1)}, u32[]{:S(2)}, u32[]{:S(2)}) collective-permute-start(bf16[24,1024]{1,0:T(8,128)(2,1)S(1)} %get-tuple-element.84), channel_id=1, source_target_pairs={{0,192},{8,200},{16,208},{24,216},{32,224},{40,232},{48,240},{56,2... | collective-permute-start | bytes 147464 | tf_op jit(solution)/shard_map/token_grad_z/ppermute | solution.py:37
  142.5 3.9 %collective-permute-start.40 = (bf16[24,1024]{1,0:T(8,128)(2,1)S(1)}, bf16[24,1024]{1,0:T(8,128)(2,1)S(1)}, u32[]{:S(2)}, u32[]{:S(2)}) collective-permute-start(bf16[24,1024]{1,0:T(8,128)(2,1)S(1)} %get-tuple-element.85), channel_id=1, source_target_pairs={{0,128},{8,136},{16,144},{24,152},{32,160},{40,168},{48,176},{56,1... | collective-permute-start | bytes 147464 | tf_op jit(solution)/shard_map/token_grad_z/ppermute | solution.py:37
  142.8 5.2 %collective-permute-start.41 = (bf16[24,1024]{1,0:T(8,128)(2,1)S(1)}, bf16[24,1024]{1,0:T(8,128)(2,1)S(1)}, u32[]{:S(2)}, u32[]{:S(2)}) collective-permute-start(bf16[24,1024]{1,0:T(8,128)(2,1)S(1)} %get-tuple-element.86), channel_id=1, source_target_pairs={{0,64},{8,72},{16,80},{24,88},{32,96},{40,104},{48,112},{56,120},{... | collective-permute-start | bytes 147464 | tf_op jit(solution)/shard_map/token_grad_z/ppermute | solution.py:37

commit v3 on v2

--- a/solution.py
+++ b/solution.py
@@ -314,17 +314,17 @@
 
     gh2 = send_half(part, "hidden_grad_half")
     got = all_y([hidden] * 3, "hidden_y")
+    grads = call(
+        grads_kernel, [((n, 2 * f), BF)], [gate_up, gate_up2, gh, gh2], after=got
+    )[0]
     all_hidden, own_out, their_out = call(
         out_kernel,
         [((Y * n, f), BF), ((half, d), F32), ((half, d), OUT_CORE)],
         [hidden, *got, down_weight],
         flops,
         y,
-        after=[gh2],
-    )
-    grads = call(
-        grads_kernel, [((n, 2 * f), BF)], [gate_up, gate_up2, gh, gh2], after=got
-    )[0]
+        after=[gh2, grads],
+    )
 
     got = all_y([grads] * 3, "grads_y")
     s1, s2, s3, own_out = first_row(own_out, send_core(their_out, "output_core"))

time: 151 us -> 149 us (0.987)
  waiting for transfers between devices: 75.2 us -> 53.3 us
  starting transfers between devices: 56.2 us -> 76.4 us
    ppermute x2, waiting for transfers between devices: 17.6 us -> 8.7 us  [send_half(): return lax.ppermute(a, 'col', col_perm(lambda h, y: (h + 1, y)))]
    ppermute x12, waiting for transfers between devices: 20 us -> 12.2 us  [send_x(): return lax.ppermute(a, 'row', row_perm(lambda z, x, c: (z, x + k, c)))]
    ppermute x12, starting transfers between devices: 11.9 us -> 18.3 us  [send_x(): return lax.ppermute(a, 'row', row_perm(lambda z, x, c: (z, x + k, c)))]
    ppermute x12, starting transfers between devices: 14.1 us -> 19.9 us  [send_y(): return lax.ppermute(a, 'col', col_perm(lambda h, y: (h, y + k)))]
    ppermute x12, waiting for transfers between devices: 25.3 us -> 20.2 us  [send_y(): return lax.ppermute(a, 'col', col_perm(lambda h, y: (h, y + k)))]
    ppermute x4, starting transfers between devices: 3.56 us -> 8.18 us  [send_core(): return lax.ppermute(a, 'row', row_perm(lambda z, x, c: (z, x, c + 1)))]
    ppermute x12, starting transfers between devices: 17.7 us -> 20.8 us  [send_z(): return lax.ppermute(a, 'row', row_perm(lambda z, x, c: (z + k, x, c)))]
  transfers between devices with their start and end apart: 42 -> 42, of which waited for: 24 -> 21; matrix products, arithmetic and copies ran while one was open for 2% -> 2% of each run, Pallas kernels for 3% -> 3%
where the time goes in v3:
time: 149 us; the launch traced here: 147 us
  starting transfers between devices  76.4 us (51%)
  waiting for transfers between devices  53.3 us (36%)
  Pallas kernels  11.2 us (8%)
  matrix products  3.09 us (2%)
  local copies, waits for them, and re-layouts  2.13 us (1%)
    ppermute x12, starting transfers between devices, send_z(): return lax.ppermute(a, 'row', row_perm(lambda z, x, c: (z + k, x, c)))  20.8 us
    ppermute x12, waiting for transfers between devices, send_y(): return lax.ppermute(a, 'col', col_perm(lambda h, y: (h, y + k)))  20.2 us
    ppermute x12, starting transfers between devices, send_y(): return lax.ppermute(a, 'col', col_perm(lambda h, y: (h, y + k)))  19.9 us
    ppermute x12, starting transfers between devices, send_x(): return lax.ppermute(a, 'row', row_perm(lambda z, x, c: (z, x + k, c)))  18.3 us
    ppermute x12, waiting for transfers between devices, send_x(): return lax.ppermute(a, 'row', row_perm(lambda z, x, c: (z, x + k, c)))  12.2 us
    ppermute x12, waiting for transfers between devices, send_z(): return lax.ppermute(a, 'row', row_perm(lambda z, x, c: (z + k, x, c)))  12 us
    pallas_call x26, Pallas kernels, call(): pl.pallas_call(body, name=kernel.__name__.removesuffix('_kernel'), out_sh...  11.2 us
    ppermute x2, starting transfers between devices, send_half(): return lax.ppermute(a, 'col', col_perm(lambda h, y: (h + 1, y)))  9.14 us
  transfers between devices with their start and end apart: 42, of which 21 were waited for; matrix products, arithmetic and copies ran while one was open for 2% of the time, Pallas kernels for 3%

profile of v3, /device:TPU:1, one launch (start us, length us, event | category | flops | bytes accessed | tf_op | source)
XLA Modules:
  0.0 147.0 jit_solution(13139741356599989410)
XLA Ops:
  0.7 2.5 %collective-permute-start = (bf16[24,1024]{1,0:T(8,128)(2,1)}, bf16[24,1024]{1,0:T(8,128)(2,1)S(1)}, u32[]{:S(2)}, u32[]{:S(2)}) collective-permute-start(bf16[24,1024]{1,0:T(8,128)(2,1)} %refs_0_.2), channel_id=1, source_target_pairs={{0,64},{8,72},{16,80},{24,88},{32,96},{40,104},{48,112},{56,120},{... | collective-permute-start | bytes 147464 | tf_op jit(solution)/shard_map/tokens_z/ppermute | solution.py:37
  3.2 3.0 %collective-permute-start.1 = (bf16[24,1024]{1,0:T(8,128)(2,1)}, bf16[24,1024]{1,0:T(8,128)(2,1)S(1)}, u32[]{:S(2)}, u32[]{:S(2)}) collective-permute-start(bf16[24,1024]{1,0:T(8,128)(2,1)} %refs_0_.2), channel_id=1, source_target_pairs={{0,128},{8,136},{16,144},{24,152},{32,160},{40,168},{48,176},{56,1... | collective-permute-start | bytes 147464 | tf_op jit(solution)/shard_map/tokens_z/ppermute | solution.py:37
  6.2 0.7 collective-permute-start.2
  6.9 0.8 copy-done.6
  8.1 2.2 %collective-permute-done.2.d = bf16[24,1024]{1,0:T(8,128)(2,1)S(1)} collective-permute-done((bf16[24,1024]{1,0:T(8,128)(2,1)}, bf16[24,1024]{1,0:T(8,128)(2,1)S(1)}, u32[]{:S(2)}, u32[]{:S(2)}) %collective-permute-start.2) | collective-permute-done | bytes 49184 | tf_op jit(solution)/shard_map/tokens_z/ppermute | solution.py:37
  10.3 1.1 collective-permute-start.3
  11.5 2.5 %collective-permute-start.4 = (bf16[96,1024]{1,0:T(8,128)(2,1)S(1)}, bf16[96,1024]{1,0:T(8,128)(2,1)S(1)}, u32[]{:S(2)}, u32[]{:S(2)}) collective-permute-start(bf16[96,1024]{1,0:T(8,128)(2,1)S(1)} %cat_z.2.refs_1_.refs_0_), channel_id=1, source_target_pairs={{0,32},{8,40},{16,48},{24,56},{32,0},{40,8},{48,16},{56,24},{64,96... | collective-permute-start | bytes 589832 | tf_op jit(solution)/shard_map/tokens_x/ppermute | solution.py:42
  13.9 1.2 collective-permute-start.5
  15.1 0.8 copy-done.5
  15.9 1.4 collective-permute-start.6
  17.9 2.7 %collective-permute-done.6.refs_4_.b = bf16[24,1024]{1,0:T(8,128)(2,1)S(1)} collective-permute-done((bf16[24,1024]{1,0:T(8,128)(2,1)S(1)}, bf16[24,1024]{1,0:T(8,128)(2,1)S(1)}, u32[]{:S(2)}, u32[]{:S(2)}) %collective-permute-start.6) | collective-permute-done | bytes 49184 | tf_op jit(solution)/shard_map/cotangent_z/ppermute | solution.py:37
  20.6 1.3 collective-permute-done.7.refs_5_.c
  22.0 3.3 %collective-permute-start.8 = (bf16[384,1024]{1,0:T(8,128)(2,1)S(1)}, bf16[384,1024]{1,0:T(8,128)(2,1)}, u32[]{:S(2)}, u32[]{:S(2)}) collective-permute-start(bf16[384,1024]{1,0:T(8,128)(2,1)S(1)} %cat_x.2.mine), channel_id=1, source_target_pairs={{0,8},{8,0},{16,24},{24,16},{32,40},{40,32},{48,56},{56,48},{64,72... | collective-permute-start | bytes 2359304 | tf_op jit(solution)/shard_map/tokens_core/ppermute | solution.py:47
  25.3 1.7 %collective-permute-start.12 = (bf16[24,1024]{1,0:T(8,128)(2,1)S(1)}, bf16[24,1024]{1,0:T(8,128)(2,1)S(1)}, u32[]{:S(2)}, u32[]{:S(2)}) collective-permute-start(bf16[24,1024]{1,0:T(8,128)(2,1)S(1)} %hold.8.refs_0_), channel_id=1, source_target_pairs={{0,192},{8,200},{16,208},{24,216},{32,224},{40,232},{48,240},{56,2... | collective-permute-start | bytes 147464 | tf_op jit(solution)/shard_map/cotangent_z/ppermute | solution.py:37
  27.0 1.2 collective-permute-done.12.d
  28.3 3.1 %up.1 = (bf16[768,1024]{1,0:T(8,128)(2,1)S(1)}, bf16[192,1024]{1,0:T(8,128)(2,1)S(1)}, bf16[192,1024]{1,0:T(8,128)(2,1)S(1)}, bf16[192,1024]{1,0:T(8,128)(2,1)S(1)}, f32[192,1024]{1,0:T(8,128)S(1)}) custom-call(s32[1]{0:T(128)} %bitcast.y.refs_0_, bf16[384,1024]{1,0:T(8,128)(2,1)S(1)} %cat_x.2.mine, bf16[384,1024]{1,0:T(8,128)(2,1)} %collective-permute-done.8.theirs, ...), custom_call_target="tpu_custom_call" | custom-call | flops 1610612736 | bytes 7208960 | tf_op jit(solution)/shard_map/up/pallas_call | solution.py:84
  31.4 1.4 collective-permute-start.9
  33.2 3.1 %collective-permute-start.10 = (bf16[192,1024]{1,0:T(8,128)(2,1)S(1)}, bf16[192,1024]{1,0:T(8,128)(2,1)S(1)}, u32[]{:S(2)}, u32[]{:S(2)}) collective-permute-start(bf16[192,1024]{1,0:T(8,128)(2,1)S(1)} %get-tuple-element.48), channel_id=1, source_target_pairs={{0,2},{1,3},{2,0},{3,1},{4,6},{5,7},{6,4},{7,5},{8,10},{9,11},{10,... | collective-permute-start | bytes 1179656 | tf_op jit(solution)/shard_map/gate_up_y/ppermute | solution.py:52
  36.3 1.1 collective-permute-start.11
  37.3 1.2 collective-permute-start.14
  39.0 0.9 collective-permute-start.15
  39.8 3.5 %collective-permute-done.14.refs_5_.refs_2_ = bf16[96,1024]{1,0:T(8,128)(2,1)S(1)} collective-permute-done((bf16[96,1024]{1,0:T(8,128)(2,1)S(1)}, bf16[96,1024]{1,0:T(8,128)(2,1)S(1)}, u32[]{:S(2)}, u32[]{:S(2)}) %collective-permute-start.14) | collective-permute-done | bytes 196640 | tf_op jit(solution)/shard_map/cotangent_x/ppermute | solution.py:42
  43.4 4.4 %collective-permute-done.15.refs_6_.refs_3_ = bf16[96,1024]{1,0:T(8,128)(2,1)S(1)} collective-permute-done((bf16[96,1024]{1,0:T(8,128)(2,1)S(1)}, bf16[96,1024]{1,0:T(8,128)(2,1)S(1)}, u32[]{:S(2)}, u32[]{:S(2)}) %collective-permute-start.15) | collective-permute-done | bytes 196640 | tf_op jit(solution)/shard_map/cotangent_x/ppermute | solution.py:42
  47.8 4.7 %collective-permute-done.10.refs_2_.refs_5_ = bf16[192,1024]{1,0:T(8,128)(2,1)S(1)} collective-permute-done((bf16[192,1024]{1,0:T(8,128)(2,1)S(1)}, bf16[192,1024]{1,0:T(8,128)(2,1)S(1)}, u32[]{:S(2)}, u32[]{:S(2)}) %collective-permute-start.10) | collective-permute-done | bytes 393248 | tf_op jit(solution)/shard_map/gate_up_y/ppermute | solution.py:52
  52.7 1.8 %collective-permute-start.17 = (bf16[384,1024]{1,0:T(8,128)(2,1)S(1)}, bf16[384,1024]{1,0:T(8,128)(2,1)S(1)}, u32[]{:S(2)}, u32[]{:S(2)}) collective-permute-start(bf16[384,1024]{1,0:T(8,128)(2,1)S(1)} %cat_x.3.mine), channel_id=1, source_target_pairs={{0,8},{8,0},{16,24},{24,16},{32,40},{40,32},{48,56},{56,48},{64,72... | collective-permute-start | bytes 2359304 | tf_op jit(solution)/shard_map/cotangent_core/ppermute | solution.py:47
  54.7 5.2 %collective-permute-start.16 = (bf16[192,1024]{1,0:T(8,128)(2,1)S(1)}, bf16[192,1024]{1,0:T(8,128)(2,1)S(1)}, u32[]{:S(2)}, u32[]{:S(2)}) collective-permute-start(bf16[192,1024]{1,0:T(8,128)(2,1)S(1)} %get-tuple-element.51), channel_id=1, source_target_pairs={{0,4},{1,5},{2,6},{3,7},{4,0},{5,1},{6,2},{7,3},{8,12},{9,13},{10,... | collective-permute-start | bytes 1179656 | tf_op jit(solution)/shard_map/gate_up_half/ppermute | solution.py:57
  60.0 1.5 %back.1 = (bf16[768,1024]{1,0:T(8,128)(2,1)S(1)}, bf16[192,512]{1,0:T(8,128)(2,1)S(1)}, bf16[192,512]{1,0:T(8,128)(2,1)S(1)}, bf16[192,512]{1,0:T(8,128)(2,1)S(1)}, f32[192,512]{1,0:T(8,128)S(1)}) custom-call(s32[1]{0:T(128)} %bitcast.y.refs_0_, bf16[384,1024]{1,0:T(8,128)(2,1)S(1)} %cat_x.3.mine, bf16[384,1024]{1,0:T(8,128)(2,1)S(1)} %collective-permute-done.17.theirs, ...), custom_call_target="tpu_custom_call" | custom-call | flops 805306368 | bytes 5177344 | tf_op jit(solution)/shard_map/back/pallas_call | solution.py:84
  61.5 1.4 collective-permute-start.18
  62.9 2.1 %collective-permute-start.19 = (bf16[192,512]{1,0:T(8,128)(2,1)S(1)}, bf16[192,512]{1,0:T(8,128)(2,1)S(1)}, u32[]{:S(2)}, u32[]{:S(2)}) collective-permute-start(bf16[192,512]{1,0:T(8,128)(2,1)S(1)} %get-tuple-element.53), channel_id=1, source_target_pairs={{0,2},{1,3},{2,0},{3,1},{4,6},{5,7},{6,4},{7,5},{8,10},{9,11},{10,... | collective-permute-start | bytes 589832 | tf_op jit(solution)/shard_map/hidden_grad_y/ppermute | solution.py:52
  65.0 1.4 collective-permute-start.20
  66.4 6.0 %collective-permute-done.16.refs_1_.refs_4_ = bf16[192,1024]{1,0:T(8,128)(2,1)S(1)} collective-permute-done((bf16[192,1024]{1,0:T(8,128)(2,1)S(1)}, bf16[192,1024]{1,0:T(8,128)(2,1)S(1)}, u32[]{:S(2)}, u32[]{:S(2)}) %collective-permute-start.16) | collective-permute-done | bytes 393248 | tf_op jit(solution)/shard_map/gate_up_half/ppermute | solution.py:57
  72.4 1.5 %collective-permute-done.19.refs_3_.refs_2_ = bf16[192,512]{1,0:T(8,128)(2,1)S(1)} collective-permute-done((bf16[192,512]{1,0:T(8,128)(2,1)S(1)}, bf16[192,512]{1,0:T(8,128)(2,1)S(1)}, u32[]{:S(2)}, u32[]{:S(2)}) %collective-permute-start.19) | collective-permute-done | bytes 196640 | tf_op jit(solution)/shard_map/hidden_grad_y/ppermute | solution.py:52
  74.0 3.9 %collective-permute-start.24 = (bf16[192,512]{1,0:T(8,128)(2,1)S(1)}, bf16[192,512]{1,0:T(8,128)(2,1)S(1)}, u32[]{:S(2)}, u32[]{:S(2)}) collective-permute-start(bf16[192,512]{1,0:T(8,128)(2,1)S(1)} %get-tuple-element.56), channel_id=1, source_target_pairs={{0,4},{1,5},{2,6},{3,7},{4,0},{5,1},{6,2},{7,3},{8,12},{9,13},{10,... | collective-permute-start | bytes 589832 | tf_op jit(solution)/shard_map/hidden_grad_half/ppermute | solution.py:57
  78.1 1.4 collective-permute-start.21
  79.4 2.1 %collective-permute-start.22 = (bf16[192,512]{1,0:T(8,128)(2,1)S(1)}, bf16[192,512]{1,0:T(8,128)(2,1)S(1)}, u32[]{:S(2)}, u32[]{:S(2)}) collective-permute-start(bf16[192,512]{1,0:T(8,128)(2,1)S(1)} %hidden.1.refs_1_), channel_id=1, source_target_pairs={{0,2},{1,3},{2,0},{3,1},{4,6},{5,7},{6,4},{7,5},{8,10},{9,11},{10,... | collective-permute-start | bytes 589832 | tf_op jit(solution)/shard_map/hidden_y/ppermute | solution.py:52
  81.6 1.4 collective-permute-start.23
  82.9 2.7 %collective-permute-done.24.refs_3_.refs_6_ = bf16[192,512]{1,0:T(8,128)(2,1)S(1)} collective-permute-done((bf16[192,512]{1,0:T(8,128)(2,1)S(1)}, bf16[192,512]{1,0:T(8,128)(2,1)S(1)}, u32[]{:S(2)}, u32[]{:S(2)}) %collective-permute-start.24) | collective-permute-done | bytes 196640 | tf_op jit(solution)/shard_map/hidden_grad_half/ppermute | solution.py:57
  85.6 3.9 %collective-permute-done.22.refs_5_.refs_3_ = bf16[192,512]{1,0:T(8,128)(2,1)S(1)} collective-permute-done((bf16[192,512]{1,0:T(8,128)(2,1)S(1)}, bf16[192,512]{1,0:T(8,128)(2,1)S(1)}, u32[]{:S(2)}, u32[]{:S(2)}) %collective-permute-start.22) | collective-permute-done | bytes 196640 | tf_op jit(solution)/shard_map/hidden_y/ppermute | solution.py:52
  89.8 1.0 out.1
  90.8 2.2 %collective-permute-start.25 = (f32[384,1024]{1,0:T(8,128)S(1)}, f32[384,1024]{1,0:T(8,128)S(1)}, u32[]{:S(2)}, u32[]{:S(2)}) collective-permute-start(f32[384,1024]{1,0:T(8,128)S(1)} %get-tuple-element.59), channel_id=1, source_target_pairs={{0,8},{8,0},{16,24},{24,16},{32,40},{40,32},{48,56},{56,48},{64,72... | collective-permute-start | bytes 4718600 | tf_op jit(solution)/shard_map/output_core/ppermute | solution.py:47
  93.0 1.3 collective-permute-start.29
  94.3 2.1 %collective-permute-start.30 = (bf16[192,1024]{1,0:T(8,128)(2,1)S(1)}, bf16[192,1024]{1,0:T(8,128)(2,1)S(1)}, u32[]{:S(2)}, u32[]{:S(2)}) collective-permute-start(bf16[192,1024]{1,0:T(8,128)(2,1)S(1)} %grads.1.refs_7_.refs_1_), channel_id=1, source_target_pairs={{0,2},{1,3},{2,0},{3,1},{4,6},{5,7},{6,4},{7,5},{8,10},{9,11},{10,... | collective-permute-start | bytes 1179656 | tf_op jit(solution)/shard_map/grads_y/ppermute | solution.py:52
  96.4 1.3 collective-permute-start.31
  97.8 2.7 %collective-permute-start.26 = (bf16[96,1024]{1,0:T(8,128)(2,1)S(1)}, bf16[96,1024]{1,0:T(8,128)(2,1)S(1)}, u32[]{:S(2)}, u32[]{:S(2)}) collective-permute-start(bf16[96,1024]{1,0:T(8,128)(2,1)S(1)} %get-tuple-element.61), channel_id=1, source_target_pairs={{0,48},{8,56},{16,0},{24,8},{32,16},{40,24},{48,32},{56,40},{64,11... | collective-permute-start | bytes 589832 | tf_op jit(solution)/shard_map/output_x/ppermute | solution.py:42
  100.5 1.6 %collective-permute-start.27 = (bf16[96,1024]{1,0:T(8,128)(2,1)S(1)}, bf16[96,1024]{1,0:T(8,128)(2,1)S(1)}, u32[]{:S(2)}, u32[]{:S(2)}) collective-permute-start(bf16[96,1024]{1,0:T(8,128)(2,1)S(1)} %get-tuple-element.62), channel_id=1, source_target_pairs={{0,32},{8,40},{16,48},{24,56},{32,0},{40,8},{48,16},{56,24},{64,96... | collective-permute-start | bytes 589832 | tf_op jit(solution)/shard_map/output_x/ppermute | solution.py:42
  102.1 2.7 %collective-permute-done.29.refs_2_ = bf16[192,1024]{1,0:T(8,128)(2,1)S(1)} collective-permute-done((bf16[192,1024]{1,0:T(8,128)(2,1)S(1)}, bf16[192,1024]{1,0:T(8,128)(2,1)S(1)}, u32[]{:S(2)}, u32[]{:S(2)}) %collective-permute-start.29) | collective-permute-done | bytes 393248 | tf_op jit(solution)/shard_map/grads_y/ppermute | solution.py:52
  104.9 2.0 %collective-permute-start.28 = (bf16[96,1024]{1,0:T(8,128)(2,1)S(1)}, bf16[96,1024]{1,0:T(8,128)(2,1)S(1)}, u32[]{:S(2)}, u32[]{:S(2)}) collective-permute-start(bf16[96,1024]{1,0:T(8,128)(2,1)S(1)} %get-tuple-element.63), channel_id=1, source_target_pairs={{0,16},{8,24},{16,32},{24,40},{32,48},{40,56},{48,0},{56,8},{64,80... | collective-permute-start | bytes 589832 | tf_op jit(solution)/shard_map/output_x/ppermute | solution.py:42
  106.9 7.1 %collective-permute-done.30.refs_3_ = bf16[192,1024]{1,0:T(8,128)(2,1)S(1)} collective-permute-done((bf16[192,1024]{1,0:T(8,128)(2,1)S(1)}, bf16[192,1024]{1,0:T(8,128)(2,1)S(1)}, u32[]{:S(2)}, u32[]{:S(2)}) %collective-permute-start.30) | collective-permute-done | bytes 393248 | tf_op jit(solution)/shard_map/grads_y/ppermute | solution.py:52
  114.1 1.0 tokens.1
  115.1 1.0 collective-permute-start.32
  116.2 1.6 %tokens_own.1.refs_0_ = f32[384,1024]{1,0:T(8,128)S(1)} custom-call(bf16[768,512]{1,0:T(8,128)(2,1)S(1)} %get-tuple-element.68.gg.refs_0_, bf16[768,512]{1,0:T(8,128)(2,1)S(1)} %get-tuple-element.69.ug.refs_1_, bf16[1024,512]{1,0:T(8,128)(2,1)S(1)} %copy-done, bf16[1024,512]{1,0:T(8,128)(2,1)S(1)} %copy-done.1), custom_call_target="tpu_custom_call" | custom-call | flops 805306368 | bytes 5242880 | tf_op jit(solution)/shard_map/tokens_own/pallas_call | solution.py:84
  117.8 1.0 convolution_convert_fusion.2.refs_2_
  119.8 3.3 %collective-permute-start.33 = (bf16[96,1024]{1,0:T(8,128)(2,1)S(1)}, bf16[96,1024]{1,0:T(8,128)(2,1)S(1)}, u32[]{:S(2)}, u32[]{:S(2)}) collective-permute-start(bf16[96,1024]{1,0:T(8,128)(2,1)S(1)} %get-tuple-element.73), channel_id=1, source_target_pairs={{0,32},{8,40},{16,48},{24,56},{32,0},{40,8},{48,16},{56,24},{64,96... | collective-permute-start | bytes 589832 | tf_op jit(solution)/shard_map/token_grad_x/ppermute | solution.py:42
  123.2 1.3 collective-permute-start.37
  124.6 3.8 %collective-permute-done.33.refs_3_.refs_2_ = bf16[96,1024]{1,0:T(8,128)(2,1)S(1)} collective-permute-done((bf16[96,1024]{1,0:T(8,128)(2,1)S(1)}, bf16[96,1024]{1,0:T(8,128)(2,1)S(1)}, u32[]{:S(2)}, u32[]{:S(2)}) %collective-permute-start.33) | collective-permute-done | bytes 196640 | tf_op jit(solution)/shard_map/token_grad_x/ppermute | solution.py:42
  128.4 5.6 %collective-permute-start.35 = (bf16[24,1024]{1,0:T(8,128)(2,1)S(1)}, bf16[24,1024]{1,0:T(8,128)(2,1)S(1)}, u32[]{:S(2)}, u32[]{:S(2)}) collective-permute-start(bf16[24,1024]{1,0:T(8,128)(2,1)S(1)} %get-tuple-element.75), channel_id=1, source_target_pairs={{0,128},{8,136},{16,144},{24,152},{32,160},{40,168},{48,176},{56,1... | collective-permute-start | bytes 147464 | tf_op jit(solution)/shard_map/output_z/ppermute | solution.py:37
  134.2 1.0 convolution_convert_fusion.refs_5_
  135.2 1.0 convolution_convert_fusion.1.refs_4_
  136.3 1.5 %collective-permute-start.34 = (bf16[24,1024]{1,0:T(8,128)(2,1)S(1)}, bf16[24,1024]{1,0:T(8,128)(2,1)S(1)}, u32[]{:S(2)}, u32[]{:S(2)}) collective-permute-start(bf16[24,1024]{1,0:T(8,128)(2,1)S(1)} %get-tuple-element.74), channel_id=1, source_target_pairs={{0,192},{8,200},{16,208},{24,216},{32,224},{40,232},{48,240},{56,2... | collective-permute-start | bytes 147464 | tf_op jit(solution)/shard_map/output_z/ppermute | solution.py:37
  138.0 3.3 %collective-permute-start.39 = (bf16[24,1024]{1,0:T(8,128)(2,1)S(1)}, bf16[24,1024]{1,0:T(8,128)(2,1)S(1)}, u32[]{:S(2)}, u32[]{:S(2)}) collective-permute-start(bf16[24,1024]{1,0:T(8,128)(2,1)S(1)} %get-tuple-element.84), channel_id=1, source_target_pairs={{0,192},{8,200},{16,208},{24,216},{32,224},{40,232},{48,240},{56,2... | collective-permute-start | bytes 147464 | tf_op jit(solution)/shard_map/token_grad_z/ppermute | solution.py:37
  141.6 0.9 collective-permute-done.36.c
  142.5 0.6 rs_last.2
  143.2 2.0 %collective-permute-done.40.b = bf16[24,1024]{1,0:T(8,128)(2,1)S(1)} collective-permute-done((bf16[24,1024]{1,0:T(8,128)(2,1)S(1)}, bf16[24,1024]{1,0:T(8,128)(2,1)S(1)}, u32[]{:S(2)}, u32[]{:S(2)}) %collective-permute-start.40) | collective-permute-done | bytes 49184 | tf_op jit(solution)/shard_map/token_grad_z/ppermute | solution.py:37
  145.1 1.2 collective-permute-done.41.c
  (65 shorter events, 5.6 us)
Async XLA Ops:
  0.6 27.6 %copy-start = (bf16[1024,512]{1,0:T(8,128)(2,1)S(1)}, bf16[1024,512]{1,0:T(8,128)(2,1)}, u32[]{:S(2)}) copy-start(bf16[1024,512]{1,0:T(8,128)(2,1)} %wg.3) | copy-start | bytes 3145732
  0.6 27.6 %copy-start.1 = (bf16[1024,512]{1,0:T(8,128)(2,1)S(1)}, bf16[1024,512]{1,0:T(8,128)(2,1)}, u32[]{:S(2)}) copy-start(bf16[1024,512]{1,0:T(8,128)(2,1)} %wu.3) | copy-start | bytes 3145732
  0.7 7.1 %collective-permute-start = (bf16[24,1024]{1,0:T(8,128)(2,1)}, bf16[24,1024]{1,0:T(8,128)(2,1)S(1)}, u32[]{:S(2)}, u32[]{:S(2)}) collective-permute-start(bf16[24,1024]{1,0:T(8,128)(2,1)} %refs_0_.2), channel_id=1, source_target_pairs={{0,64},{8,72},{16,80},{24,88},{32,96},{40,104},{48,112},{56,120},{... | collective-permute-start | bytes 147464 | tf_op jit(solution)/shard_map/tokens_z/ppermute | solution.py:37
  3.2 4.9 %collective-permute-start.1 = (bf16[24,1024]{1,0:T(8,128)(2,1)}, bf16[24,1024]{1,0:T(8,128)(2,1)S(1)}, u32[]{:S(2)}, u32[]{:S(2)}) collective-permute-start(bf16[24,1024]{1,0:T(8,128)(2,1)} %refs_0_.2), channel_id=1, source_target_pairs={{0,128},{8,136},{16,144},{24,152},{32,160},{40,168},{48,176},{56,1... | collective-permute-start | bytes 147464 | tf_op jit(solution)/shard_map/tokens_z/ppermute | solution.py:37
  6.2 4.1 %collective-permute-start.2 = (bf16[24,1024]{1,0:T(8,128)(2,1)}, bf16[24,1024]{1,0:T(8,128)(2,1)S(1)}, u32[]{:S(2)}, u32[]{:S(2)}) collective-permute-start(bf16[24,1024]{1,0:T(8,128)(2,1)} %refs_0_.2), channel_id=1, source_target_pairs={{0,192},{8,200},{16,208},{24,216},{32,224},{40,232},{48,240},{56,2... | collective-permute-start | bytes 147464 | tf_op jit(solution)/shard_map/tokens_z/ppermute | solution.py:37
  6.9 0.8 copy-start.6
  10.3 11.6 %collective-permute-start.3 = (bf16[96,1024]{1,0:T(8,128)(2,1)S(1)}, bf16[96,1024]{1,0:T(8,128)(2,1)S(1)}, u32[]{:S(2)}, u32[]{:S(2)}) collective-permute-start(bf16[96,1024]{1,0:T(8,128)(2,1)S(1)} %cat_z.2.refs_1_.refs_0_), channel_id=1, source_target_pairs={{0,16},{8,24},{16,32},{24,40},{32,48},{40,56},{48,0},{56,8},{64,80... | collective-permute-start | bytes 589832 | tf_op jit(solution)/shard_map/tokens_x/ppermute | solution.py:42
  11.5 10.5 %collective-permute-start.4 = (bf16[96,1024]{1,0:T(8,128)(2,1)S(1)}, bf16[96,1024]{1,0:T(8,128)(2,1)S(1)}, u32[]{:S(2)}, u32[]{:S(2)}) collective-permute-start(bf16[96,1024]{1,0:T(8,128)(2,1)S(1)} %cat_z.2.refs_1_.refs_0_), channel_id=1, source_target_pairs={{0,32},{8,40},{16,48},{24,56},{32,0},{40,8},{48,16},{56,24},{64,96... | collective-permute-start | bytes 589832 | tf_op jit(solution)/shard_map/tokens_x/ppermute | solution.py:42
  13.9 8.1 %collective-permute-start.5 = (bf16[96,1024]{1,0:T(8,128)(2,1)S(1)}, bf16[96,1024]{1,0:T(8,128)(2,1)S(1)}, u32[]{:S(2)}, u32[]{:S(2)}) collective-permute-start(bf16[96,1024]{1,0:T(8,128)(2,1)S(1)} %cat_z.2.refs_1_.refs_0_), channel_id=1, source_target_pairs={{0,48},{8,56},{16,0},{24,8},{32,16},{40,24},{48,32},{56,40},{64,11... | collective-permute-start | bytes 589832 | tf_op jit(solution)/shard_map/tokens_x/ppermute | solution.py:42
  15.1 0.8 copy-start.5
  15.9 4.7 %collective-permute-start.6 = (bf16[24,1024]{1,0:T(8,128)(2,1)S(1)}, bf16[24,1024]{1,0:T(8,128)(2,1)S(1)}, u32[]{:S(2)}, u32[]{:S(2)}) collective-permute-start(bf16[24,1024]{1,0:T(8,128)(2,1)S(1)} %hold.8.refs_0_), channel_id=1, source_target_pairs={{0,64},{8,72},{16,80},{24,88},{32,96},{40,104},{48,112},{56,120},{... | collective-permute-start | bytes 147464 | tf_op jit(solution)/shard_map/cotangent_z/ppermute | solution.py:37
  17.2 4.7 %collective-permute-start.7 = (bf16[24,1024]{1,0:T(8,128)(2,1)S(1)}, bf16[24,1024]{1,0:T(8,128)(2,1)S(1)}, u32[]{:S(2)}, u32[]{:S(2)}) collective-permute-start(bf16[24,1024]{1,0:T(8,128)(2,1)S(1)} %hold.8.refs_0_), channel_id=1, source_target_pairs={{0,128},{8,136},{16,144},{24,152},{32,160},{40,168},{48,176},{56,1... | collective-permute-start | bytes 147464 | tf_op jit(solution)/shard_map/cotangent_z/ppermute | solution.py:37
  22.0 6.2 %collective-permute-start.8 = (bf16[384,1024]{1,0:T(8,128)(2,1)S(1)}, bf16[384,1024]{1,0:T(8,128)(2,1)}, u32[]{:S(2)}, u32[]{:S(2)}) collective-permute-start(bf16[384,1024]{1,0:T(8,128)(2,1)S(1)} %cat_x.2.mine), channel_id=1, source_target_pairs={{0,8},{8,0},{16,24},{24,16},{32,40},{40,32},{48,56},{56,48},{64,72... | collective-permute-start | bytes 2359304 | tf_op jit(solution)/shard_map/tokens_core/ppermute | solution.py:47
  25.3 3.0 %collective-permute-start.12 = (bf16[24,1024]{1,0:T(8,128)(2,1)S(1)}, bf16[24,1024]{1,0:T(8,128)(2,1)S(1)}, u32[]{:S(2)}, u32[]{:S(2)}) collective-permute-start(bf16[24,1024]{1,0:T(8,128)(2,1)S(1)} %hold.8.refs_0_), channel_id=1, source_target_pairs={{0,192},{8,200},{16,208},{24,216},{32,224},{40,232},{48,240},{56,2... | collective-permute-start | bytes 147464 | tf_op jit(solution)/shard_map/cotangent_z/ppermute | solution.py:37
  31.4 16.4 %collective-permute-start.9 = (bf16[192,1024]{1,0:T(8,128)(2,1)S(1)}, bf16[192,1024]{1,0:T(8,128)(2,1)S(1)}, u32[]{:S(2)}, u32[]{:S(2)}) collective-permute-start(bf16[192,1024]{1,0:T(8,128)(2,1)S(1)} %get-tuple-element.47.refs_1_), channel_id=1, source_target_pairs={{0,1},{1,2},{2,3},{3,0},{4,5},{5,6},{6,7},{7,4},{8,9},{9,10},{10,1... | collective-permute-start | bytes 1179656 | tf_op jit(solution)/shard_map/gate_up_y/ppermute | solution.py:52
  32.8 6.2 %collective-permute-start.13 = (bf16[96,1024]{1,0:T(8,128)(2,1)S(1)}, bf16[96,1024]{1,0:T(8,128)(2,1)S(1)}, u32[]{:S(2)}, u32[]{:S(2)}) collective-permute-start(bf16[96,1024]{1,0:T(8,128)(2,1)S(1)} %hold.10.refs_0_), channel_id=1, source_target_pairs={{0,16},{8,24},{16,32},{24,40},{32,48},{40,56},{48,0},{56,8},{64,80... | collective-permute-start | bytes 589832 | tf_op jit(solution)/shard_map/cotangent_x/ppermute | solution.py:42
  33.2 19.3 %collective-permute-start.10 = (bf16[192,1024]{1,0:T(8,128)(2,1)S(1)}, bf16[192,1024]{1,0:T(8,128)(2,1)S(1)}, u32[]{:S(2)}, u32[]{:S(2)}) collective-permute-start(bf16[192,1024]{1,0:T(8,128)(2,1)S(1)} %get-tuple-element.48), channel_id=1, source_target_pairs={{0,2},{1,3},{2,0},{3,1},{4,6},{5,7},{6,4},{7,5},{8,10},{9,11},{10,... | collective-permute-start | bytes 1179656 | tf_op jit(solution)/shard_map/gate_up_y/ppermute | solution.py:52
  36.3 16.4 %collective-permute-start.11 = (bf16[192,1024]{1,0:T(8,128)(2,1)S(1)}, bf16[192,1024]{1,0:T(8,128)(2,1)S(1)}, u32[]{:S(2)}, u32[]{:S(2)}) collective-permute-start(bf16[192,1024]{1,0:T(8,128)(2,1)S(1)} %get-tuple-element.49), channel_id=1, source_target_pairs={{0,3},{1,0},{2,1},{3,2},{4,7},{5,4},{6,5},{7,6},{8,11},{9,8},{10,9... | collective-permute-start | bytes 1179656 | tf_op jit(solution)/shard_map/gate_up_y/ppermute | solution.py:52
  37.3 6.0 %collective-permute-start.14 = (bf16[96,1024]{1,0:T(8,128)(2,1)S(1)}, bf16[96,1024]{1,0:T(8,128)(2,1)S(1)}, u32[]{:S(2)}, u32[]{:S(2)}) collective-permute-start(bf16[96,1024]{1,0:T(8,128)(2,1)S(1)} %hold.10.refs_0_), channel_id=1, source_target_pairs={{0,32},{8,40},{16,48},{24,56},{32,0},{40,8},{48,16},{56,24},{64,96... | collective-permute-start | bytes 589832 | tf_op jit(solution)/shard_map/cotangent_x/ppermute | solution.py:42
  39.0 8.8 %collective-permute-start.15 = (bf16[96,1024]{1,0:T(8,128)(2,1)S(1)}, bf16[96,1024]{1,0:T(8,128)(2,1)S(1)}, u32[]{:S(2)}, u32[]{:S(2)}) collective-permute-start(bf16[96,1024]{1,0:T(8,128)(2,1)S(1)} %hold.10.refs_0_), channel_id=1, source_target_pairs={{0,48},{8,56},{16,0},{24,8},{32,16},{40,24},{48,32},{56,40},{64,11... | collective-permute-start | bytes 589832 | tf_op jit(solution)/shard_map/cotangent_x/ppermute | solution.py:42
  52.7 7.3 %copy-start.7 = (bf16[512,1024]{1,0:T(8,128)(2,1)S(1)}, bf16[512,1024]{1,0:T(8,128)(2,1)}, u32[]{:S(2)}) copy-start(bf16[512,1024]{1,0:T(8,128)(2,1)} %refs_5_.2) | copy-start | bytes 3145732
  52.7 7.2 %collective-permute-start.17 = (bf16[384,1024]{1,0:T(8,128)(2,1)S(1)}, bf16[384,1024]{1,0:T(8,128)(2,1)S(1)}, u32[]{:S(2)}, u32[]{:S(2)}) collective-permute-start(bf16[384,1024]{1,0:T(8,128)(2,1)S(1)} %cat_x.3.mine), channel_id=1, source_target_pairs={{0,8},{8,0},{16,24},{24,16},{32,40},{40,32},{48,56},{56,48},{64,72... | collective-permute-start | bytes 2359304 | tf_op jit(solution)/shard_map/cotangent_core/ppermute | solution.py:47
  54.7 17.7 %collective-permute-start.16 = (bf16[192,1024]{1,0:T(8,128)(2,1)S(1)}, bf16[192,1024]{1,0:T(8,128)(2,1)S(1)}, u32[]{:S(2)}, u32[]{:S(2)}) collective-permute-start(bf16[192,1024]{1,0:T(8,128)(2,1)S(1)} %get-tuple-element.51), channel_id=1, source_target_pairs={{0,4},{1,5},{2,6},{3,7},{4,0},{5,1},{6,2},{7,3},{8,12},{9,13},{10,... | collective-permute-start | bytes 1179656 | tf_op jit(solution)/shard_map/gate_up_half/ppermute | solution.py:57
  61.5 10.9 %collective-permute-start.18 = (bf16[192,512]{1,0:T(8,128)(2,1)S(1)}, bf16[192,512]{1,0:T(8,128)(2,1)S(1)}, u32[]{:S(2)}, u32[]{:S(2)}) collective-permute-start(bf16[192,512]{1,0:T(8,128)(2,1)S(1)} %get-tuple-element.52), channel_id=1, source_target_pairs={{0,1},{1,2},{2,3},{3,0},{4,5},{5,6},{6,7},{7,4},{8,9},{9,10},{10,1... | collective-permute-start | bytes 589832 | tf_op jit(solution)/shard_map/hidden_grad_y/ppermute | solution.py:52
  62.9 11.1 %collective-permute-start.19 = (bf16[192,512]{1,0:T(8,128)(2,1)S(1)}, bf16[192,512]{1,0:T(8,128)(2,1)S(1)}, u32[]{:S(2)}, u32[]{:S(2)}) collective-permute-start(bf16[192,512]{1,0:T(8,128)(2,1)S(1)} %get-tuple-element.53), channel_id=1, source_target_pairs={{0,2},{1,3},{2,0},{3,1},{4,6},{5,7},{6,4},{7,5},{8,10},{9,11},{10,... | collective-permute-start | bytes 589832 | tf_op jit(solution)/shard_map/hidden_grad_y/ppermute | solution.py:52
  65.0 9.0 %collective-permute-start.20 = (bf16[192,512]{1,0:T(8,128)(2,1)S(1)}, bf16[192,512]{1,0:T(8,128)(2,1)S(1)}, u32[]{:S(2)}, u32[]{:S(2)}) collective-permute-start(bf16[192,512]{1,0:T(8,128)(2,1)S(1)} %get-tuple-element.54), channel_id=1, source_target_pairs={{0,3},{1,0},{2,1},{3,2},{4,7},{5,4},{6,5},{7,6},{8,11},{9,8},{10,9... | collective-permute-start | bytes 589832 | tf_op jit(solution)/shard_map/hidden_grad_y/ppermute | solution.py:52
  74.0 11.6 %collective-permute-start.24 = (bf16[192,512]{1,0:T(8,128)(2,1)S(1)}, bf16[192,512]{1,0:T(8,128)(2,1)S(1)}, u32[]{:S(2)}, u32[]{:S(2)}) collective-permute-start(bf16[192,512]{1,0:T(8,128)(2,1)S(1)} %get-tuple-element.56), channel_id=1, source_target_pairs={{0,4},{1,5},{2,6},{3,7},{4,0},{5,1},{6,2},{7,3},{8,12},{9,13},{10,... | collective-permute-start | bytes 589832 | tf_op jit(solution)/shard_map/hidden_grad_half/ppermute | solution.py:57
  78.1 7.5 %collective-permute-start.21 = (bf16[192,512]{1,0:T(8,128)(2,1)S(1)}, bf16[192,512]{1,0:T(8,128)(2,1)S(1)}, u32[]{:S(2)}, u32[]{:S(2)}) collective-permute-start(bf16[192,512]{1,0:T(8,128)(2,1)S(1)} %hidden.1.refs_1_), channel_id=1, source_target_pairs={{0,1},{1,2},{2,3},{3,0},{4,5},{5,6},{6,7},{7,4},{8,9},{9,10},{10,1... | collective-permute-start | bytes 589832 | tf_op jit(solution)/shard_map/hidden_y/ppermute | solution.py:52
  79.4 10.1 %collective-permute-start.22 = (bf16[192,512]{1,0:T(8,128)(2,1)S(1)}, bf16[192,512]{1,0:T(8,128)(2,1)S(1)}, u32[]{:S(2)}, u32[]{:S(2)}) collective-permute-start(bf16[192,512]{1,0:T(8,128)(2,1)S(1)} %hidden.1.refs_1_), channel_id=1, source_target_pairs={{0,2},{1,3},{2,0},{3,1},{4,6},{5,7},{6,4},{7,5},{8,10},{9,11},{10,... | collective-permute-start | bytes 589832 | tf_op jit(solution)/shard_map/hidden_y/ppermute | solution.py:52
  81.6 8.0 %collective-permute-start.23 = (bf16[192,512]{1,0:T(8,128)(2,1)S(1)}, bf16[192,512]{1,0:T(8,128)(2,1)S(1)}, u32[]{:S(2)}, u32[]{:S(2)}) collective-permute-start(bf16[192,512]{1,0:T(8,128)(2,1)S(1)} %hidden.1.refs_1_), channel_id=1, source_target_pairs={{0,3},{1,0},{2,1},{3,2},{4,7},{5,4},{6,5},{7,6},{8,11},{9,8},{10,9... | collective-permute-start | bytes 589832 | tf_op jit(solution)/shard_map/hidden_y/ppermute | solution.py:52
  90.8 6.9 %collective-permute-start.25 = (f32[384,1024]{1,0:T(8,128)S(1)}, f32[384,1024]{1,0:T(8,128)S(1)}, u32[]{:S(2)}, u32[]{:S(2)}) collective-permute-start(f32[384,1024]{1,0:T(8,128)S(1)} %get-tuple-element.59), channel_id=1, source_target_pairs={{0,8},{8,0},{16,24},{24,16},{32,40},{40,32},{48,56},{56,48},{64,72... | collective-permute-start | bytes 4718600 | tf_op jit(solution)/shard_map/output_core/ppermute | solution.py:47
  93.0 11.9 %collective-permute-start.29 = (bf16[192,1024]{1,0:T(8,128)(2,1)S(1)}, bf16[192,1024]{1,0:T(8,128)(2,1)S(1)}, u32[]{:S(2)}, u32[]{:S(2)}) collective-permute-start(bf16[192,1024]{1,0:T(8,128)(2,1)S(1)} %grads.1.refs_7_.refs_1_), channel_id=1, source_target_pairs={{0,1},{1,2},{2,3},{3,0},{4,5},{5,6},{6,7},{7,4},{8,9},{9,10},{10,1... | collective-permute-start | bytes 1179656 | tf_op jit(solution)/shard_map/grads_y/ppermute | solution.py:52
  94.3 19.7 %collective-permute-start.30 = (bf16[192,1024]{1,0:T(8,128)(2,1)S(1)}, bf16[192,1024]{1,0:T(8,128)(2,1)S(1)}, u32[]{:S(2)}, u32[]{:S(2)}) collective-permute-start(bf16[192,1024]{1,0:T(8,128)(2,1)S(1)} %grads.1.refs_7_.refs_1_), channel_id=1, source_target_pairs={{0,2},{1,3},{2,0},{3,1},{4,6},{5,7},{6,4},{7,5},{8,10},{9,11},{10,... | collective-permute-start | bytes 1179656 | tf_op jit(solution)/shard_map/grads_y/ppermute | solution.py:52
  96.4 17.6 %collective-permute-start.31 = (bf16[192,1024]{1,0:T(8,128)(2,1)S(1)}, bf16[192,1024]{1,0:T(8,128)(2,1)S(1)}, u32[]{:S(2)}, u32[]{:S(2)}) collective-permute-start(bf16[192,1024]{1,0:T(8,128)(2,1)S(1)} %grads.1.refs_7_.refs_1_), channel_id=1, source_target_pairs={{0,3},{1,0},{2,1},{3,2},{4,7},{5,4},{6,5},{7,6},{8,11},{9,8},{10,9... | collective-permute-start | bytes 1179656 | tf_op jit(solution)/shard_map/grads_y/ppermute | solution.py:52
  97.8 16.2 %collective-permute-start.26 = (bf16[96,1024]{1,0:T(8,128)(2,1)S(1)}, bf16[96,1024]{1,0:T(8,128)(2,1)S(1)}, u32[]{:S(2)}, u32[]{:S(2)}) collective-permute-start(bf16[96,1024]{1,0:T(8,128)(2,1)S(1)} %get-tuple-element.61), channel_id=1, source_target_pairs={{0,48},{8,56},{16,0},{24,8},{32,16},{40,24},{48,32},{56,40},{64,11... | collective-permute-start | bytes 589832 | tf_op jit(solution)/shard_map/output_x/ppermute | solution.py:42
  100.5 13.5 %collective-permute-start.27 = (bf16[96,1024]{1,0:T(8,128)(2,1)S(1)}, bf16[96,1024]{1,0:T(8,128)(2,1)S(1)}, u32[]{:S(2)}, u32[]{:S(2)}) collective-permute-start(bf16[96,1024]{1,0:T(8,128)(2,1)S(1)} %get-tuple-element.62), channel_id=1, source_target_pairs={{0,32},{8,40},{16,48},{24,56},{32,0},{40,8},{48,16},{56,24},{64,96... | collective-permute-start | bytes 589832 | tf_op jit(solution)/shard_map/output_x/ppermute | solution.py:42
  104.9 9.2 %collective-permute-start.28 = (bf16[96,1024]{1,0:T(8,128)(2,1)S(1)}, bf16[96,1024]{1,0:T(8,128)(2,1)S(1)}, u32[]{:S(2)}, u32[]{:S(2)}) collective-permute-start(bf16[96,1024]{1,0:T(8,128)(2,1)S(1)} %get-tuple-element.63), channel_id=1, source_target_pairs={{0,16},{8,24},{16,32},{24,40},{32,48},{40,56},{48,0},{56,8},{64,80... | collective-permute-start | bytes 589832 | tf_op jit(solution)/shard_map/output_x/ppermute | solution.py:42
  115.1 4.0 %collective-permute-start.32 = (f32[384,1024]{1,0:T(8,128)S(1)}, f32[384,1024]{1,0:T(8,128)S(1)}, u32[]{:S(2)}, u32[]{:S(2)}) collective-permute-start(f32[384,1024]{1,0:T(8,128)S(1)} %get-tuple-element.70.refs_1_), channel_id=1, source_target_pairs={{0,8},{8,0},{16,24},{24,16},{32,40},{40,32},{48,56},{56,48},{64,72... | collective-permute-start | bytes 4718600 | tf_op jit(solution)/shard_map/token_grad_core/ppermute | solution.py:47
  118.9 1.0 copy-start.4
  119.8 8.6 %collective-permute-start.33 = (bf16[96,1024]{1,0:T(8,128)(2,1)S(1)}, bf16[96,1024]{1,0:T(8,128)(2,1)S(1)}, u32[]{:S(2)}, u32[]{:S(2)}) collective-permute-start(bf16[96,1024]{1,0:T(8,128)(2,1)S(1)} %get-tuple-element.73), channel_id=1, source_target_pairs={{0,32},{8,40},{16,48},{24,56},{32,0},{40,8},{48,16},{56,24},{64,96... | collective-permute-start | bytes 589832 | tf_op jit(solution)/shard_map/token_grad_x/ppermute | solution.py:42
  123.2 14.7 %collective-permute-start.37 = (bf16[96,1024]{1,0:T(8,128)(2,1)S(1)}, bf16[96,1024]{1,0:T(8,128)(2,1)S(1)}, u32[]{:S(2)}, u32[]{:S(2)}) collective-permute-start(bf16[96,1024]{1,0:T(8,128)(2,1)S(1)} %get-tuple-element.78), channel_id=1, source_target_pairs={{0,48},{8,56},{16,0},{24,8},{32,16},{40,24},{48,32},{56,40},{64,11... | collective-permute-start | bytes 589832 | tf_op jit(solution)/shard_map/token_grad_x/ppermute | solution.py:42
  124.5 13.4 %collective-permute-start.38 = (bf16[96,1024]{1,0:T(8,128)(2,1)S(1)}, bf16[96,1024]{1,0:T(8,128)(2,1)S(1)}, u32[]{:S(2)}, u32[]{:S(2)}) collective-permute-start(bf16[96,1024]{1,0:T(8,128)(2,1)S(1)} %get-tuple-element.79), channel_id=1, source_target_pairs={{0,16},{8,24},{16,32},{24,40},{32,48},{40,56},{48,0},{56,8},{64,80... | collective-permute-start | bytes 589832 | tf_op jit(solution)/shard_map/token_grad_x/ppermute | solution.py:42
  128.4 9.4 %collective-permute-start.35 = (bf16[24,1024]{1,0:T(8,128)(2,1)S(1)}, bf16[24,1024]{1,0:T(8,128)(2,1)S(1)}, u32[]{:S(2)}, u32[]{:S(2)}) collective-permute-start(bf16[24,1024]{1,0:T(8,128)(2,1)S(1)} %get-tuple-element.75), channel_id=1, source_target_pairs={{0,128},{8,136},{16,144},{24,152},{32,160},{40,168},{48,176},{56,1... | collective-permute-start | bytes 147464 | tf_op jit(solution)/shard_map/output_z/ppermute | solution.py:37
  135.2 2.6 %copy-start.2 = (bf16[1024,512]{1,0:T(8,128)(2,1)}, bf16[1024,512]{1,0:T(8,128)(2,1)S(1)}, u32[]{:S(2)}) copy-start(bf16[1024,512]{1,0:T(8,128)(2,1)S(1)} %convolution_convert_fusion.refs_5_) | copy-start | bytes 3145732
  136.3 6.9 %copy-start.3 = (bf16[1024,512]{1,0:T(8,128)(2,1)}, bf16[1024,512]{1,0:T(8,128)(2,1)S(1)}, u32[]{:S(2)}) copy-start(bf16[1024,512]{1,0:T(8,128)(2,1)S(1)} %convolution_convert_fusion.1.refs_4_) | copy-start | bytes 3145732
  136.3 5.3 %collective-permute-start.34 = (bf16[24,1024]{1,0:T(8,128)(2,1)S(1)}, bf16[24,1024]{1,0:T(8,128)(2,1)S(1)}, u32[]{:S(2)}, u32[]{:S(2)}) collective-permute-start(bf16[24,1024]{1,0:T(8,128)(2,1)S(1)} %get-tuple-element.74), channel_id=1, source_target_pairs={{0,192},{8,200},{16,208},{24,216},{32,224},{40,232},{48,240},{56,2... | collective-permute-start | bytes 147464 | tf_op jit(solution)/shard_map/output_z/ppermute | solution.py:37
  137.8 4.7 %collective-permute-start.36 = (bf16[24,1024]{1,0:T(8,128)(2,1)S(1)}, bf16[24,1024]{1,0:T(8,128)(2,1)S(1)}, u32[]{:S(2)}, u32[]{:S(2)}) collective-permute-start(bf16[24,1024]{1,0:T(8,128)(2,1)S(1)} %get-tuple-element.76), channel_id=1, source_target_pairs={{0,64},{8,72},{16,80},{24,88},{32,96},{40,104},{48,112},{56,120},{... | collective-permute-start | bytes 147464 | tf_op jit(solution)/shard_map/output_z/ppermute | solution.py:37
  138.0 5.2 %collective-permute-start.39 = (bf16[24,1024]{1,0:T(8,128)(2,1)S(1)}, bf16[24,1024]{1,0:T(8,128)(2,1)S(1)}, u32[]{:S(2)}, u32[]{:S(2)}) collective-permute-start(bf16[24,1024]{1,0:T(8,128)(2,1)S(1)} %get-tuple-element.84), channel_id=1, source_target_pairs={{0,192},{8,200},{16,208},{24,216},{32,224},{40,232},{48,240},{56,2... | collective-permute-start | bytes 147464 | tf_op jit(solution)/shard_map/token_grad_z/ppermute | solution.py:37
  141.2 3.9 %collective-permute-start.40 = (bf16[24,1024]{1,0:T(8,128)(2,1)S(1)}, bf16[24,1024]{1,0:T(8,128)(2,1)S(1)}, u32[]{:S(2)}, u32[]{:S(2)}) collective-permute-start(bf16[24,1024]{1,0:T(8,128)(2,1)S(1)} %get-tuple-element.85), channel_id=1, source_target_pairs={{0,128},{8,136},{16,144},{24,152},{32,160},{40,168},{48,176},{56,1... | collective-permute-start | bytes 147464 | tf_op jit(solution)/shard_map/token_grad_z/ppermute | solution.py:37
  141.2 5.1 %collective-permute-start.41 = (bf16[24,1024]{1,0:T(8,128)(2,1)S(1)}, bf16[24,1024]{1,0:T(8,128)(2,1)S(1)}, u32[]{:S(2)}, u32[]{:S(2)}) collective-permute-start(bf16[24,1024]{1,0:T(8,128)(2,1)S(1)} %get-tuple-element.86), channel_id=1, source_target_pairs={{0,64},{8,72},{16,80},{24,88},{32,96},{40,104},{48,112},{56,120},{... | collective-permute-start | bytes 147464 | tf_op jit(solution)/shard_map/token_grad_z/ppermute | solution.py:37
